TPU v7x, 32 devices: a whole 2x2x4 slice. The times are simulated.
32 devices in a mesh: groups: 2 (over y), dp: 4 (over z), tensor: 2 (over x), pair: 2 (over core).
Axes of the slice: x: 2, y: 2, z: 4, core: 2. Of those that a mesh axis runs over, the one named last changes fastest.
Arguments:
- activations: bfloat16 [8192, 4096], P(('groups', 'dp'), ('tensor', 'pair')), parts along dimension 0, may hold values from -6 to 6
- tile_dest: int32 [8, 8], P('groups'), parts along dimension 0, may hold values from -1 to 3, as said below
- segment_ids: int32 [8, 8, 128], P('groups'), parts along dimension 0, may hold values from 0 to 2, never falling along the last dimension, each value on 1 to 96 neighbouring positions
- norm_gain: bfloat16 [4096], replicated, may hold values from 0.099609375 to 1.8984375
- q_weight: bfloat16 [4096, 4096], P('dp', ('tensor', 'pair')), may hold values from -0.09375 to 0.09375
- k_weight: bfloat16 [4096, 1024], P('dp', 'tensor'), may hold values from -0.09375 to 0.09375
- v_weight: bfloat16 [4096, 1024], P('dp', 'tensor'), may hold values from -0.09375 to 0.09375
- q_bias: bfloat16 [4096], P(('tensor', 'pair')), may hold values from -100 to 100
- k_bias: bfloat16 [1024], P('tensor'), may hold values from -24 to 24
- v_bias: bfloat16 [1024], P('tensor'), may hold values from -6 to 6
- o_weight: bfloat16 [4096, 4096], P(('tensor', 'pair'), 'dp'), may hold values from -0.25 to 0.25
Outputs:
- layer_out: bfloat16 [4096, 4096], P(('groups', 'dp'), ('tensor', 'pair')), parts along dimension 0
There are 2 independent parts, one for each index of `groups`. A program takes and returns all parts, laid end to end along the dimension named above; an argument that names none is the same for every part. Nothing has to cross between parts.
Inputs may be any that keep to these rules, and one draw needn't show every extreme that they name: `tile_dest`: for each of the 8 slots of each dp index, the dp index its tile goes to, or -1 where the slot is empty; a dp index's tiles fill its first slots; every dp index receives exactly 4 tiles; at most 2 tiles go from one dp index to any one, and some pair reaches 2; some dp index fills all 8 slots. `segment_ids`: within each tile the segment number never falls; each segment of a tile holds at most 96 rows, and some segment exactly that many.
All inputs are finite; a program needn't handle non-finite values.
Results may differ from a plain program's by a relative error of at most 0.014.
The roundings to bfloat16 on the way count: a program that leaves them out, or rounds other values in their place, can miss the bound.
Values may be sent and summed in bfloat16 or wider, within the bound.
No kernel may reach another device: no remote copies, remote signals or barrier semaphores. Data moves between devices by JAX's collectives and lax.ppermute only.
A program may use at most 128 MiB of HBM per device.

v0:
```python
import math

import jax
import jax.numpy as jnp
from jax import lax
from jax.sharding import PartitionSpec as P

QHEADS = 32
KVH = 8
HEAD = 128
TPD = 4


norm_eps = 1e-06


def normalize(values, gain_vector):
    widened = values.astype(jnp.float32)
    meansq = jnp.mean(widened * widened, axis=-1, keepdims=True)
    return (widened * lax.rsqrt(meansq + norm_eps) * gain_vector.astype(jnp.float32)).astype(
        jnp.bfloat16
    )


def rotary(values, positions):
    half_size = values.shape[-1] // 2
    inverse = jnp.power(
        jnp.float32(1000000.0), -2.0 * jnp.arange(half_size, dtype=jnp.float32) / values.shape[-1]
    )
    angles = positions.astype(jnp.float32)[:, None] * inverse[None, :]
    cosine = jnp.cos(angles)[:, None, :]
    sine_part = jnp.sin(angles)[:, None, :]
    front_half = values[..., :half_size]
    back_half = values[..., half_size:]
    return jnp.concatenate(
        [front_half * cosine - back_half * sine_part, back_half * cosine + front_half * sine_part],
        axis=-1,
    )


def tile_positions(segment):
    earlier = (segment[..., None, :] < segment[..., :, None]).astype(jnp.int32)
    first_row = jnp.sum(earlier, axis=-1)
    return jnp.arange(segment.shape[-1], dtype=jnp.int32) - first_row


def attend_tiles(query_groups, key_rows, value_rows, segment):
    tile_rows = query_groups.shape[1]
    scores = jnp.einsum(
        "tqgsd,tkgd->tgsqk", query_groups, key_rows, preferred_element_type=jnp.float32
    )
    scores = scores * (1.0 / math.sqrt(query_groups.shape[-1]))
    places = jnp.arange(tile_rows, dtype=jnp.int32)
    allowed = (segment[:, :, None] == segment[:, None, :]) & (
        places[None, None, :] <= places[None, :, None]
    )
    scores = jnp.where(allowed[:, None, None, :, :], scores, -1e30)
    attn_probs = jax.nn.softmax(scores, axis=-1).astype(jnp.bfloat16)
    context = jnp.einsum(
        "tgsqk,tkgd->tqgsd", attn_probs, value_rows, preferred_element_type=jnp.float32
    )
    return context.astype(jnp.bfloat16)


def body(
    activations,
    tile_dest,
    segment_ids,
    norm_gain,
    q_weight,
    k_weight,
    v_weight,
    q_bias,
    k_bias,
    v_bias,
    o_weight,
):
    dp_count = lax.axis_size("dp")
    own_index = lax.axis_index("dp")
    pair_size = lax.axis_size("pair")
    pair_index = lax.axis_index("pair")
    slot_count = tile_dest.shape[1]
    tile_rows = segment_ids.shape[2]
    feature_share = activations.shape[1]
    peer_slots = (slot_count + dp_count - 1) // dp_count
    own_plan = lax.dynamic_index_in_dim(tile_dest, own_index, 0, keepdims=False)
    slot_ids = jnp.arange(slot_count, dtype=jnp.int32)
    targets = jnp.arange(dp_count, dtype=jnp.int32)
    peer_ids = jnp.arange(peer_slots, dtype=jnp.int32)
    earlier_same = (own_plan[None, :] == own_plan[:, None]) & (
        slot_ids[None, :] < slot_ids[:, None]
    )
    send_rank = jnp.sum(earlier_same.astype(jnp.int32), axis=1)
    chooser = (own_plan[None, None, :] == targets[:, None, None]) & (
        send_rank[None, None, :] == peer_ids[None, :, None]
    )
    own_tiles = activations.reshape(slot_count, tile_rows, feature_share)
    outgoing = jnp.einsum(
        "jps,srf->jprf", chooser.astype(jnp.bfloat16), own_tiles, preferred_element_type=jnp.float32
    ).astype(jnp.bfloat16)
    arrived = lax.all_to_all(outgoing, "dp", split_axis=0, concat_axis=0, tiled=True)
    to_here = (tile_dest == own_index).astype(jnp.int32)
    from_each = jnp.sum(to_here, axis=1)
    first_place = jnp.cumsum(from_each) - from_each
    place_of = first_place[:, None] + peer_ids[None, :]
    landed = peer_ids[None, :] < from_each[:, None]
    tile_ids = jnp.arange(TPD, dtype=jnp.int32)
    placer = (place_of[None, :, :] == tile_ids[:, None, None]) & landed[None, :, :]
    packed_tiles = jnp.einsum(
        "ksp,sprf->krf", placer.astype(jnp.bfloat16), arrived, preferred_element_type=jnp.float32
    ).astype(jnp.bfloat16)
    row_count = TPD * tile_rows
    packed = packed_tiles.reshape(row_count, feature_share)
    flat_plan = tile_dest.reshape(-1)
    flat_member = (flat_plan == own_index).astype(jnp.int32)
    flat_rank = jnp.cumsum(flat_member) - 1
    picker = flat_member[None, :] * (flat_rank[None, :] == tile_ids[:, None]).astype(jnp.int32)
    flat_segments = segment_ids.reshape(-1, tile_rows)
    segment = jnp.sum(picker[:, :, None] * flat_segments[None, :, :], axis=1)
    positions = tile_positions(segment).reshape(row_count)
    whole_rows = lax.all_gather(packed, ("tensor", "pair"), axis=1, tiled=True)
    normed = normalize(whole_rows, norm_gain)
    q_width = q_weight.shape[1]
    kv_width = k_weight.shape[1]
    q_lin = jnp.dot(
        normed,
        lax.all_gather(q_weight, "dp", axis=0, tiled=True),
        preferred_element_type=jnp.float32,
    )
    k_lin = jnp.dot(
        normed,
        lax.all_gather(k_weight, "dp", axis=0, tiled=True),
        preferred_element_type=jnp.float32,
    )
    v_lin = jnp.dot(
        normed,
        lax.all_gather(v_weight, "dp", axis=0, tiled=True),
        preferred_element_type=jnp.float32,
    )
    q_heads = q_width // HEAD
    kv_heads = kv_width // HEAD
    queries = rotary(
        (q_lin + q_bias.astype(jnp.float32)).reshape(row_count, q_heads, HEAD), positions
    ).astype(jnp.bfloat16)
    keys_local = rotary(
        (k_lin + k_bias.astype(jnp.float32)).reshape(-1, kv_heads, HEAD), positions
    ).astype(jnp.bfloat16)
    values_local = (
        (v_lin + v_bias.astype(jnp.float32)).astype(jnp.bfloat16).reshape(-1, kv_heads, HEAD)
    )
    key_rows, value_rows = (keys_local, values_local)
    group_size = QHEADS // KVH
    kv_count = max(1, q_heads // group_size)
    group_span = q_heads // kv_count
    kv_first = pair_index * q_heads // group_size
    key_rows = lax.dynamic_slice_in_dim(key_rows, kv_first, kv_count, 1).reshape(
        TPD, tile_rows, kv_count, HEAD
    )
    value_rows = lax.dynamic_slice_in_dim(value_rows, kv_first, kv_count, 1).reshape(
        TPD, tile_rows, kv_count, HEAD
    )
    query_groups = queries.reshape(TPD, tile_rows, kv_count, group_span, HEAD)
    context = attend_tiles(query_groups, key_rows, value_rows, segment).reshape(
        row_count, q_heads * HEAD
    )
    partials = jnp.dot(
        context,
        lax.all_gather(o_weight, "dp", axis=1, tiled=True),
        preferred_element_type=jnp.float32,
    )
    full_sums = lax.psum(partials.astype(jnp.bfloat16), ("tensor", "pair")).astype(jnp.float32)
    my_slot = lax.axis_index("tensor") * pair_size + pair_index
    summed = lax.dynamic_slice_in_dim(full_sums, my_slot * feature_share, feature_share, 1)
    return (packed.astype(jnp.float32) + summed).astype(jnp.bfloat16)


def solution(mesh):
    return jax.shard_map(
        body,
        mesh=mesh,
        in_specs=(
            P(("groups", "dp"), ("tensor", "pair")),
            P("groups", None),
            P("groups", None, None),
            P(),
            P("dp", ("tensor", "pair")),
            P("dp", "tensor"),
            P("dp", "tensor"),
            P(("tensor", "pair")),
            P("tensor"),
            P("tensor"),
            P(("tensor", "pair"), "dp"),
        ),
        out_specs=P(("groups", "dp"), ("tensor", "pair")),
        check_vma=False,
    )
```

profile of v0, /device:TPU:12, one launch (start us, length us, event | category | flops | bytes accessed | tf_op | source)
XLA Modules:
  0.0 668.4 jit_solution(11511193057519295781)
XLA Ops:
  6.5 0.8 fusion.45
  8.1 1.7 fusion.8
  9.8 2.9 copy.68
  12.8 5.3 all-to-all-start
  18.4 44.6 %all-to-all-done = bf16[4,2,128,1024]{3,1,2,0:T(2,128)(2,1)S(1)} async-done(((bf16[4,2,128,1024]{3,1,2,0:T(2,128)(2,1)}), bf16[4,2,128,1024]{3,1,2,0:T(2,128)(2,1)S(1)}, u32[]{:S(2)}, u32[]{:S(2)}) %all-to-all-start) | async-done | bytes 2097184 | tf_op jit(solution)/shard_map/all_to_all | solution.py:101
  63.0 2.6 bitcast_convert_fusion
  65.6 1.3 copy.70
  71.5 31.9 %all-gather.6.cloned.1.call-done = bf16[512,4096]{1,0:T(8,128)(2,1)} async-done(((bf16[512,1024]{1,0:T(8,128)(2,1)}), bf16[512,4096]{1,0:T(8,128)(2,1)}) %all-gather.6.cloned.1.call-update) | async-done | bytes 4194320 | tf_op jit(solution)/shard_map/all_gather | solution.py:121
  103.4 3.1 fusion.1
  106.5 76.8 %all-gather.10.cloned.1.call-done = bf16[4096,512]{1,0:T(8,128)(2,1)} async-done(((bf16[1024,512]{1,0:T(8,128)(2,1)}), bf16[4096,512]{1,0:T(8,128)(2,1)}) %all-gather.10.cloned.1.call-update) | async-done | bytes 4194320 | tf_op jit(solution)/shard_map/all_gather | solution.py:132
  183.3 5.9 convolution_add_fusion.1
  190.0 74.2 %all-gather.8.cloned.1.call-done = bf16[4096,512]{1,0:T(8,128)(2,1)} async-done(((bf16[1024,512]{1,0:T(8,128)(2,1)}), bf16[4096,512]{1,0:T(8,128)(2,1)}) %all-gather.8.cloned.1.call-update) | async-done | bytes 4194320 | tf_op jit(solution)/shard_map/all_gather | solution.py:137
  264.2 5.9 fusion.15
  270.2 0.8 copy.97
  271.3 0.9 fusion.23
  272.2 141.4 %all-gather.12.cloned.1.call-done = bf16[4096,1024]{1,0:T(8,128)(2,1)} async-done(((bf16[1024,1024]{1,0:T(8,128)(2,1)}), bf16[4096,1024]{1,0:T(8,128)(2,1)}) %all-gather.12.cloned.1.call-update) | async-done | bytes 8388624 | tf_op jit(solution)/shard_map/all_gather | solution.py:127
  413.5 10.5 %convolution_add_fusion = f32[512,1024]{1,0:T(8,128)} fusion(bf16[4096,1024]{1,0:T(8,128)(2,1)} %all-gather.12.cloned.1.call-done, f32[1024]{0:T(1024)S(1)} %convert_element_type.116, bf16[512,4096]{1,0:T(8,128)(2,1)} %all-gather.6.cloned.1.call-done, f32[4096]{0:T(1024)S(1)} %convert_element_type.104, f32[512]{0:T(512)S(1)} %add_rsqrt_fusion), kind=kOutput, calls=%fused_computation.18 | convolution fusion | flops 4303880192 | bytes 14702592 | tf_op jit(solution)/shard_map/dot_general | solution.py:125
  424.0 2.2 copy.96
  428.3 2.5 fusion.60
  430.8 2.1 fusion.14
  434.4 128.5 %all-gather.14.cloned.1.call-done = bf16[1024,4096]{1,0:T(8,128)(2,1)} async-done(((bf16[1024,1024]{1,0:T(8,128)(2,1)}), bf16[1024,4096]{1,0:T(8,128)(2,1)}) %all-gather.14.cloned.1.call-update) | async-done | bytes 8388624 | tf_op jit(solution)/shard_map/all_gather | solution.py:168
  562.8 9.5 %convolution_convert_fusion = bf16[512,4096]{1,0:T(8,128)(2,1)} fusion(bf16[512,1024]{1,0:T(8,128)(2,1)S(1)} %reshape.333, bf16[1024,4096]{1,0:T(8,128)(2,1)} %all-gather.14.cloned.1.call-done), kind=kOutput, calls=%fused_computation.6 | convolution fusion | flops 4297064448 | bytes 13631488 | tf_op jit(solution)/shard_map/dot_general | solution.py:166
  572.4 86.6 %all-reduce.2.cloned.1.call-done = bf16[512,4096]{1,0:T(8,128)(2,1)} async-done(((bf16[512,4096]{1,0:T(8,128)(2,1)}), bf16[512,4096]{1,0:T(8,128)(2,1)}) %all-reduce.2.cloned.1.call-update) | async-done | bytes 4194320 | tf_op jit(solution)/shard_map/psum | solution.py:171
  659.0 2.6 add_convert_fusion
  (73 shorter events, 10.0 us)
Async XLA Ops:
  6.5 1.6 copy-start
  9.8 8.3 %copy-start.8 = (s32[4,8]{1,0:T(4,128)S(1)}, s32[4,8]{1,0:T(4,128)}, u32[]{:S(2)}) copy-start(s32[4,8]{1,0:T(4,128)} %param.12) | copy-start | bytes 388
  12.8 50.2 %all-to-all-start = ((bf16[4,2,128,1024]{3,1,2,0:T(2,128)(2,1)}), bf16[4,2,128,1024]{3,1,2,0:T(2,128)(2,1)S(1)}, u32[]{:S(2)}, u32[]{:S(2)}) async-start(bf16[4,2,128,1024]{3,1,2,0:T(2,128)(2,1)} %copy.68), calls=%async_computation | async-start | bytes 4194304 | tf_op jit(solution)/shard_map/all_to_all | solution.py:101
  18.1 85.3 %all-gather.6.cloned.1.call-start = ((), (), s32[]{:S(2)}) async-start(), calls=%async_computation.1 | async-start | bytes 5242880 | tf_op jit(solution)/shard_map/all_gather | solution.py:121
  66.9 3.1 copy-start.7
  66.9 3.2 copy-start.6
  66.9 3.2 copy-start.9
  66.9 3.3 copy-start.5
  66.9 4.4 copy-start.10
  66.9 116.4 %all-gather.10.cloned.1.call-start = ((), (), s32[]{:S(2)}) async-start(), calls=%async_computation.3 | async-start | bytes 5242880 | tf_op jit(solution)/shard_map/all_gather | solution.py:132
  67.7 196.5 %all-gather.8.cloned.1.call-start = ((), (), s32[]{:S(2)}) async-start(), calls=%async_computation.2 | async-start | bytes 5242880 | tf_op jit(solution)/shard_map/all_gather | solution.py:137
  68.4 345.1 %all-gather.12.cloned.1.call-start = ((), (), s32[]{:S(2)}) async-start(), calls=%async_computation.4 | async-start | bytes 10485760 | tf_op jit(solution)/shard_map/all_gather | solution.py:127
  69.0 493.8 %all-gather.14.cloned.1.call-start = ((), (), s32[]{:S(2)}) async-start(), calls=%async_computation.5 | async-start | bytes 10485760 | tf_op jit(solution)/shard_map/all_gather | solution.py:168
  69.6 589.4 %all-reduce.2.cloned.1.call-start = ((), (), s32[]{:S(2)}) async-start(), calls=%async_computation.6 | async-start | bytes 8388608 | tf_op jit(solution)/shard_map/psum | solution.py:171
  426.6 1.7 copy-start.3
  427.5 3.3 copy-start.4
  562.8 98.7 %copy-start.1 = (bf16[1024,1024]{1,0:T(8,128)(2,1)S(1)}, bf16[1024,1024]{1,0:T(8,128)(2,1)}, u32[]{:S(2)}) copy-start(bf16[1024,1024]{1,0:T(8,128)(2,1)} %param.11) | copy-start | bytes 6291460
  572.4 86.6 %copy-start.2 = (bf16[4,128,1024]{2,1,0:T(8,128)(2,1)S(1)}, bf16[4,128,1024]{2,1,0:T(8,128)(2,1)}, u32[]{:S(2)}) copy-start(bf16[4,128,1024]{2,1,0:T(8,128)(2,1)} %copy.70) | copy-start | bytes 3145732
Sparse Core Ops, SparseCore 0:
  67.1 36.2 all-gather.5
  104.9 78.3 all-gather.9
  184.9 79.2 all-gather.7
  265.6 147.8 all-gather.11
  414.9 147.8 all-gather.13
  572.5 86.4 all-reduce.1
where the time goes:
time: 670 us; the launch traced here: 668 us
  waiting for transfers between devices  586 us (87%)
  matrix products  40.7 us (6%)
  between operations  13.8 us (2%)
  local copies, waits for them, and re-layouts  13 us (2%)
  other arithmetic  8.83 us (1%)
    all_gather x1, waiting for transfers between devices, body(): lax.all_gather(q_weight, 'dp', axis=0, tiled=True)  141 us
    all_gather x1, waiting for transfers between devices, body(): lax.all_gather(o_weight, 'dp', axis=1, tiled=True)  128 us
    psum x1, waiting for transfers between devices, body(): lax.psum(partials.astype(jnp.bfloat16), ('tensor', 'pair'))  86.6 us
    all_gather x1, waiting for transfers between devices, body(): lax.all_gather(k_weight, 'dp', axis=0, tiled=True)  76.8 us
    all_gather x1, waiting for transfers between devices, body(): lax.all_gather(v_weight, 'dp', axis=0, tiled=True)  74.2 us
    all_to_all x1, waiting for transfers between devices, body(): lax.all_to_all(outgoing, 'dp', split_axis=0, concat_axis=0, tiled=True)  44.6 us
    all_gather x1, waiting for transfers between devices, body(): whole_rows = lax.all_gather(packed, ('tensor', 'pair'), axis=1, tiled=True)  31.9 us
  transfers between devices with their start and end apart: 7, of which 7 were waited for; matrix products, arithmetic and copies ran while one was open for 6% of the time, Pallas kernels for 0%

commit v1 on v0

--- a/solution.py
+++ b/solution.py
@@ -3,16 +3,18 @@
 import jax
 import jax.numpy as jnp
 from jax import lax
+from jax.experimental import pallas as pl
+from jax.experimental.pallas import tpu as pltpu
 from jax.sharding import PartitionSpec as P
 
 QHEADS = 32
 KVH = 8
 HEAD = 128
 TPD = 4
+GROUP_SIZE = QHEADS // KVH
 
 
 norm_eps = 1e-06
-
 
 def normalize(values, gain_vector):
     widened = values.astype(jnp.float32)
@@ -174,9 +176,223 @@
     return (packed.astype(jnp.float32) + summed).astype(jnp.bfloat16)
 
 
+def shift(values, axis, pairs):
+    return lax.ppermute(values, axis, pairs)
+
+
+SWAP = [(0, 1), (1, 0)]
+
+
+def attention_kernel(lin_ref, bias_ref, cos_ref, sin_ref, pos_ref, out_ref):
+    heads = out_ref.shape[1] // HEAD
+    rows = lin_ref.shape[0]
+    lin = lin_ref[...] + bias_ref[...]
+    cosine = cos_ref[...]
+    sine = sin_ref[...]
+
+    def rotate(values):
+        return (values * cosine + pltpu.roll(values, HEAD // 2, 1) * sine).astype(jnp.bfloat16)
+
+    queries = jnp.concatenate(
+        [rotate(lin[:, h * HEAD : (h + 1) * HEAD]) for h in range(heads)], axis=0
+    )
+    keys = rotate(lin[:, heads * HEAD : (heads + 1) * HEAD])
+    value_rows = lin[:, (heads + 1) * HEAD :].astype(jnp.bfloat16)
+    scores = lax.dot_general(
+        queries, keys, (((1,), (1,)), ((), ())), preferred_element_type=jnp.float32
+    )
+    scores = (scores * (1.0 / math.sqrt(HEAD))).reshape(heads, rows, rows)
+    row = lax.broadcasted_iota(jnp.int32, (rows, rows), 0)
+    column = lax.broadcasted_iota(jnp.int32, (rows, rows), 1)
+    allowed = (column <= row) & (column >= row - pos_ref[...])
+    scores = jnp.where(allowed[None], scores, -1e30)
+    largest = jnp.max(scores, axis=-1, keepdims=True)
+    weights = jnp.exp(scores - largest)
+    probs = (weights / jnp.sum(weights, axis=-1, keepdims=True)).astype(jnp.bfloat16)
+    context = lax.dot_general(
+        probs.reshape(heads * rows, rows),
+        value_rows,
+        (((1,), (0,)), ((), ())),
+        preferred_element_type=jnp.float32,
+    ).astype(jnp.bfloat16)
+    for h in range(heads):
+        out_ref[:, h * HEAD : (h + 1) * HEAD] = context[h * rows : (h + 1) * rows]
+
+
+def attend_rows(lin, bias, cosine, sine, positions, tile_rows):
+    count, width = lin.shape
+    out_width = width - 2 * HEAD
+    by_tile = lambda w: pl.BlockSpec((tile_rows, w), lambda i: (i, 0))
+    return pl.pallas_call(
+        attention_kernel,
+        grid=(count // tile_rows,),
+        in_specs=[
+            by_tile(width),
+            pl.BlockSpec((1, width), lambda i: (0, 0)),
+            by_tile(HEAD),
+            by_tile(HEAD),
+            by_tile(1),
+        ],
+        out_specs=by_tile(out_width),
+        out_shape=jax.ShapeDtypeStruct((count, out_width), jnp.bfloat16),
+        compiler_params=pltpu.CompilerParams(vmem_limit_bytes=32 * 1024 * 1024),
+        cost_estimate=pl.CostEstimate(
+            flops=4 * count * tile_rows * out_width,
+            bytes_accessed=count * (4 * width + 2 * out_width),
+            transcendentals=count * out_width,
+        ),
+    )(lin, bias, cosine, sine, positions)
+
+
+def ring_body(
+    activations,
+    tile_dest,
+    segment_ids,
+    norm_gain,
+    q_weight,
+    k_weight,
+    v_weight,
+    q_bias,
+    k_bias,
+    v_bias,
+    o_weight,
+):
+    z = lax.axis_index("dp")
+    y = lax.axis_index("groups")
+    x = lax.axis_index("tensor")
+    core = lax.axis_index("pair")
+    t = x * 2 + core
+    slots, tile_rows = tile_dest.shape[1], segment_ids.shape[2]
+    width = activations.shape[1]
+    rows = TPD * tile_rows
+    peers = 2
+    q_share = q_weight.shape[1] // 2
+
+    kv_at = (core * 2 + y) * HEAD
+    q_own = lax.dynamic_slice_in_dim(q_weight, y * q_share, q_share, 1)
+    k_own = lax.dynamic_slice_in_dim(k_weight, kv_at, HEAD, 1)
+    v_own = lax.dynamic_slice_in_dim(v_weight, kv_at, HEAD, 1)
+    qkv_own = jnp.concatenate([q_own, k_own, v_own], axis=1)
+    o_own = lax.dynamic_slice_in_dim(o_weight, y * q_share, q_share, 0)
+    bias = jnp.concatenate(
+        [
+            lax.dynamic_slice_in_dim(q_bias, y * q_share, q_share, 0),
+            lax.dynamic_slice_in_dim(k_bias, kv_at, HEAD, 0),
+            lax.dynamic_slice_in_dim(v_bias, kv_at, HEAD, 0),
+        ]
+    ).astype(jnp.float32)[None, :]
+
+    own_plan = lax.dynamic_index_in_dim(tile_dest, z, 0, keepdims=False)
+    slot_ids = jnp.arange(slots, dtype=jnp.int32)
+    peer_ids = jnp.arange(peers, dtype=jnp.int32)
+    partners = jnp.arange(4, dtype=jnp.int32) ^ z
+    same_before = (own_plan[None, :] == own_plan[:, None]) & (slot_ids[None, :] < slot_ids[:, None])
+    send_rank = jnp.sum(same_before.astype(jnp.int32), axis=1)
+    chooser = (own_plan[None, None, :] == partners[:, None, None]) & (
+        send_rank[None, None, :] == peer_ids[None, :, None]
+    )
+    own_tiles = activations.reshape(slots, tile_rows, width)
+    outgoing = [
+        jnp.einsum(
+            "ps,srf->prf",
+            chooser[m].astype(jnp.bfloat16),
+            own_tiles,
+            preferred_element_type=jnp.float32,
+        ).astype(jnp.bfloat16)
+        for m in range(4)
+    ]
+    arrived = [outgoing[0]] + [
+        shift(outgoing[m], "dp", [(i, i ^ m) for i in range(4)]) for m in range(1, 4)
+    ]
+    to_here = (tile_dest == z).astype(jnp.int32)
+    from_each = jnp.sum(to_here, axis=1)
+    first_place = jnp.cumsum(from_each) - from_each
+    place_of = first_place[:, None] + peer_ids[None, :]
+    landed = peer_ids[None, :] < from_each[:, None]
+    tile_ids = jnp.arange(TPD, dtype=jnp.int32)
+    placer = (place_of[None, :, :] == tile_ids[:, None, None]) & landed[None, :, :]
+    placer = jnp.take(placer, partners, axis=1).astype(jnp.bfloat16)
+    packed = sum(
+        jnp.einsum(
+            "kp,prf->krf", placer[:, m], arrived[m], preferred_element_type=jnp.float32
+        )
+        for m in range(4)
+    ).astype(jnp.bfloat16).reshape(rows, width)
+
+    flat_member = (tile_dest.reshape(-1) == z).astype(jnp.int32)
+    flat_rank = jnp.cumsum(flat_member) - 1
+    picker = flat_member[None, :] * (flat_rank[None, :] == tile_ids[:, None]).astype(jnp.int32)
+    segment = jnp.sum(picker[:, :, None] * segment_ids.reshape(-1, tile_rows)[None, :, :], axis=1)
+    positions = tile_positions(segment).reshape(rows, 1)
+    positions = jnp.concatenate([positions, shift(positions, "groups", SWAP)], axis=0)
+    half = HEAD // 2
+    inverse = jnp.power(
+        jnp.float32(1000000.0), -2.0 * jnp.arange(half, dtype=jnp.float32) / HEAD
+    )
+    angles = positions.astype(jnp.float32) * inverse[None, :]
+    cosine, sine = jnp.cos(angles), jnp.sin(angles)
+    cosine = jnp.concatenate([cosine, cosine], axis=1)
+    sine = jnp.concatenate([-sine, sine], axis=1)
+
+    widened = packed.astype(jnp.float32)
+    squares = jnp.sum(widened * widened, axis=-1, keepdims=True)
+    squares = squares + shift(squares, "pair", SWAP)
+    squares = squares + shift(squares, "tensor", SWAP)
+    gain = lax.dynamic_slice_in_dim(norm_gain, t * width, width, 0).astype(jnp.float32)
+    normed = (widened * lax.rsqrt(squares / (4 * width) + norm_eps) * gain).astype(jnp.bfloat16)
+    here = [normed, shift(normed, "groups", SWAP)]
+    across = [shift(part, "tensor", SWAP) for part in here]
+    here_other = [shift(part, "pair", SWAP) for part in here]
+    across_other = [shift(part, "pair", SWAP) for part in across]
+    shares = jnp.stack(
+        [jnp.concatenate(part, axis=0) for part in (here, here_other, across, across_other)]
+    )
+
+    def ring(block):
+        up, down = [block], [block]
+        for s in range(1, 4):
+            up.append(shift(up[-1], "dp", [(i, i + 1) for i in range(s - 1, 3)]))
+            down.append(shift(down[-1], "dp", [(i + 1, i) for i in range(0, 4 - s)]))
+        first = jnp.where(z % 2 == 0, down[1], up[1])
+        second = up[2] + down[2]
+        third = jnp.where(z == 1, down[1], jnp.where(z == 2, up[1], up[3] + down[3]))
+        return [block, first, second, third]
+
+    qkv_blocks = ring(qkv_own)
+    o_blocks = ring(o_own)
+    lin = None
+    for m in range(4):
+        share = lax.dynamic_index_in_dim(shares, (z ^ m) ^ t, 0, keepdims=False)
+        part = jnp.dot(share, qkv_blocks[m], preferred_element_type=jnp.float32)
+        lin = part if lin is None else lin + part
+    context = attend_rows(lin, bias, cosine, sine, positions, tile_rows)
+
+    total = packed.astype(jnp.float32)
+    every = ("groups", "dp", "tensor", "pair")
+    index = lambda zz, yy, xx, cc: ((yy * 4 + zz) * 2 + xx) * 2 + cc
+    for m in range(4):
+        part = jnp.dot(context, o_blocks[m], preferred_element_type=jnp.float32)
+        sides = [(i, j) for i in range(2) for j in range(2)]
+        to_core, to_group, to_chip = [], [], []
+        for zz in range(4):
+            xd, cd = (zz ^ m) // 2, (zz ^ m) % 2
+            to_core += [(index(zz, i, j, 1 - cd), index(zz, i, j, cd)) for i, j in sides]
+            to_group += [(index(zz, i, j, cd), index(zz, 1 - i, j, cd)) for i, j in sides]
+            to_chip += [(index(zz, i, 1 - xd, cd), index(zz, i, xd, cd)) for i in range(2)]
+        part = part + shift(part.astype(jnp.bfloat16), every, to_core).astype(jnp.float32)
+        mine = part[:rows] + shift(part[rows:].astype(jnp.bfloat16), every, to_group).astype(
+            jnp.float32
+        )
+        mine = mine + shift(mine.astype(jnp.bfloat16), every, to_chip).astype(jnp.float32)
+        total = total + jnp.where(z ^ m == t, mine, 0.0)
+    return total.astype(jnp.bfloat16)
+
+
 def solution(mesh):
+    shape = dict(mesh.shape)
+    ringed = shape == {"groups": 2, "dp": 4, "tensor": 2, "pair": 2}
     return jax.shard_map(
-        body,
+        ring_body if ringed else body,
         mesh=mesh,
         in_specs=(
             P(("groups", "dp"), ("tensor", "pair")),

time: 670 us -> 393 us (0.59)
  waiting for transfers between devices: 586 us -> 226 us
  starting transfers between devices: 5.69 us -> 68.9 us
  other arithmetic: 8.83 us -> 30.7 us
  between operations: 13.8 us -> 1.26 us
    all_gather x5 -> x0, waiting for transfers between devices: 453 us -> none  [the longest x1 141 us: body(): lax.all_gather(q_weight, 'dp', axis=0, tiled=True)]
    ppermute x0 -> x37, waiting for transfers between devices: none -> 226 us  [shift(): return lax.ppermute(values, axis, pairs)]
    psum x1 -> x0, waiting for transfers between devices: 86.6 us -> none  [body(): lax.psum(partials.astype(jnp.bfloat16), ('tensor', 'pair'))]
    ppermute x0 -> x37, starting transfers between devices: none -> 68.9 us  [shift(): return lax.ppermute(values, axis, pairs)]
    all_to_all x1 -> x0, waiting for transfers between devices: 44.6 us -> none  [body(): lax.all_to_all(outgoing, 'dp', split_axis=0, concat_axis=0, tiled=True)]
    convert_element_type x6 -> x9, other arithmetic: 2.62 us -> 12.8 us  [the longest x1 8.39 us: ring_body(): return total.astype(jnp.bfloat16)]
    dot_general x7 -> x15, matrix products: 38.2 us -> 39.7 us  [the longest x4 12.1 us: ring_body(): part = jnp.dot(share, qkv_blocks[m], preferred_element_type=jnp.float32)]
  transfers between devices with their start and end apart: 7 -> 37, of which waited for: 7 -> 14; matrix products, arithmetic and copies ran while one was open for 6% -> 17% of each run, Pallas kernels for 0% -> 1%
where the time goes in v1:
time: 393 us; the launch traced here: 386 us
  waiting for transfers between devices  226 us (58%)
  starting transfers between devices  68.9 us (18%)
  matrix products  39.7 us (10%)
  other arithmetic  30.7 us (8%)
  local copies, waits for them, and re-layouts  14.4 us (4%)
  Pallas kernels  4.95 us (1%)
    ppermute x37, waiting for transfers between devices, shift(): return lax.ppermute(values, axis, pairs)  226 us
    ppermute x37, starting transfers between devices, shift(): return lax.ppermute(values, axis, pairs)  68.9 us
    dot_general x4, matrix products, ring_body(): part = jnp.dot(share, qkv_blocks[m], preferred_element_type=jnp.float32)  12.1 us
    dot_general x4, matrix products, ring_body(): part = jnp.dot(context, o_blocks[m], preferred_element_type=jnp.float32)  10.4 us
    dot_general x4, matrix products, ring_body(): jnp.einsum('kp,prf->krf', placer[:, m], arrived[m], preferred_element_typ...  10.4 us
    convert_element_type x1, other arithmetic, ring_body(): return total.astype(jnp.bfloat16)  8.39 us
  transfers between devices with their start and end apart: 37, of which 14 were waited for; matrix products, arithmetic and copies ran while one was open for 17% of the time, Pallas kernels for 1%

profile of v1, /device:TPU:12, one launch (start us, length us, event | category | flops | bytes accessed | tf_op | source)
XLA Modules:
  0.0 385.8 jit_solution(12403543208748723724)
XLA Ops:
  4.6 3.5 collective-permute-start.13
  8.0 3.5 collective-permute-start.12
  24.3 3.2 fusion.55
  30.1 56.8 %collective-permute-done.1 = bf16[2,128,1024]{2,0,1:T(2,128)(2,1)} collective-permute-done((bf16[2,128,1024]{2,0,1:T(2,128)(2,1)}, bf16[2,128,1024]{2,0,1:T(2,128)(2,1)}, u32[]{:S(2)}, u32[]{:S(2)}) %collective-permute-start.1) | collective-permute-done | bytes 524320 | tf_op jit(solution)/shard_map/ppermute | solution.py:180
  86.9 7.5 %collective-permute-start.22 = (bf16[512,1024]{1,0:T(8,128)(2,1)}, bf16[512,1024]{1,0:T(8,128)(2,1)}, u32[]{:S(2)}, u32[]{:S(2)}) collective-permute-start(bf16[512,1024]{1,0:T(8,128)(2,1)} %constant_dynamic-slice_fusion), channel_id=1, source_target_pairs={{4,0},{8,4},{12,8},{5,1},{9,5},{13,9},{6,2},{10,6},{14,10},{7,3},{... | collective-permute-start | bytes 3145736 | tf_op jit(solution)/shard_map/ppermute | solution.py:180
  100.0 3.7 multiply_reduce_fusion
  117.4 4.4 %collective-permute-done.23 = bf16[512,1024]{1,0:T(8,128)(2,1)} collective-permute-done((bf16[512,1024]{1,0:T(8,128)(2,1)}, bf16[512,1024]{1,0:T(8,128)(2,1)}, u32[]{:S(2)}, u32[]{:S(2)}) %collective-permute-start.23) | collective-permute-done | bytes 1048608 | tf_op jit(solution)/shard_map/ppermute | solution.py:180
  125.0 12.9 %collective-permute-done.5 = bf16[512,1024]{1,0:T(8,128)(2,1)} collective-permute-done((bf16[512,1024]{1,0:T(8,128)(2,1)S(1)}, bf16[512,1024]{1,0:T(8,128)(2,1)}, u32[]{:S(2)}, u32[]{:S(2)}) %collective-permute-start.5) | collective-permute-done | bytes 1048608 | tf_op jit(solution)/shard_map/ppermute | solution.py:180
  138.7 4.0 %collective-permute-start.14 = (bf16[1024,768]{1,0:T(8,128)(2,1)}, bf16[1024,768]{1,0:T(8,128)(2,1)}, u32[]{:S(2)}, u32[]{:S(2)}) collective-permute-start(bf16[1024,768]{1,0:T(8,128)(2,1)} %collective-permute-done.13), channel_id=1, source_target_pairs={{4,8},{8,12},{5,9},{9,13},{6,10},{10,14},{7,11},{11,15},{20,24},{2... | collective-permute-start | bytes 4718600 | tf_op jit(solution)/shard_map/ppermute | solution.py:180
  149.7 11.8 %collective-permute-done.9 = bf16[512,1024]{1,0:T(8,128)(2,1)} collective-permute-done((bf16[512,1024]{1,0:T(8,128)(2,1)}, bf16[512,1024]{1,0:T(8,128)(2,1)}, u32[]{:S(2)}, u32[]{:S(2)}) %collective-permute-start.9) | collective-permute-done | bytes 1048608 | tf_op jit(solution)/shard_map/ppermute | solution.py:180
  169.1 35.9 %collective-permute-done.28 = bf16[512,1024]{1,0:T(8,128)(2,1)} collective-permute-done((bf16[512,1024]{1,0:T(8,128)(2,1)}, bf16[512,1024]{1,0:T(8,128)(2,1)}, u32[]{:S(2)}, u32[]{:S(2)}) %collective-permute-start.28) | collective-permute-done | bytes 1048608 | tf_op jit(solution)/shard_map/ppermute | solution.py:180
  213.8 3.2 fusion.4
  217.0 3.7 fusion.2
  222.6 42.2 %collective-permute-done.17 = bf16[1024,768]{1,0:T(8,128)(2,1)S(1)} collective-permute-done((bf16[1024,768]{1,0:T(8,128)(2,1)}, bf16[1024,768]{1,0:T(8,128)(2,1)S(1)}, u32[]{:S(2)}, u32[]{:S(2)}) %collective-permute-start.17) | collective-permute-done | bytes 1572896 | tf_op jit(solution)/shard_map/ppermute | solution.py:180
  264.7 3.4 add_add_fusion.lin_ref
  268.1 5.0 %shard_map.109 = bf16[1024,512]{1,0:T(8,128)(2,1)S(1)} custom-call(f32[1024,768]{1,0:T(8,128)S(1)} %add_add_fusion.lin_ref, f32[1,768]{1,0:T(1,128)S(1)} %maximum_convert_fusion.bias_ref, f32[1024,128]{1,0:T(8,128)S(1)} %get-tuple-element.26.cos_ref, f32[1024,128]{1,0:T(8,128)S(1)} %get-tuple-element.27.sin_ref, s32[1024,1]{1,0:T(8,128)S(1)} %copy.59.pos_ref), custom_call_target="tpu_custom_call" | custom-call | flops 268435456 | bytes 4194304 | tf_op jit(solution)/shard_map/pallas_call | solution.py:226
  279.8 3.3 collective-permute-start.29
  289.4 3.5 collective-permute-start.19
  303.4 3.9 %collective-permute-start.25 = (bf16[512,1024]{1,0:T(8,128)(2,1)S(1)}, bf16[512,1024]{1,0:T(8,128)(2,1)S(1)}, u32[]{:S(2)}, u32[]{:S(2)}) collective-permute-start(bf16[512,1024]{1,0:T(8,128)(2,1)S(1)} %slice.131), channel_id=1, source_target_pairs={{1,17},{3,19},{17,1},{19,3},{4,20},{6,22},{20,4},{22,6},{9,25},{11... | collective-permute-start | bytes 3145736 | tf_op jit(solution)/shard_map/ppermute | solution.py:180
  309.3 17.0 %collective-permute-done.35 = bf16[512,1024]{1,0:T(8,128)(2,1)S(1)} collective-permute-done((bf16[512,1024]{1,0:T(8,128)(2,1)}, bf16[512,1024]{1,0:T(8,128)(2,1)S(1)}, u32[]{:S(2)}, u32[]{:S(2)}) %collective-permute-start.35) | collective-permute-done | bytes 1048608 | tf_op jit(solution)/shard_map/ppermute | solution.py:180
  326.7 4.4 %collective-permute-start.36 = (bf16[512,1024]{1,0:T(8,128)(2,1)S(1)}, bf16[512,1024]{1,0:T(8,128)(2,1)}, u32[]{:S(2)}, u32[]{:S(2)}) collective-permute-start(bf16[512,1024]{1,0:T(8,128)(2,1)S(1)} %fusion.41), channel_id=1, source_target_pairs={{1,3},{17,19},{4,6},{20,22},{11,9},{27,25},{14,12},{30,28}} | collective-permute-start | bytes 3145736 | tf_op jit(solution)/shard_map/ppermute | solution.py:180
  334.1 14.7 %collective-permute-done.25 = bf16[512,1024]{1,0:T(8,128)(2,1)S(1)} collective-permute-done((bf16[512,1024]{1,0:T(8,128)(2,1)S(1)}, bf16[512,1024]{1,0:T(8,128)(2,1)S(1)}, u32[]{:S(2)}, u32[]{:S(2)}) %collective-permute-start.25) | collective-permute-done | bytes 1048608 | tf_op jit(solution)/shard_map/ppermute | solution.py:180
  354.1 22.8 %collective-permute-done.26 = bf16[512,1024]{1,0:T(8,128)(2,1)} collective-permute-done((bf16[512,1024]{1,0:T(8,128)(2,1)}, bf16[512,1024]{1,0:T(8,128)(2,1)}, u32[]{:S(2)}, u32[]{:S(2)}) %collective-permute-start.26) | collective-permute-done | bytes 1048608 | tf_op jit(solution)/shard_map/ppermute | solution.py:180
  376.9 8.4 %fusion.13 = bf16[512,1024]{1,0:T(8,128)(2,1)} fusion(f32[4,128,1024]{2,1,0:T(8,128)} %copy-done.6, bf16[512,1024]{1,0:T(8,128)(2,1)} %collective-permute-done.36, bf16[512,1024]{1,0:T(8,128)(2,1)} %collective-permute-done.31, bf16[512,1024]{1,0:T(8,128)(2,1)} %collective-permute-done.26, bf16[512,1024]{1,0:T(8,128)(2,1)} %collective-permute-done.21, ...), kind=kLoop, calls=%fused_computation.34 | loop fusion | flops 13107200 | bytes 19922948 | tf_op jit(solution)/shard_map/convert_element_type | solution.py:388
  (179 shorter events, 101.8 us)
Async XLA Ops:
  4.6 117.3 %collective-permute-start.13 = (bf16[1024,768]{1,0:T(8,128)(2,1)}, bf16[1024,768]{1,0:T(8,128)(2,1)}, u32[]{:S(2)}, u32[]{:S(2)}) collective-permute-start(bf16[1024,768]{1,0:T(8,128)(2,1)} %pad_maximum_fusion.1), channel_id=1, source_target_pairs={{0,4},{4,8},{8,12},{1,5},{5,9},{9,13},{2,6},{6,10},{10,14},{3,7},{... | collective-permute-start | bytes 4718600 | tf_op jit(solution)/shard_map/ppermute | solution.py:180
  8.0 130.4 %collective-permute-start.12 = (bf16[1024,768]{1,0:T(8,128)(2,1)}, bf16[1024,768]{1,0:T(8,128)(2,1)}, u32[]{:S(2)}, u32[]{:S(2)}) collective-permute-start(bf16[1024,768]{1,0:T(8,128)(2,1)} %pad_maximum_fusion.1), channel_id=1, source_target_pairs={{4,0},{8,4},{12,8},{5,1},{9,5},{13,9},{6,2},{10,6},{14,10},{7,3},{... | collective-permute-start | bytes 4718600 | tf_op jit(solution)/shard_map/ppermute | solution.py:180
  14.1 85.9 %collective-permute-start.2 = (bf16[2,128,1024]{2,0,1:T(2,128)(2,1)}, bf16[2,128,1024]{2,0,1:T(2,128)(2,1)}, u32[]{:S(2)}, u32[]{:S(2)}) collective-permute-start(bf16[2,128,1024]{2,0,1:T(2,128)(2,1)} %fusion.51), channel_id=1, source_target_pairs={{0,12},{4,8},{8,4},{12,0},{1,13},{5,9},{9,5},{13,1},{2,14},{6,10},... | collective-permute-start | bytes 1572872 | tf_op jit(solution)/shard_map/ppermute | solution.py:180
  16.8 70.1 %collective-permute-start.1 = (bf16[2,128,1024]{2,0,1:T(2,128)(2,1)}, bf16[2,128,1024]{2,0,1:T(2,128)(2,1)}, u32[]{:S(2)}, u32[]{:S(2)}) collective-permute-start(bf16[2,128,1024]{2,0,1:T(2,128)(2,1)} %fusion.48), channel_id=1, source_target_pairs={{0,8},{4,12},{8,0},{12,4},{1,9},{5,13},{9,1},{13,5},{2,10},{6,14},... | collective-permute-start | bytes 1572872 | tf_op jit(solution)/shard_map/ppermute | solution.py:180
  21.3 74.9 %collective-permute-start = (bf16[2,128,1024]{2,0,1:T(2,128)(2,1)}, bf16[2,128,1024]{2,0,1:T(2,128)(2,1)}, u32[]{:S(2)}, u32[]{:S(2)}) collective-permute-start(bf16[2,128,1024]{2,0,1:T(2,128)(2,1)} %fusion.45), channel_id=1, source_target_pairs={{0,4},{4,0},{8,12},{12,8},{1,5},{5,1},{9,13},{13,9},{2,6},{6,2},{1... | collective-permute-start | bytes 1572872 | tf_op jit(solution)/shard_map/ppermute | solution.py:180
  86.9 29.0 %collective-permute-start.22 = (bf16[512,1024]{1,0:T(8,128)(2,1)}, bf16[512,1024]{1,0:T(8,128)(2,1)}, u32[]{:S(2)}, u32[]{:S(2)}) collective-permute-start(bf16[512,1024]{1,0:T(8,128)(2,1)} %constant_dynamic-slice_fusion), channel_id=1, source_target_pairs={{4,0},{8,4},{12,8},{5,1},{9,5},{13,9},{6,2},{10,6},{14,10},{7,3},{... | collective-permute-start | bytes 3145736 | tf_op jit(solution)/shard_map/ppermute | solution.py:180
  96.2 25.6 %collective-permute-start.23 = (bf16[512,1024]{1,0:T(8,128)(2,1)}, bf16[512,1024]{1,0:T(8,128)(2,1)}, u32[]{:S(2)}, u32[]{:S(2)}) collective-permute-start(bf16[512,1024]{1,0:T(8,128)(2,1)} %constant_dynamic-slice_fusion), channel_id=1, source_target_pairs={{0,4},{4,8},{8,12},{1,5},{5,9},{9,13},{2,6},{6,10},{10,14},{3,7},{... | collective-permute-start | bytes 3145736 | tf_op jit(solution)/shard_map/ppermute | solution.py:180
  113.6 24.3 %collective-permute-start.5 = (bf16[512,1024]{1,0:T(8,128)(2,1)S(1)}, bf16[512,1024]{1,0:T(8,128)(2,1)}, u32[]{:S(2)}, u32[]{:S(2)}) collective-permute-start(bf16[512,1024]{1,0:T(8,128)(2,1)S(1)} %fusion.9), channel_id=1, source_target_pairs={{0,16},{16,0},{1,17},{17,1},{2,18},{18,2},{3,19},{19,3},{4,20},{20... | collective-permute-start | bytes 3145736 | tf_op jit(solution)/shard_map/ppermute | solution.py:180
  121.8 26.0 %collective-permute-start.27 = (bf16[512,1024]{1,0:T(8,128)(2,1)}, bf16[512,1024]{1,0:T(8,128)(2,1)}, u32[]{:S(2)}, u32[]{:S(2)}) collective-permute-start(bf16[512,1024]{1,0:T(8,128)(2,1)} %collective-permute-done.23), channel_id=1, source_target_pairs={{4,8},{8,12},{5,9},{9,13},{6,10},{10,14},{7,11},{11,15},{20,24},{2... | collective-permute-start | bytes 3145736 | tf_op jit(solution)/shard_map/ppermute | solution.py:180
  138.7 69.8 %collective-permute-start.14 = (bf16[1024,768]{1,0:T(8,128)(2,1)}, bf16[1024,768]{1,0:T(8,128)(2,1)}, u32[]{:S(2)}, u32[]{:S(2)}) collective-permute-start(bf16[1024,768]{1,0:T(8,128)(2,1)} %collective-permute-done.13), channel_id=1, source_target_pairs={{4,8},{8,12},{5,9},{9,13},{6,10},{10,14},{7,11},{11,15},{20,24},{2... | collective-permute-start | bytes 4718600 | tf_op jit(solution)/shard_map/ppermute | solution.py:180
  143.8 65.5 %collective-permute-start.15 = (bf16[1024,768]{1,0:T(8,128)(2,1)}, bf16[1024,768]{1,0:T(8,128)(2,1)}, u32[]{:S(2)}, u32[]{:S(2)}) collective-permute-start(bf16[1024,768]{1,0:T(8,128)(2,1)} %collective-permute-done.12), channel_id=1, source_target_pairs={{4,0},{8,4},{5,1},{9,5},{6,2},{10,6},{7,3},{11,7},{20,16},{24,20},... | collective-permute-start | bytes 4718600 | tf_op jit(solution)/shard_map/ppermute | solution.py:180
  147.8 57.1 %collective-permute-start.28 = (bf16[512,1024]{1,0:T(8,128)(2,1)}, bf16[512,1024]{1,0:T(8,128)(2,1)}, u32[]{:S(2)}, u32[]{:S(2)}) collective-permute-start(bf16[512,1024]{1,0:T(8,128)(2,1)} %collective-permute-done.22), channel_id=1, source_target_pairs={{4,0},{8,4},{5,1},{9,5},{6,2},{10,6},{7,3},{11,7},{20,16},{24,20},... | collective-permute-start | bytes 3145736 | tf_op jit(solution)/shard_map/ppermute | solution.py:180
  161.6 44.1 %collective-permute-start.10 = (bf16[512,1024]{1,0:T(8,128)(2,1)}, bf16[512,1024]{1,0:T(8,128)(2,1)}, u32[]{:S(2)}, u32[]{:S(2)}) collective-permute-start(bf16[512,1024]{1,0:T(8,128)(2,1)} %copy-done.16), channel_id=1, source_target_pairs={{0,1},{1,0},{2,3},{3,2},{4,5},{5,4},{6,7},{7,6},{8,9},{9,8},{10,11... | collective-permute-start | bytes 3145736 | tf_op jit(solution)/shard_map/ppermute | solution.py:180
  161.6 49.4 %collective-permute-start.11 = (bf16[512,1024]{1,0:T(8,128)(2,1)}, bf16[512,1024]{1,0:T(8,128)(2,1)}, u32[]{:S(2)}, u32[]{:S(2)}) collective-permute-start(bf16[512,1024]{1,0:T(8,128)(2,1)} %collective-permute-done.9), channel_id=1, source_target_pairs={{0,1},{1,0},{2,3},{3,2},{4,5},{5,4},{6,7},{7,6},{8,9},{9,8},{10,11... | collective-permute-start | bytes 3145736 | tf_op jit(solution)/shard_map/ppermute | solution.py:180
  204.9 68.1 %collective-permute-start.32 = (bf16[512,1024]{1,0:T(8,128)(2,1)}, bf16[512,1024]{1,0:T(8,128)(2,1)S(1)}, u32[]{:S(2)}, u32[]{:S(2)}) collective-permute-start(bf16[512,1024]{1,0:T(8,128)(2,1)} %collective-permute-done.27), channel_id=1, source_target_pairs={{8,12},{9,13},{10,14},{11,15},{24,28},{25,29},{26,30},{27,31}} | collective-permute-start | bytes 3145736 | tf_op jit(solution)/shard_map/ppermute | solution.py:180
  205.7 67.4 %collective-permute-start.33 = (bf16[512,1024]{1,0:T(8,128)(2,1)}, bf16[512,1024]{1,0:T(8,128)(2,1)S(1)}, u32[]{:S(2)}, u32[]{:S(2)}) collective-permute-start(bf16[512,1024]{1,0:T(8,128)(2,1)} %collective-permute-done.28), channel_id=1, source_target_pairs={{4,0},{5,1},{6,2},{7,3},{20,16},{21,17},{22,18},{23,19}} | collective-permute-start | bytes 3145736 | tf_op jit(solution)/shard_map/ppermute | solution.py:180
  209.3 55.4 %collective-permute-start.17 = (bf16[1024,768]{1,0:T(8,128)(2,1)}, bf16[1024,768]{1,0:T(8,128)(2,1)S(1)}, u32[]{:S(2)}, u32[]{:S(2)}) collective-permute-start(bf16[1024,768]{1,0:T(8,128)(2,1)} %collective-permute-done.15), channel_id=1, source_target_pairs={{4,0},{5,1},{6,2},{7,3},{20,16},{21,17},{22,18},{23,19}} | collective-permute-start | bytes 4718600 | tf_op jit(solution)/shard_map/ppermute | solution.py:180
  298.3 28.1 %collective-permute-start.35 = (bf16[512,1024]{1,0:T(8,128)(2,1)}, bf16[512,1024]{1,0:T(8,128)(2,1)S(1)}, u32[]{:S(2)}, u32[]{:S(2)}) collective-permute-start(bf16[512,1024]{1,0:T(8,128)(2,1)} %slice.129), channel_id=1, source_target_pairs={{1,17},{3,19},{17,1},{19,3},{4,20},{6,22},{20,4},{22,6},{9,25},{11... | collective-permute-start | bytes 3145736 | tf_op jit(solution)/shard_map/ppermute | solution.py:180
  301.4 29.7 %collective-permute-start.30 = (bf16[512,1024]{1,0:T(8,128)(2,1)S(1)}, bf16[512,1024]{1,0:T(8,128)(2,1)S(1)}, u32[]{:S(2)}, u32[]{:S(2)}) collective-permute-start(bf16[512,1024]{1,0:T(8,128)(2,1)S(1)} %slice.130), channel_id=1, source_target_pairs={{0,16},{2,18},{16,0},{18,2},{5,21},{7,23},{21,5},{23,7},{8,24},{10... | collective-permute-start | bytes 3145736 | tf_op jit(solution)/shard_map/ppermute | solution.py:180
  303.4 45.4 %collective-permute-start.25 = (bf16[512,1024]{1,0:T(8,128)(2,1)S(1)}, bf16[512,1024]{1,0:T(8,128)(2,1)S(1)}, u32[]{:S(2)}, u32[]{:S(2)}) collective-permute-start(bf16[512,1024]{1,0:T(8,128)(2,1)S(1)} %slice.131), channel_id=1, source_target_pairs={{1,17},{3,19},{17,1},{19,3},{4,20},{6,22},{20,4},{22,6},{9,25},{11... | collective-permute-start | bytes 3145736 | tf_op jit(solution)/shard_map/ppermute | solution.py:180
  308.6 42.8 %collective-permute-start.20 = (bf16[512,1024]{1,0:T(8,128)(2,1)S(1)}, bf16[512,1024]{1,0:T(8,128)(2,1)S(1)}, u32[]{:S(2)}, u32[]{:S(2)}) collective-permute-start(bf16[512,1024]{1,0:T(8,128)(2,1)S(1)} %slice.132), channel_id=1, source_target_pairs={{0,16},{2,18},{16,0},{18,2},{5,21},{7,23},{21,5},{23,7},{8,24},{10... | collective-permute-start | bytes 3145736 | tf_op jit(solution)/shard_map/ppermute | solution.py:180
  326.7 27.4 %collective-permute-start.36 = (bf16[512,1024]{1,0:T(8,128)(2,1)S(1)}, bf16[512,1024]{1,0:T(8,128)(2,1)}, u32[]{:S(2)}, u32[]{:S(2)}) collective-permute-start(bf16[512,1024]{1,0:T(8,128)(2,1)S(1)} %fusion.41), channel_id=1, source_target_pairs={{1,3},{17,19},{4,6},{20,22},{11,9},{27,25},{14,12},{30,28}} | collective-permute-start | bytes 3145736 | tf_op jit(solution)/shard_map/ppermute | solution.py:180
  350.1 26.8 %collective-permute-start.26 = (bf16[512,1024]{1,0:T(8,128)(2,1)}, bf16[512,1024]{1,0:T(8,128)(2,1)}, u32[]{:S(2)}, u32[]{:S(2)}) collective-permute-start(bf16[512,1024]{1,0:T(8,128)(2,1)} %fusion.39), channel_id=1, source_target_pairs={{3,1},{19,17},{6,4},{22,20},{9,11},{25,27},{12,14},{28,30}} | collective-permute-start | bytes 3145736 | tf_op jit(solution)/shard_map/ppermute | solution.py:180
  352.4 24.5 %collective-permute-start.21 = (bf16[512,1024]{1,0:T(8,128)(2,1)S(1)}, bf16[512,1024]{1,0:T(8,128)(2,1)}, u32[]{:S(2)}, u32[]{:S(2)}) collective-permute-start(bf16[512,1024]{1,0:T(8,128)(2,1)S(1)} %fusion.38), channel_id=1, source_target_pairs={{2,0},{18,16},{7,5},{23,21},{8,10},{24,26},{13,15},{29,31}} | collective-permute-start | bytes 3145736 | tf_op jit(solution)/shard_map/ppermute | solution.py:180
  (38 other events, 643.0 us)

commit v2 on v1

--- a/solution.py
+++ b/solution.py
@@ -183,10 +183,76 @@
 SWAP = [(0, 1), (1, 0)]
 
 
-def attention_kernel(lin_ref, bias_ref, cos_ref, sin_ref, pos_ref, out_ref):
+def fetch_share(which, shares, target, sem):
+    def each(act):
+        for k, share in enumerate(shares):
+
+            @pl.when(which == k)
+            def _():
+                act(pltpu.make_async_copy(share, target, sem))
+
+    return each
+
+
+def linear_kernel(at_ref, *refs):
+    shares, blocks = refs[:4], refs[4:7]
+    out_ref, share_buf, block_buf, sems = refs[7:]
+    fetches = []
+    for m in range(3):
+        fetches.append(fetch_share(at_ref[m], shares, share_buf.at[m], sems.at[m]))
+        fetches[m](lambda copy: copy.start())
+        pltpu.make_async_copy(blocks[m], block_buf.at[m], sems.at[3 + m]).start()
+    for m in range(3):
+        fetches[m](lambda copy: copy.wait())
+        pltpu.make_async_copy(blocks[m], block_buf.at[m], sems.at[3 + m]).wait()
+    step = 128
+
+    @pl.loop(0, out_ref.shape[0] // step)
+    def _(i):
+        at = pl.ds(pl.multiple_of(i * step, step), step)
+        total = None
+        for m in range(3):
+            part = jnp.dot(share_buf[m, at], block_buf[m], preferred_element_type=jnp.float32)
+            total = part if total is None else total + part
+        out_ref[at] = total
+
+
+def linear_rows(at, shares, blocks):
+    (count, depth), width = shares[0].shape, blocks[0].shape[1]
+    return pl.pallas_call(
+        linear_kernel,
+        in_specs=[pl.BlockSpec(memory_space=pltpu.SMEM)]
+        + [pl.BlockSpec(memory_space=pl.ANY)] * 7,
+        out_specs=pl.BlockSpec(memory_space=pltpu.VMEM),
+        out_shape=jax.ShapeDtypeStruct((count, width), jnp.float32),
+        scratch_shapes=[
+            pltpu.VMEM((3, count, depth), jnp.bfloat16),
+            pltpu.VMEM((3, depth, width), jnp.bfloat16),
+            pltpu.SemaphoreType.DMA((6,)),
+        ],
+        compiler_params=pltpu.CompilerParams(vmem_limit_bytes=32 * 1024 * 1024),
+    )(at, *shares, *blocks)
+
+
+def attention_kernel(at_ref, *refs):
+    shares, refs = refs[:4], refs[4:]
+    block_ref, lin_ref, bias_ref, cos_ref, sin_ref, pos_ref, out_ref, share_buf, sem = refs
+    step = pl.program_id(0)
+
+    @pl.when(step == 0)
+    def _():
+        fetch = fetch_share(at_ref[0], shares, share_buf, sem)
+        fetch(lambda copy: copy.start())
+        fetch(lambda copy: copy.wait())
+
+    own = pl.ds(pl.multiple_of(step * lin_ref.shape[0], lin_ref.shape[0]), lin_ref.shape[0])
+
     heads = out_ref.shape[1] // HEAD
     rows = lin_ref.shape[0]
-    lin = lin_ref[...] + bias_ref[...]
+    lin = lin_ref[...] + jnp.dot(
+        share_buf[own], block_ref[...], preferred_element_type=jnp.float32
+    )
+    lin = lin + bias_ref[...]
     cosine = cos_ref[...]
     sine = sin_ref[...]
 
@@ -219,29 +285,104 @@
         out_ref[:, h * HEAD : (h + 1) * HEAD] = context[h * rows : (h + 1) * rows]
 
 
-def attend_rows(lin, bias, cosine, sine, positions, tile_rows):
+def attend_rows(shares, at, block, lin, bias, cosine, sine, positions, tile_rows):
     count, width = lin.shape
     out_width = width - 2 * HEAD
-    by_tile = lambda w: pl.BlockSpec((tile_rows, w), lambda i: (i, 0))
+    by_tile = lambda w: pl.BlockSpec((tile_rows, w), lambda i, at: (i, 0))
     return pl.pallas_call(
         attention_kernel,
-        grid=(count // tile_rows,),
-        in_specs=[
-            by_tile(width),
-            pl.BlockSpec((1, width), lambda i: (0, 0)),
-            by_tile(HEAD),
-            by_tile(HEAD),
-            by_tile(1),
-        ],
-        out_specs=by_tile(out_width),
+        grid_spec=pltpu.PrefetchScalarGridSpec(
+            num_scalar_prefetch=1,
+            grid=(count // tile_rows,),
+            in_specs=[
+                *[pl.BlockSpec(memory_space=pl.ANY)] * 4,
+                pl.BlockSpec(block.shape, lambda i, at: (0, 0)),
+                by_tile(width),
+                pl.BlockSpec((1, width), lambda i, at: (0, 0)),
+                by_tile(HEAD),
+                by_tile(HEAD),
+                by_tile(1),
+            ],
+            out_specs=by_tile(out_width),
+            scratch_shapes=[
+                pltpu.VMEM(shares[0].shape, jnp.bfloat16),
+                pltpu.SemaphoreType.DMA(()),
+            ],
+        ),
         out_shape=jax.ShapeDtypeStruct((count, out_width), jnp.bfloat16),
         compiler_params=pltpu.CompilerParams(vmem_limit_bytes=32 * 1024 * 1024),
+    )(at.reshape(1), *shares, block, lin, bias, cosine, sine, positions)
+
+
+def pack_kernel(slots_ref, *refs):
+    for m in range(4):
+        refs[4 + m][...] = refs[m][...]
+
+
+def pack_tiles(send_slots, activations, tile_rows):
+    width = activations.shape[1]
+    tiles = activations.reshape(-1, tile_rows, width)
+    peers = send_slots.shape[0] // 4
+    block = (1, tile_rows, width)
+    pick = lambda m: pl.BlockSpec(block, lambda p, slots: (slots[m * peers + p], 0, 0))
+    outs = pl.pallas_call(
+        pack_kernel,
+        grid_spec=pltpu.PrefetchScalarGridSpec(
+            num_scalar_prefetch=1,
+            grid=(peers,),
+            in_specs=[pick(m) for m in range(4)],
+            out_specs=[pl.BlockSpec(block, lambda p, slots: (p, 0, 0))] * 4,
+        ),
+        out_shape=[jax.ShapeDtypeStruct((peers, tile_rows, width), activations.dtype)] * 4,
         cost_estimate=pl.CostEstimate(
-            flops=4 * count * tile_rows * out_width,
-            bytes_accessed=count * (4 * width + 2 * out_width),
-            transcendentals=count * out_width,
+            flops=0, bytes_accessed=4 * activations.size, transcendentals=0
         ),
-    )(lin, bias, cosine, sine, positions)
+    )(jnp.clip(send_slots, 0, tiles.shape[0] - 1), *[tiles] * 4)
+    return [out.reshape(peers * tile_rows, width) for out in outs]
+
+
+def place_kernel(picks_ref, *refs):
+    arrived, (packed_ref, squares_ref, sems) = refs[:4], refs[4:]
+    count = packed_ref.shape[0]
+
+    def each(act):
+        for k in range(count):
+            for m in range(4):
+
+                @pl.when(picks_ref[k] == m)
+                def _():
+                    act(
+                        pltpu.make_async_copy(
+                            arrived[m].at[picks_ref[count + k]], packed_ref.at[k], sems.at[k]
+                        )
+                    )
+
+    each(lambda copy: copy.start())
+    each(lambda copy: copy.wait())
+    for k in range(count):
+        widened = packed_ref[k].astype(jnp.float32)
+        squares_ref[k] = jnp.sum(widened * widened, axis=-1, keepdims=True)
+
+
+def place_tiles(picks, arrived, tile_rows):
+    width = arrived[0].shape[1]
+    blocks = [part.reshape(-1, tile_rows, width) for part in arrived]
+    count = picks.shape[0] // 2
+    limits = jnp.repeat(jnp.array([3, blocks[0].shape[0] - 1], jnp.int32), count)
+    packed, squares = pl.pallas_call(
+        place_kernel,
+        in_specs=[pl.BlockSpec(memory_space=pltpu.SMEM)]
+        + [pl.BlockSpec(memory_space=pl.ANY)] * 4,
+        out_shape=[
+            jax.ShapeDtypeStruct((count, tile_rows, width), arrived[0].dtype),
+            jax.ShapeDtypeStruct((count, tile_rows, 1), jnp.float32),
+        ],
+        scratch_shapes=[pltpu.SemaphoreType.DMA((count,))],
+        cost_estimate=pl.CostEstimate(
+            flops=0, bytes_accessed=4 * count * tile_rows * width, transcendentals=0
+        ),
+    )(jnp.clip(picks, 0, limits), *blocks)
+    return packed.reshape(-1, width), squares.reshape(-1, 1)
 
 
 def ring_body(
@@ -282,6 +423,14 @@
         ]
     ).astype(jnp.float32)[None, :]
 
+    def hop(up, down):
+        s = len(up)
+        up.append(shift(up[-1], "dp", [(i, i + 1) for i in range(s - 1, 3)]))
+        down.append(shift(down[-1], "dp", [(i + 1, i) for i in range(0, 4 - s)]))
+
+    q_up, q_down = [qkv_own], [qkv_own]
+    hop(q_up, q_down)
+
     own_plan = lax.dynamic_index_in_dim(tile_dest, z, 0, keepdims=False)
     slot_ids = jnp.arange(slots, dtype=jnp.int32)
     peer_ids = jnp.arange(peers, dtype=jnp.int32)
@@ -291,34 +440,23 @@
     chooser = (own_plan[None, None, :] == partners[:, None, None]) & (
         send_rank[None, None, :] == peer_ids[None, :, None]
     )
-    own_tiles = activations.reshape(slots, tile_rows, width)
-    outgoing = [
-        jnp.einsum(
-            "ps,srf->prf",
-            chooser[m].astype(jnp.bfloat16),
-            own_tiles,
-            preferred_element_type=jnp.float32,
-        ).astype(jnp.bfloat16)
-        for m in range(4)
-    ]
+    send_slots = jnp.sum(chooser.astype(jnp.int32) * slot_ids, axis=2).reshape(-1)
+    outgoing = pack_tiles(send_slots, activations, tile_rows)
     arrived = [outgoing[0]] + [
         shift(outgoing[m], "dp", [(i, i ^ m) for i in range(4)]) for m in range(1, 4)
     ]
     to_here = (tile_dest == z).astype(jnp.int32)
     from_each = jnp.sum(to_here, axis=1)
     first_place = jnp.cumsum(from_each) - from_each
-    place_of = first_place[:, None] + peer_ids[None, :]
-    landed = peer_ids[None, :] < from_each[:, None]
     tile_ids = jnp.arange(TPD, dtype=jnp.int32)
-    placer = (place_of[None, :, :] == tile_ids[:, None, None]) & landed[None, :, :]
-    placer = jnp.take(placer, partners, axis=1).astype(jnp.bfloat16)
-    packed = sum(
-        jnp.einsum(
-            "kp,prf->krf", placer[:, m], arrived[m], preferred_element_type=jnp.float32
-        )
-        for m in range(4)
-    ).astype(jnp.bfloat16).reshape(rows, width)
-
+    inside = (tile_ids[:, None] >= first_place[None, :]) & (
+        tile_ids[:, None] < (first_place + from_each)[None, :]
+    )
+    source = jnp.sum(inside.astype(jnp.int32) * jnp.arange(4, dtype=jnp.int32)[None, :], axis=1)
+    rank = jnp.sum(inside.astype(jnp.int32) * (tile_ids[:, None] - first_place[None, :]), axis=1)
+    packed, squares = place_tiles(
+        jnp.concatenate([source ^ z, rank]), arrived, tile_rows
+    )
     flat_member = (tile_dest.reshape(-1) == z).astype(jnp.int32)
     flat_rank = jnp.cumsum(flat_member) - 1
     picker = flat_member[None, :] * (flat_rank[None, :] == tile_ids[:, None]).astype(jnp.int32)
@@ -334,58 +472,91 @@
     cosine = jnp.concatenate([cosine, cosine], axis=1)
     sine = jnp.concatenate([-sine, sine], axis=1)
 
+    packed, squares, q_up[1], q_down[1] = lax.optimization_barrier(
+        (packed, squares, q_up[1], q_down[1])
+    )
+    hop(q_up, q_down)
+
     widened = packed.astype(jnp.float32)
-    squares = jnp.sum(widened * widened, axis=-1, keepdims=True)
     squares = squares + shift(squares, "pair", SWAP)
     squares = squares + shift(squares, "tensor", SWAP)
     gain = lax.dynamic_slice_in_dim(norm_gain, t * width, width, 0).astype(jnp.float32)
     normed = (widened * lax.rsqrt(squares / (4 * width) + norm_eps) * gain).astype(jnp.bfloat16)
-    here = [normed, shift(normed, "groups", SWAP)]
-    across = [shift(part, "tensor", SWAP) for part in here]
-    here_other = [shift(part, "pair", SWAP) for part in here]
-    across_other = [shift(part, "pair", SWAP) for part in across]
-    shares = jnp.stack(
-        [jnp.concatenate(part, axis=0) for part in (here, here_other, across, across_other)]
-    )
-
-    def ring(block):
-        up, down = [block], [block]
-        for s in range(1, 4):
-            up.append(shift(up[-1], "dp", [(i, i + 1) for i in range(s - 1, 3)]))
-            down.append(shift(down[-1], "dp", [(i + 1, i) for i in range(0, 4 - s)]))
+    peer = shift(normed, "groups", SWAP)
+    across_own = shift(normed, "tensor", SWAP)
+    across_peer = shift(peer, "tensor", SWAP)
+    q_up[2], q_down[2], peer, across_own, across_peer = lax.optimization_barrier(
+        (q_up[2], q_down[2], peer, across_own, across_peer)
+    )
+    hop(q_up, q_down)
+    here = jnp.concatenate([normed, peer], axis=0)
+    across = jnp.concatenate([across_own, across_peer], axis=0)
+    shares = [here, shift(here, "pair", SWAP), across, shift(across, "pair", SWAP)]
+    *shares, o_own = lax.optimization_barrier((*shares, o_own))
+    o_up, o_down = [o_own], [o_own]
+    hop(o_up, o_down)
+
+    def by_partner(up, down):
         first = jnp.where(z % 2 == 0, down[1], up[1])
         second = up[2] + down[2]
         third = jnp.where(z == 1, down[1], jnp.where(z == 2, up[1], up[3] + down[3]))
-        return [block, first, second, third]
-
-    qkv_blocks = ring(qkv_own)
-    o_blocks = ring(o_own)
-    lin = None
-    for m in range(4):
-        share = lax.dynamic_index_in_dim(shares, (z ^ m) ^ t, 0, keepdims=False)
-        part = jnp.dot(share, qkv_blocks[m], preferred_element_type=jnp.float32)
-        lin = part if lin is None else lin + part
-    context = attend_rows(lin, bias, cosine, sine, positions, tile_rows)
-
-    total = packed.astype(jnp.float32)
+        return [up[0], first, second, third]
+
+    q_blocks = by_partner(q_up[:3] + [q_up[2]], q_down[:3] + [q_down[2]])
+    at = jnp.arange(4, dtype=jnp.int32) ^ z ^ t
+    lin = linear_rows(at[:3], shares, q_blocks[:3])
+    lin, q_up[3], q_down[3] = lax.optimization_barrier((lin, q_up[3], q_down[3]))
+    context = attend_rows(
+        shares, at[3], by_partner(q_up, q_down)[3], lin, bias, cosine, sine, positions, tile_rows
+    )
+    context, o_up[1], o_down[1] = lax.optimization_barrier((context, o_up[1], o_down[1]))
+    hop(o_up, o_down)
+
     every = ("groups", "dp", "tensor", "pair")
     index = lambda zz, yy, xx, cc: ((yy * 4 + zz) * 2 + xx) * 2 + cc
-    for m in range(4):
-        part = jnp.dot(context, o_blocks[m], preferred_element_type=jnp.float32)
-        sides = [(i, j) for i in range(2) for j in range(2)]
-        to_core, to_group, to_chip = [], [], []
+
+    def project(block):
+        return jnp.dot(context, block, preferred_element_type=jnp.float32)
+
+    def to_chip(part, m, cores):
+        pairs = []
         for zz in range(4):
-            xd, cd = (zz ^ m) // 2, (zz ^ m) % 2
-            to_core += [(index(zz, i, j, 1 - cd), index(zz, i, j, cd)) for i, j in sides]
-            to_group += [(index(zz, i, j, cd), index(zz, 1 - i, j, cd)) for i, j in sides]
-            to_chip += [(index(zz, i, 1 - xd, cd), index(zz, i, xd, cd)) for i in range(2)]
-        part = part + shift(part.astype(jnp.bfloat16), every, to_core).astype(jnp.float32)
-        mine = part[:rows] + shift(part[rows:].astype(jnp.bfloat16), every, to_group).astype(
+            xd = (zz ^ m) // 2
+            for cc in cores(zz):
+                pairs += [(index(zz, i, 1 - xd, cc), index(zz, i, xd, cc)) for i in range(2)]
+        return part + shift(part.astype(jnp.bfloat16), every, pairs).astype(jnp.float32)
+
+    both = lambda zz: (0, 1)
+    keeps_first = (z ^ core) % 2 == 0
+
+    def halves(block):
+        return jnp.split(block, 2, axis=1)
+
+    def to_core(one, two):
+        kept = project(jnp.where(keeps_first, one, two))
+        sent = project(jnp.where(keeps_first, two, one)).astype(jnp.bfloat16)
+        return kept + shift(sent, "pair", SWAP).astype(jnp.float32)
+
+    def to_group(part):
+        return part[:rows] + shift(part[rows:].astype(jnp.bfloat16), "groups", SWAP).astype(
             jnp.float32
         )
-        mine = mine + shift(mine.astype(jnp.bfloat16), every, to_chip).astype(jnp.float32)
-        total = total + jnp.where(z ^ m == t, mine, 0.0)
-    return total.astype(jnp.bfloat16)
+
+    o_first = jnp.where(z % 2 == 0, o_down[1], o_up[1])
+    first = to_core(o_own, o_first)
+    first, o_up[2], o_down[2] = lax.optimization_barrier((first, o_up[2], o_down[2]))
+    hop(o_up, o_down)
+    first = to_group(first)
+    first, o_up[3], o_down[3] = lax.optimization_barrier((first, o_up[3], o_down[3]))
+    first = to_chip(first, 0, both)
+    o_blocks = by_partner(o_up, o_down)
+    second = [
+        to_group(to_core(one, two)) for one, two in zip(halves(o_blocks[2]), halves(o_blocks[3]))
+    ]
+    first, second[1] = lax.optimization_barrier((first, second[1]))
+    second = jnp.concatenate([to_chip(part, 2, both) for part in second], axis=1)
+    total = jnp.where(z // 2 == x, first, second)
+    return (packed.astype(jnp.float32) + total).astype(jnp.bfloat16)
 
 
 def solution(mesh):

time: 393 us -> 327 us (0.83); the launches traced: 386 us -> 324 us
  waiting for transfers between devices: 226 us -> 193 us
  matrix products: 39.7 us -> 7.86 us
  Pallas kernels: 4.95 us -> 26.5 us
  starting transfers between devices: 68.9 us -> 56.5 us
  other arithmetic: 30.7 us -> 24.7 us
    ppermute x37 -> x32, waiting for transfers between devices: 226 us -> 193 us  [shift(): return lax.ppermute(values, axis, pairs)]
    dot_general x15 -> x6, matrix products: 39.7 us -> 7.86 us  [project(): return jnp.dot(context, block, preferred_element_type=jnp.float32)]
    pallas_call x1 -> x4, Pallas kernels: 4.95 us -> 26.5 us  [the longest x1 10.5 us: attend_rows(): pl.pallas_call(attention_kernel, grid_spec=pltpu.PrefetchScalarGridSpec(n...]
    ppermute x37 -> x32, starting transfers between devices: 68.9 us -> 56.5 us  [shift(): return lax.ppermute(values, axis, pairs)]
    convert_element_type x5 -> x4, other arithmetic: 11.8 us -> 3.57 us  [the longest x3 2 us: to_chip(): part.astype(jnp.bfloat16)]
    another operation x7 -> x2, other arithmetic: 7.43 us -> 0.23 us  [the longest x5 7.2 us: ring_body(): jnp.stack([jnp.concatenate(part, axis=0) for part in (here, here_other, a...]
    unnamed x50 -> x41, local copies, waits for them, and re-layouts: 3.78 us -> 8.5 us
    select_n x2 -> x3, other arithmetic: 0.08 us -> 4.49 us  [the longest x2 4.28 us: by_partner(): jnp.where(z == 1, down[1], jnp.where(z == 2, up[1], up[3] + down[3]))]
  transfers between devices with their start and end apart: 37 -> 32, of which waited for: 14 -> 19; matrix products, arithmetic and copies ran while one was open for 17% -> 9% of each run, Pallas kernels for 1% -> 8%
where the time goes in v2:
time: 327 us; the launch traced here: 324 us
  waiting for transfers between devices  193 us (59%)
  starting transfers between devices  56.5 us (17%)
  Pallas kernels  26.5 us (8%)
  other arithmetic  24.7 us (8%)
  local copies, waits for them, and re-layouts  15.3 us (5%)
  matrix products  7.86 us (2%)
    ppermute x32, waiting for transfers between devices, shift(): return lax.ppermute(values, axis, pairs)  193 us
    ppermute x32, starting transfers between devices, shift(): return lax.ppermute(values, axis, pairs)  56.5 us
    pallas_call x1, Pallas kernels, attend_rows(): pl.pallas_call(attention_kernel, grid_spec=pltpu.PrefetchScalarGridSpec(n...  10.5 us
    pallas_call x1, Pallas kernels, linear_rows(): pl.pallas_call(linear_kernel, in_specs=[pl.BlockSpec(memory_space=pltpu.S...  9.28 us
    unnamed x41, local copies, waits for them, and re-layouts  8.5 us
    dot_general x6, matrix products, project(): return jnp.dot(context, block, preferred_element_type=jnp.float32)  7.86 us
  transfers between devices with their start and end apart: 32, of which 19 were waited for; matrix products, arithmetic and copies ran while one was open for 9% of the time, Pallas kernels for 8%

profile of v2, /device:TPU:12, one launch (start us, length us, event | category | flops | bytes accessed | tf_op | source)
XLA Modules:
  0.0 324.1 jit_solution(8684641893922282606)
XLA Ops:
  2.9 3.5 %collective-permute-start.3 = (bf16[1024,768]{1,0:T(8,128)(2,1)S(1)}, bf16[1024,768]{1,0:T(8,128)(2,1)S(1)}, u32[]{:S(2)}, u32[]{:S(2)}) collective-permute-start(bf16[1024,768]{1,0:T(8,128)(2,1)S(1)} %pad_maximum_fusion.1.refs_4_), channel_id=1, source_target_pairs={{0,4},{4,8},{8,12},{1,5},{5,9},{9,13},{2,6},{6,10},{10,14},{3,7},{... | collective-permute-start | bytes 4718600 | tf_op jit(solution)/shard_map/ppermute | solution.py:180
  10.0 3.7 %shard_map.118 = (bf16[2,128,1024]{2,1,0:T(8,128)(2,1)}, bf16[2,128,1024]{2,1,0:T(8,128)(2,1)}, bf16[2,128,1024]{2,1,0:T(8,128)(2,1)}, bf16[2,128,1024]{2,1,0:T(8,128)(2,1)}) custom-call(s32[8]{0:T(128)} %min.17.slots_ref, bf16[8,128,1024]{2,1,0:T(8,128)(2,1)} %bitcast.32, bf16[8,128,1024]{2,1,0:T(8,128)(2,1)} %bitcast.33, bf16[8,128,1024]{2,1,0:T(8,128)(2,1)} %bitcast.34, ...), custom_call_target="tpu_custom_call" | custom-call | bytes 4194304 | tf_op jit(solution)/shard_map/pallas_call | solution.py:328
  13.8 3.7 %collective-permute-start.1 = (bf16[256,1024]{1,0:T(8,128)(2,1)}, bf16[256,1024]{1,0:T(8,128)(2,1)}, u32[]{:S(2)}, u32[]{:S(2)}) collective-permute-start(bf16[256,1024]{1,0:T(8,128)(2,1)} %bitcast.48), channel_id=1, source_target_pairs={{0,8},{4,12},{8,0},{12,4},{1,9},{5,13},{9,1},{13,5},{2,10},{6,14},... | collective-permute-start | bytes 1572872 | tf_op jit(solution)/shard_map/ppermute | solution.py:180
  19.3 45.3 %collective-permute-done = bf16[256,1024]{1,0:T(8,128)(2,1)} collective-permute-done((bf16[256,1024]{1,0:T(8,128)(2,1)}, bf16[256,1024]{1,0:T(8,128)(2,1)}, u32[]{:S(2)}, u32[]{:S(2)}) %collective-permute-start) | collective-permute-done | bytes 524320 | tf_op jit(solution)/shard_map/ppermute | solution.py:180
  64.6 10.4 %collective-permute-done.1 = bf16[256,1024]{1,0:T(8,128)(2,1)} collective-permute-done((bf16[256,1024]{1,0:T(8,128)(2,1)}, bf16[256,1024]{1,0:T(8,128)(2,1)}, u32[]{:S(2)}, u32[]{:S(2)}) %collective-permute-start.1) | collective-permute-done | bytes 524320 | tf_op jit(solution)/shard_map/ppermute | solution.py:180
  75.1 14.2 %collective-permute-done.2 = bf16[256,1024]{1,0:T(8,128)(2,1)} collective-permute-done((bf16[256,1024]{1,0:T(8,128)(2,1)}, bf16[256,1024]{1,0:T(8,128)(2,1)}, u32[]{:S(2)}, u32[]{:S(2)}) %collective-permute-start.2) | collective-permute-done | bytes 524320 | tf_op jit(solution)/shard_map/ppermute | solution.py:180
  105.3 18.6 %collective-permute-done.9 = bf16[512,1024]{1,0:T(8,128)(2,1)S(1)} collective-permute-done((bf16[512,1024]{1,0:T(8,128)(2,1)S(1)}, bf16[512,1024]{1,0:T(8,128)(2,1)S(1)}, u32[]{:S(2)}, u32[]{:S(2)}) %collective-permute-start.9) | collective-permute-done | bytes 1048608 | tf_op jit(solution)/shard_map/ppermute | solution.py:180
  125.4 4.6 %collective-permute-done.10 = bf16[512,1024]{1,0:T(8,128)(2,1)S(1)} collective-permute-done((bf16[512,1024]{1,0:T(8,128)(2,1)S(1)}, bf16[512,1024]{1,0:T(8,128)(2,1)S(1)}, u32[]{:S(2)}, u32[]{:S(2)}) %collective-permute-start.10) | collective-permute-done | bytes 1048608 | tf_op jit(solution)/shard_map/ppermute | solution.py:180
  129.9 4.5 %collective-permute-done.7 = bf16[1024,768]{1,0:T(8,128)(2,1)S(1)} collective-permute-done((bf16[1024,768]{1,0:T(8,128)(2,1)S(1)}, bf16[1024,768]{1,0:T(8,128)(2,1)S(1)}, u32[]{:S(2)}, u32[]{:S(2)}) %collective-permute-start.7) | collective-permute-done | bytes 1572896 | tf_op jit(solution)/shard_map/ppermute | solution.py:180
  135.6 3.3 %collective-permute-done.8 = bf16[1024,768]{1,0:T(8,128)(2,1)S(1)} collective-permute-done((bf16[1024,768]{1,0:T(8,128)(2,1)}, bf16[1024,768]{1,0:T(8,128)(2,1)S(1)}, u32[]{:S(2)}, u32[]{:S(2)}) %collective-permute-start.8) | collective-permute-done | bytes 1572896 | tf_op jit(solution)/shard_map/ppermute | solution.py:180
  140.0 9.9 %collective-permute-done.11 = bf16[512,1024]{1,0:T(8,128)(2,1)S(1)} collective-permute-done((bf16[512,1024]{1,0:T(8,128)(2,1)S(1)}, bf16[512,1024]{1,0:T(8,128)(2,1)S(1)}, u32[]{:S(2)}, u32[]{:S(2)}) %collective-permute-start.11) | collective-permute-done | bytes 1048608 | tf_op jit(solution)/shard_map/ppermute | solution.py:180
  162.6 3.7 %collective-permute-start.17 = (bf16[512,1024]{1,0:T(8,128)(2,1)}, bf16[512,1024]{1,0:T(8,128)(2,1)}, u32[]{:S(2)}, u32[]{:S(2)}) collective-permute-start(bf16[512,1024]{1,0:T(8,128)(2,1)} %constant_dynamic-slice_fusion), channel_id=1, source_target_pairs={{0,4},{4,8},{8,12},{1,5},{5,9},{9,13},{2,6},{6,10},{10,14},{3,7},{... | collective-permute-start | bytes 3145736 | tf_op jit(solution)/shard_map/ppermute | solution.py:180
  177.9 9.3 %shard_map.120.refs_5_ = f32[1024,768]{1,0:T(8,128)S(1)} custom-call(s32[3]{0:T(128)S(1)} %bitcast.31, bf16[1024,1024]{1,0:T(8,128)(2,1)S(1)} %pad_maximum_fusion.refs_0_, bf16[1024,1024]{1,0:T(8,128)(2,1)} %collective-permute-done.12.refs_1_, bf16[1024,1024]{1,0:T(8,128)(2,1)} %constant_dynamic-update-slice_fusion.refs_2_, ...), custom_call_target="tpu_custom_call" | custom-call | tf_op jit(solution)/shard_map/pallas_call | solution.py:222
  187.2 4.6 %collective-permute-done.15 = bf16[1024,768]{1,0:T(8,128)(2,1)} collective-permute-done((bf16[1024,768]{1,0:T(8,128)(2,1)}, bf16[1024,768]{1,0:T(8,128)(2,1)}, u32[]{:S(2)}, u32[]{:S(2)}) %collective-permute-start.15) | collective-permute-done | bytes 1572896 | tf_op jit(solution)/shard_map/ppermute | solution.py:180
  194.5 10.5 %shard_map.121 = bf16[1024,512]{1,0:T(8,128)(2,1)S(1)} custom-call(s32[1]{0:T(128)} %slice.27.at_ref, bf16[1024,1024]{1,0:T(8,128)(2,1)S(1)} %pad_maximum_fusion.refs_0_, bf16[1024,1024]{1,0:T(8,128)(2,1)} %collective-permute-done.12.refs_1_, bf16[1024,1024]{1,0:T(8,128)(2,1)} %constant_dynamic-update-slice_fusion.refs_2_, ...), custom_call_target="tpu_custom_call" | custom-call | tf_op jit(solution)/shard_map/pallas_call | solution.py:292
  205.1 8.6 %collective-permute-done.18 = bf16[512,1024]{1,0:T(8,128)(2,1)} collective-permute-done((bf16[512,1024]{1,0:T(8,128)(2,1)}, bf16[512,1024]{1,0:T(8,128)(2,1)}, u32[]{:S(2)}, u32[]{:S(2)}) %collective-permute-start.18) | collective-permute-done | bytes 1048608 | tf_op jit(solution)/shard_map/ppermute | solution.py:180
  223.9 17.6 %collective-permute-done.20 = bf16[512,1024]{1,0:T(8,128)(2,1)S(1)} collective-permute-done((bf16[512,1024]{1,0:T(8,128)(2,1)}, bf16[512,1024]{1,0:T(8,128)(2,1)S(1)}, u32[]{:S(2)}, u32[]{:S(2)}) %collective-permute-start.20) | collective-permute-done | bytes 1048608 | tf_op jit(solution)/shard_map/ppermute | solution.py:180
  241.5 4.1 %collective-permute-done.21 = bf16[512,1024]{1,0:T(8,128)(2,1)S(1)} collective-permute-done((bf16[512,1024]{1,0:T(8,128)(2,1)}, bf16[512,1024]{1,0:T(8,128)(2,1)S(1)}, u32[]{:S(2)}, u32[]{:S(2)}) %collective-permute-start.21) | collective-permute-done | bytes 1048608 | tf_op jit(solution)/shard_map/ppermute | solution.py:180
  248.1 3.6 %collective-permute-start.24 = (bf16[512,1024]{1,0:T(8,128)(2,1)S(1)}, bf16[512,1024]{1,0:T(8,128)(2,1)S(1)}, u32[]{:S(2)}, u32[]{:S(2)}) collective-permute-start(bf16[512,1024]{1,0:T(8,128)(2,1)S(1)} %collective-permute-done.21), channel_id=1, source_target_pairs={{4,0},{5,1},{6,2},{7,3},{20,16},{21,17},{22,18},{23,19}} | collective-permute-start | bytes 3145736 | tf_op jit(solution)/shard_map/ppermute | solution.py:180
  252.1 18.2 %collective-permute-done.22 = bf16[512,1024]{1,0:T(8,128)(2,1)S(1)} collective-permute-done((bf16[512,1024]{1,0:T(8,128)(2,1)S(1)}, bf16[512,1024]{1,0:T(8,128)(2,1)S(1)}, u32[]{:S(2)}, u32[]{:S(2)}) %collective-permute-start.22) | collective-permute-done | bytes 1048608 | tf_op jit(solution)/shard_map/ppermute | solution.py:180
  282.3 11.9 %collective-permute-done.29 = bf16[512,512]{1,0:T(8,128)(2,1)S(1)} collective-permute-done((bf16[512,512]{1,0:T(8,128)(2,1)S(1)}, bf16[512,512]{1,0:T(8,128)(2,1)S(1)}, u32[]{:S(2)}, u32[]{:S(2)}) %collective-permute-start.29) | collective-permute-done | bytes 524320 | tf_op jit(solution)/shard_map/ppermute | solution.py:180
  296.0 5.5 %collective-permute-start.30 = (bf16[512,512]{1,0:T(8,128)(2,1)}, bf16[512,512]{1,0:T(8,128)(2,1)}, u32[]{:S(2)}, u32[]{:S(2)}) collective-permute-start(bf16[512,512]{1,0:T(8,128)(2,1)} %fusion.7), channel_id=1, source_target_pairs={{0,2},{16,18},{1,3},{17,19},{4,6},{20,22},{5,7},{21,23},{10,8},{26... | collective-permute-start | bytes 1572872 | tf_op jit(solution)/shard_map/ppermute | solution.py:180
  306.9 3.7 %collective-permute-start.31 = (bf16[512,512]{1,0:T(8,128)(2,1)}, bf16[512,512]{1,0:T(8,128)(2,1)}, u32[]{:S(2)}, u32[]{:S(2)}) collective-permute-start(bf16[512,512]{1,0:T(8,128)(2,1)} %convert_element_type.141), channel_id=1, source_target_pairs={{0,2},{16,18},{1,3},{17,19},{4,6},{20,22},{5,7},{21,23},{10,8},{26... | collective-permute-start | bytes 1572872 | tf_op jit(solution)/shard_map/ppermute | solution.py:180
  312.2 8.9 %collective-permute-done.31 = bf16[512,512]{1,0:T(8,128)(2,1)} collective-permute-done((bf16[512,512]{1,0:T(8,128)(2,1)}, bf16[512,512]{1,0:T(8,128)(2,1)}, u32[]{:S(2)}, u32[]{:S(2)}) %collective-permute-start.31) | collective-permute-done | bytes 524320 | tf_op jit(solution)/shard_map/ppermute | solution.py:180
  (156 shorter events, 91.5 us)
Async XLA Ops:
  2.9 90.4 %collective-permute-start.3 = (bf16[1024,768]{1,0:T(8,128)(2,1)S(1)}, bf16[1024,768]{1,0:T(8,128)(2,1)S(1)}, u32[]{:S(2)}, u32[]{:S(2)}) collective-permute-start(bf16[1024,768]{1,0:T(8,128)(2,1)S(1)} %pad_maximum_fusion.1.refs_4_), channel_id=1, source_target_pairs={{0,4},{4,8},{8,12},{1,5},{5,9},{9,13},{2,6},{6,10},{10,14},{3,7},{... | collective-permute-start | bytes 4718600 | tf_op jit(solution)/shard_map/ppermute | solution.py:180
  6.4 86.9 %collective-permute-start.4 = (bf16[1024,768]{1,0:T(8,128)(2,1)S(1)}, bf16[1024,768]{1,0:T(8,128)(2,1)}, u32[]{:S(2)}, u32[]{:S(2)}) collective-permute-start(bf16[1024,768]{1,0:T(8,128)(2,1)S(1)} %pad_maximum_fusion.1.refs_4_), channel_id=1, source_target_pairs={{4,0},{8,4},{12,8},{5,1},{9,5},{13,9},{6,2},{10,6},{14,10},{7,3},{... | collective-permute-start | bytes 4718600 | tf_op jit(solution)/shard_map/ppermute | solution.py:180
  13.8 50.9 %collective-permute-start = (bf16[256,1024]{1,0:T(8,128)(2,1)}, bf16[256,1024]{1,0:T(8,128)(2,1)}, u32[]{:S(2)}, u32[]{:S(2)}) collective-permute-start(bf16[256,1024]{1,0:T(8,128)(2,1)} %bitcast.49), channel_id=1, source_target_pairs={{0,4},{4,0},{8,12},{12,8},{1,5},{5,1},{9,13},{13,9},{2,6},{6,2},{1... | collective-permute-start | bytes 1572872 | tf_op jit(solution)/shard_map/ppermute | solution.py:180
  13.8 61.2 %collective-permute-start.1 = (bf16[256,1024]{1,0:T(8,128)(2,1)}, bf16[256,1024]{1,0:T(8,128)(2,1)}, u32[]{:S(2)}, u32[]{:S(2)}) collective-permute-start(bf16[256,1024]{1,0:T(8,128)(2,1)} %bitcast.48), channel_id=1, source_target_pairs={{0,8},{4,12},{8,0},{12,4},{1,9},{5,13},{9,1},{13,5},{2,10},{6,14},... | collective-permute-start | bytes 1572872 | tf_op jit(solution)/shard_map/ppermute | solution.py:180
  17.6 71.7 %collective-permute-start.2 = (bf16[256,1024]{1,0:T(8,128)(2,1)}, bf16[256,1024]{1,0:T(8,128)(2,1)}, u32[]{:S(2)}, u32[]{:S(2)}) collective-permute-start(bf16[256,1024]{1,0:T(8,128)(2,1)} %bitcast.47), channel_id=1, source_target_pairs={{0,12},{4,8},{8,4},{12,0},{1,13},{5,9},{9,5},{13,1},{2,14},{6,10},... | collective-permute-start | bytes 1572872 | tf_op jit(solution)/shard_map/ppermute | solution.py:180
  99.7 24.2 %collective-permute-start.9 = (bf16[512,1024]{1,0:T(8,128)(2,1)S(1)}, bf16[512,1024]{1,0:T(8,128)(2,1)S(1)}, u32[]{:S(2)}, u32[]{:S(2)}) collective-permute-start(bf16[512,1024]{1,0:T(8,128)(2,1)S(1)} %fusion.1), channel_id=1, source_target_pairs={{0,16},{16,0},{1,17},{17,1},{2,18},{18,2},{3,19},{19,3},{4,20},{20... | collective-permute-start | bytes 3145736 | tf_op jit(solution)/shard_map/ppermute | solution.py:180
  100.3 34.1 %collective-permute-start.7 = (bf16[1024,768]{1,0:T(8,128)(2,1)S(1)}, bf16[1024,768]{1,0:T(8,128)(2,1)S(1)}, u32[]{:S(2)}, u32[]{:S(2)}) collective-permute-start(bf16[1024,768]{1,0:T(8,128)(2,1)S(1)} %collective-permute-done.3), channel_id=1, source_target_pairs={{4,8},{8,12},{5,9},{9,13},{6,10},{10,14},{7,11},{11,15},{20,24},{2... | collective-permute-start | bytes 4718600 | tf_op jit(solution)/shard_map/ppermute | solution.py:180
  101.8 37.0 %collective-permute-start.8 = (bf16[1024,768]{1,0:T(8,128)(2,1)}, bf16[1024,768]{1,0:T(8,128)(2,1)S(1)}, u32[]{:S(2)}, u32[]{:S(2)}) collective-permute-start(bf16[1024,768]{1,0:T(8,128)(2,1)} %collective-permute-done.4), channel_id=1, source_target_pairs={{4,0},{8,4},{5,1},{9,5},{6,2},{10,6},{7,3},{11,7},{20,16},{24,20},... | collective-permute-start | bytes 4718600 | tf_op jit(solution)/shard_map/ppermute | solution.py:180
  103.8 26.2 %collective-permute-start.10 = (bf16[512,1024]{1,0:T(8,128)(2,1)S(1)}, bf16[512,1024]{1,0:T(8,128)(2,1)S(1)}, u32[]{:S(2)}, u32[]{:S(2)}) collective-permute-start(bf16[512,1024]{1,0:T(8,128)(2,1)S(1)} %fusion.1), channel_id=1, source_target_pairs={{0,2},{2,0},{1,3},{3,1},{4,6},{6,4},{5,7},{7,5},{8,10},{10,8},{9,1... | collective-permute-start | bytes 3145736 | tf_op jit(solution)/shard_map/ppermute | solution.py:180
  123.9 26.1 %collective-permute-start.11 = (bf16[512,1024]{1,0:T(8,128)(2,1)S(1)}, bf16[512,1024]{1,0:T(8,128)(2,1)S(1)}, u32[]{:S(2)}, u32[]{:S(2)}) collective-permute-start(bf16[512,1024]{1,0:T(8,128)(2,1)S(1)} %collective-permute-done.9), channel_id=1, source_target_pairs={{0,2},{2,0},{1,3},{3,1},{4,6},{6,4},{5,7},{7,5},{8,10},{10,8},{9,1... | collective-permute-start | bytes 3145736 | tf_op jit(solution)/shard_map/ppermute | solution.py:180
  153.6 33.6 %collective-permute-start.14 = (bf16[1024,768]{1,0:T(8,128)(2,1)}, bf16[1024,768]{1,0:T(8,128)(2,1)}, u32[]{:S(2)}, u32[]{:S(2)}) collective-permute-start(bf16[1024,768]{1,0:T(8,128)(2,1)} %copy-done.10), channel_id=1, source_target_pairs={{8,12},{9,13},{10,14},{11,15},{24,28},{25,29},{26,30},{27,31}} | collective-permute-start | bytes 4718600 | tf_op jit(solution)/shard_map/ppermute | solution.py:180
  155.5 36.3 %collective-permute-start.15 = (bf16[1024,768]{1,0:T(8,128)(2,1)}, bf16[1024,768]{1,0:T(8,128)(2,1)}, u32[]{:S(2)}, u32[]{:S(2)}) collective-permute-start(bf16[1024,768]{1,0:T(8,128)(2,1)} %copy-done.12), channel_id=1, source_target_pairs={{4,0},{5,1},{6,2},{7,3},{20,16},{21,17},{22,18},{23,19}} | collective-permute-start | bytes 4718600 | tf_op jit(solution)/shard_map/ppermute | solution.py:180
  162.6 42.5 %collective-permute-start.17 = (bf16[512,1024]{1,0:T(8,128)(2,1)}, bf16[512,1024]{1,0:T(8,128)(2,1)}, u32[]{:S(2)}, u32[]{:S(2)}) collective-permute-start(bf16[512,1024]{1,0:T(8,128)(2,1)} %constant_dynamic-slice_fusion), channel_id=1, source_target_pairs={{0,4},{4,8},{8,12},{1,5},{5,9},{9,13},{2,6},{6,10},{10,14},{3,7},{... | collective-permute-start | bytes 3145736 | tf_op jit(solution)/shard_map/ppermute | solution.py:180
  166.3 47.3 %collective-permute-start.18 = (bf16[512,1024]{1,0:T(8,128)(2,1)}, bf16[512,1024]{1,0:T(8,128)(2,1)}, u32[]{:S(2)}, u32[]{:S(2)}) collective-permute-start(bf16[512,1024]{1,0:T(8,128)(2,1)} %constant_dynamic-slice_fusion), channel_id=1, source_target_pairs={{4,0},{8,4},{12,8},{5,1},{9,5},{13,9},{6,2},{10,6},{14,10},{7,3},{... | collective-permute-start | bytes 3145736 | tf_op jit(solution)/shard_map/ppermute | solution.py:180
  216.2 25.3 %collective-permute-start.20 = (bf16[512,1024]{1,0:T(8,128)(2,1)}, bf16[512,1024]{1,0:T(8,128)(2,1)S(1)}, u32[]{:S(2)}, u32[]{:S(2)}) collective-permute-start(bf16[512,1024]{1,0:T(8,128)(2,1)} %collective-permute-done.17), channel_id=1, source_target_pairs={{4,8},{8,12},{5,9},{9,13},{6,10},{10,14},{7,11},{11,15},{20,24},{2... | collective-permute-start | bytes 3145736 | tf_op jit(solution)/shard_map/ppermute | solution.py:180
  218.2 27.4 %collective-permute-start.21 = (bf16[512,1024]{1,0:T(8,128)(2,1)}, bf16[512,1024]{1,0:T(8,128)(2,1)S(1)}, u32[]{:S(2)}, u32[]{:S(2)}) collective-permute-start(bf16[512,1024]{1,0:T(8,128)(2,1)} %collective-permute-done.18), channel_id=1, source_target_pairs={{4,0},{8,4},{5,1},{9,5},{6,2},{10,6},{7,3},{11,7},{20,16},{24,20},... | collective-permute-start | bytes 3145736 | tf_op jit(solution)/shard_map/ppermute | solution.py:180
  245.8 24.6 %collective-permute-start.22 = (bf16[512,1024]{1,0:T(8,128)(2,1)S(1)}, bf16[512,1024]{1,0:T(8,128)(2,1)S(1)}, u32[]{:S(2)}, u32[]{:S(2)}) collective-permute-start(bf16[512,1024]{1,0:T(8,128)(2,1)S(1)} %slice.50), channel_id=1, source_target_pairs={{0,16},{16,0},{1,17},{17,1},{2,18},{18,2},{3,19},{19,3},{4,20},{20... | collective-permute-start | bytes 3145736 | tf_op jit(solution)/shard_map/ppermute | solution.py:180
  247.4 23.4 %collective-permute-start.23 = (bf16[512,1024]{1,0:T(8,128)(2,1)S(1)}, bf16[512,1024]{1,0:T(8,128)(2,1)S(1)}, u32[]{:S(2)}, u32[]{:S(2)}) collective-permute-start(bf16[512,1024]{1,0:T(8,128)(2,1)S(1)} %collective-permute-done.20), channel_id=1, source_target_pairs={{8,12},{9,13},{10,14},{11,15},{24,28},{25,29},{26,30},{27,31}} | collective-permute-start | bytes 3145736 | tf_op jit(solution)/shard_map/ppermute | solution.py:180
  248.1 25.3 %collective-permute-start.24 = (bf16[512,1024]{1,0:T(8,128)(2,1)S(1)}, bf16[512,1024]{1,0:T(8,128)(2,1)S(1)}, u32[]{:S(2)}, u32[]{:S(2)}) collective-permute-start(bf16[512,1024]{1,0:T(8,128)(2,1)S(1)} %collective-permute-done.21), channel_id=1, source_target_pairs={{4,0},{5,1},{6,2},{7,3},{20,16},{21,17},{22,18},{23,19}} | collective-permute-start | bytes 3145736 | tf_op jit(solution)/shard_map/ppermute | solution.py:180
  277.3 27.0 %collective-permute-start.25 = (bf16[512,1024]{1,0:T(8,128)(2,1)S(1)}, bf16[512,1024]{1,0:T(8,128)(2,1)S(1)}, u32[]{:S(2)}, u32[]{:S(2)}) collective-permute-start(bf16[512,1024]{1,0:T(8,128)(2,1)S(1)} %convert_element_type.131), channel_id=1, source_target_pairs={{2,0},{18,16},{3,1},{19,17},{6,4},{22,20},{7,5},{23,21},{8,10},{24... | collective-permute-start | bytes 3145736 | tf_op jit(solution)/shard_map/ppermute | solution.py:180
  279.4 14.9 %collective-permute-start.29 = (bf16[512,512]{1,0:T(8,128)(2,1)S(1)}, bf16[512,512]{1,0:T(8,128)(2,1)S(1)}, u32[]{:S(2)}, u32[]{:S(2)}) collective-permute-start(bf16[512,512]{1,0:T(8,128)(2,1)S(1)} %slice.51), channel_id=1, source_target_pairs={{0,16},{16,0},{1,17},{17,1},{2,18},{18,2},{3,19},{19,3},{4,20},{20... | collective-permute-start | bytes 1572872 | tf_op jit(solution)/shard_map/ppermute | solution.py:180
  280.8 25.1 %collective-permute-start.27 = (bf16[512,512]{1,0:T(8,128)(2,1)S(1)}, bf16[512,512]{1,0:T(8,128)(2,1)S(1)}, u32[]{:S(2)}, u32[]{:S(2)}) collective-permute-start(bf16[512,512]{1,0:T(8,128)(2,1)S(1)} %slice.52), channel_id=1, source_target_pairs={{0,16},{16,0},{1,17},{17,1},{2,18},{18,2},{3,19},{19,3},{4,20},{20... | collective-permute-start | bytes 1572872 | tf_op jit(solution)/shard_map/ppermute | solution.py:180
  296.0 14.7 %collective-permute-start.30 = (bf16[512,512]{1,0:T(8,128)(2,1)}, bf16[512,512]{1,0:T(8,128)(2,1)}, u32[]{:S(2)}, u32[]{:S(2)}) collective-permute-start(bf16[512,512]{1,0:T(8,128)(2,1)} %fusion.7), channel_id=1, source_target_pairs={{0,2},{16,18},{1,3},{17,19},{4,6},{20,22},{5,7},{21,23},{10,8},{26... | collective-permute-start | bytes 1572872 | tf_op jit(solution)/shard_map/ppermute | solution.py:180
  306.9 14.2 %collective-permute-start.31 = (bf16[512,512]{1,0:T(8,128)(2,1)}, bf16[512,512]{1,0:T(8,128)(2,1)}, u32[]{:S(2)}, u32[]{:S(2)}) collective-permute-start(bf16[512,512]{1,0:T(8,128)(2,1)} %convert_element_type.141), channel_id=1, source_target_pairs={{0,2},{16,18},{1,3},{17,19},{4,6},{20,22},{5,7},{21,23},{10,8},{26... | collective-permute-start | bytes 1572872 | tf_op jit(solution)/shard_map/ppermute | solution.py:180
  (28 other events, 204.5 us)

commit v3 on v2

--- a/solution.py
+++ b/solution.py
@@ -445,6 +445,8 @@
     arrived = [outgoing[0]] + [
         shift(outgoing[m], "dp", [(i, i ^ m) for i in range(4)]) for m in range(1, 4)
     ]
+    *arrived, q_up[1], q_down[1] = lax.optimization_barrier((*arrived, q_up[1], q_down[1]))
+    hop(q_up, q_down)
     to_here = (tile_dest == z).astype(jnp.int32)
     from_each = jnp.sum(to_here, axis=1)
     first_place = jnp.cumsum(from_each) - from_each
@@ -472,11 +474,6 @@
     cosine = jnp.concatenate([cosine, cosine], axis=1)
     sine = jnp.concatenate([-sine, sine], axis=1)
 
-    packed, squares, q_up[1], q_down[1] = lax.optimization_barrier(
-        (packed, squares, q_up[1], q_down[1])
-    )
-    hop(q_up, q_down)
-
     widened = packed.astype(jnp.float32)
     squares = squares + shift(squares, "pair", SWAP)
     squares = squares + shift(squares, "tensor", SWAP)
@@ -484,15 +481,17 @@
     normed = (widened * lax.rsqrt(squares / (4 * width) + norm_eps) * gain).astype(jnp.bfloat16)
     peer = shift(normed, "groups", SWAP)
     across_own = shift(normed, "tensor", SWAP)
-    across_peer = shift(peer, "tensor", SWAP)
-    q_up[2], q_down[2], peer, across_own, across_peer = lax.optimization_barrier(
-        (q_up[2], q_down[2], peer, across_own, across_peer)
+    q_up[2], q_down[2], peer, across_own = lax.optimization_barrier(
+        (q_up[2], q_down[2], peer, across_own)
     )
     hop(q_up, q_down)
     here = jnp.concatenate([normed, peer], axis=0)
+    here_other, across_peer = shift(here, "pair", SWAP), shift(peer, "tensor", SWAP)
+    here_other, across_peer, o_own, q_up[3], q_down[3] = lax.optimization_barrier(
+        (here_other, across_peer, o_own, q_up[3], q_down[3])
+    )
     across = jnp.concatenate([across_own, across_peer], axis=0)
-    shares = [here, shift(here, "pair", SWAP), across, shift(across, "pair", SWAP)]
-    *shares, o_own = lax.optimization_barrier((*shares, o_own))
+    shares = [here, here_other, across, shift(across, "pair", SWAP)]
     o_up, o_down = [o_own], [o_own]
     hop(o_up, o_down)
 
@@ -505,7 +504,6 @@
     q_blocks = by_partner(q_up[:3] + [q_up[2]], q_down[:3] + [q_down[2]])
     at = jnp.arange(4, dtype=jnp.int32) ^ z ^ t
     lin = linear_rows(at[:3], shares, q_blocks[:3])
-    lin, q_up[3], q_down[3] = lax.optimization_barrier((lin, q_up[3], q_down[3]))
     context = attend_rows(
         shares, at[3], by_partner(q_up, q_down)[3], lin, bias, cosine, sine, positions, tile_rows
     )

time: 327 us -> 326 us (level)
  waiting for transfers between devices: 193 us -> 197 us
  local copies, waits for them, and re-layouts: 15.3 us -> 11.6 us
    unnamed x41 -> x33, local copies, waits for them, and re-layouts: 8.5 us -> 3.51 us
    ppermute x32, waiting for transfers between devices: 193 us -> 197 us  [shift(): return lax.ppermute(values, axis, pairs)]
  transfers between devices with their start and end apart: 32 -> 32, of which waited for: 19 -> 18; matrix products, arithmetic and copies ran while one was open for 9% -> 9% of each run, Pallas kernels for 8% -> 7%
where the time goes in v3:
time: 326 us; the launch traced here: 323 us
  waiting for transfers between devices  197 us (60%)
  starting transfers between devices  54.3 us (17%)
  Pallas kernels  26.3 us (8%)
  other arithmetic  25.3 us (8%)
  local copies, waits for them, and re-layouts  11.6 us (4%)
  matrix products  8.21 us (3%)
    ppermute x32, waiting for transfers between devices, shift(): return lax.ppermute(values, axis, pairs)  197 us
    ppermute x32, starting transfers between devices, shift(): return lax.ppermute(values, axis, pairs)  54.3 us
    pallas_call x1, Pallas kernels, attend_rows(): pl.pallas_call(attention_kernel, grid_spec=pltpu.PrefetchScalarGridSpec(n...  10.3 us
    pallas_call x1, Pallas kernels, linear_rows(): pl.pallas_call(linear_kernel, in_specs=[pl.BlockSpec(memory_space=pltpu.S...  9.28 us
    dot_general x6, matrix products, project(): return jnp.dot(context, block, preferred_element_type=jnp.float32)  8.21 us
  transfers between devices with their start and end apart: 32, of which 18 were waited for; matrix products, arithmetic and copies ran while one was open for 9% of the time, Pallas kernels for 7%

profile of v3, /device:TPU:12, one launch (start us, length us, event | category | flops | bytes accessed | tf_op | source)
XLA Modules:
  0.0 323.0 jit_solution(995874316049686495)
XLA Ops:
  2.9 3.5 %collective-permute-start.3 = (bf16[1024,768]{1,0:T(8,128)(2,1)S(1)}, bf16[1024,768]{1,0:T(8,128)(2,1)}, u32[]{:S(2)}, u32[]{:S(2)}) collective-permute-start(bf16[1024,768]{1,0:T(8,128)(2,1)S(1)} %pad_maximum_fusion.1.refs_4_), channel_id=1, source_target_pairs={{0,4},{4,8},{8,12},{1,5},{5,9},{9,13},{2,6},{6,10},{10,14},{3,7},{... | collective-permute-start | bytes 4718600 | tf_op jit(solution)/shard_map/ppermute | solution.py:180
  6.4 3.5 %collective-permute-start.4 = (bf16[1024,768]{1,0:T(8,128)(2,1)S(1)}, bf16[1024,768]{1,0:T(8,128)(2,1)}, u32[]{:S(2)}, u32[]{:S(2)}) collective-permute-start(bf16[1024,768]{1,0:T(8,128)(2,1)S(1)} %pad_maximum_fusion.1.refs_4_), channel_id=1, source_target_pairs={{4,0},{8,4},{12,8},{5,1},{9,5},{13,9},{6,2},{10,6},{14,10},{7,3},{... | collective-permute-start | bytes 4718600 | tf_op jit(solution)/shard_map/ppermute | solution.py:180
  11.6 3.8 %shard_map.118 = (bf16[2,128,1024]{2,1,0:T(8,128)(2,1)}, bf16[2,128,1024]{2,1,0:T(8,128)(2,1)}, bf16[2,128,1024]{2,1,0:T(8,128)(2,1)}, bf16[2,128,1024]{2,1,0:T(8,128)(2,1)}) custom-call(s32[8]{0:T(128)} %min.17.slots_ref, bf16[8,128,1024]{2,1,0:T(8,128)(2,1)} %bitcast.37, bf16[8,128,1024]{2,1,0:T(8,128)(2,1)} %bitcast.38, bf16[8,128,1024]{2,1,0:T(8,128)(2,1)} %bitcast.39, ...), custom_call_target="tpu_custom_call" | custom-call | bytes 4194304 | tf_op jit(solution)/shard_map/pallas_call | solution.py:328
  19.7 46.2 %collective-permute-done = bf16[256,1024]{1,0:T(8,128)(2,1)S(1)} collective-permute-done((bf16[256,1024]{1,0:T(8,128)(2,1)}, bf16[256,1024]{1,0:T(8,128)(2,1)S(1)}, u32[]{:S(2)}, u32[]{:S(2)}) %collective-permute-start) | collective-permute-done | bytes 524320 | tf_op jit(solution)/shard_map/ppermute | solution.py:180
  65.8 9.3 %collective-permute-done.1 = bf16[256,1024]{1,0:T(8,128)(2,1)S(1)} collective-permute-done((bf16[256,1024]{1,0:T(8,128)(2,1)}, bf16[256,1024]{1,0:T(8,128)(2,1)S(1)}, u32[]{:S(2)}, u32[]{:S(2)}) %collective-permute-start.1) | collective-permute-done | bytes 524320 | tf_op jit(solution)/shard_map/ppermute | solution.py:180
  75.1 14.1 %collective-permute-done.2 = bf16[256,1024]{1,0:T(8,128)(2,1)S(1)} collective-permute-done((bf16[256,1024]{1,0:T(8,128)(2,1)}, bf16[256,1024]{1,0:T(8,128)(2,1)S(1)}, u32[]{:S(2)}, u32[]{:S(2)}) %collective-permute-start.2) | collective-permute-done | bytes 524320 | tf_op jit(solution)/shard_map/ppermute | solution.py:180
  90.0 2.9 shard_map.119
  106.1 22.1 %collective-permute-done.10 = bf16[512,1024]{1,0:T(8,128)(2,1)S(1)} collective-permute-done((bf16[512,1024]{1,0:T(8,128)(2,1)S(1)}, bf16[512,1024]{1,0:T(8,128)(2,1)S(1)}, u32[]{:S(2)}, u32[]{:S(2)}) %collective-permute-start.10) | collective-permute-done | bytes 1048608 | tf_op jit(solution)/shard_map/ppermute | solution.py:180
  130.3 5.3 %collective-permute-done.8 = bf16[1024,768]{1,0:T(8,128)(2,1)} collective-permute-done((bf16[1024,768]{1,0:T(8,128)(2,1)}, bf16[1024,768]{1,0:T(8,128)(2,1)}, u32[]{:S(2)}, u32[]{:S(2)}) %collective-permute-start.8) | collective-permute-done | bytes 1572896 | tf_op jit(solution)/shard_map/ppermute | solution.py:180
  138.9 3.3 %collective-permute-start.14 = (bf16[1024,768]{1,0:T(8,128)(2,1)}, bf16[1024,768]{1,0:T(8,128)(2,1)}, u32[]{:S(2)}, u32[]{:S(2)}) collective-permute-start(bf16[1024,768]{1,0:T(8,128)(2,1)} %collective-permute-done.8), channel_id=1, source_target_pairs={{4,0},{5,1},{6,2},{7,3},{20,16},{21,17},{22,18},{23,19}} | collective-permute-start | bytes 4718600 | tf_op jit(solution)/shard_map/ppermute | solution.py:180
  147.5 20.3 %collective-permute-done.12 = bf16[512,1024]{1,0:T(8,128)(2,1)} collective-permute-done((bf16[512,1024]{1,0:T(8,128)(2,1)}, bf16[512,1024]{1,0:T(8,128)(2,1)}, u32[]{:S(2)}, u32[]{:S(2)}) %collective-permute-start.12) | collective-permute-done | bytes 1048608 | tf_op jit(solution)/shard_map/ppermute | solution.py:180
  167.8 7.9 %collective-permute-done.14 = bf16[1024,768]{1,0:T(8,128)(2,1)} collective-permute-done((bf16[1024,768]{1,0:T(8,128)(2,1)}, bf16[1024,768]{1,0:T(8,128)(2,1)}, u32[]{:S(2)}, u32[]{:S(2)}) %collective-permute-start.14) | collective-permute-done | bytes 1572896 | tf_op jit(solution)/shard_map/ppermute | solution.py:180
  181.6 4.9 %collective-permute-start.18 = (bf16[512,1024]{1,0:T(8,128)(2,1)}, bf16[512,1024]{1,0:T(8,128)(2,1)}, u32[]{:S(2)}, u32[]{:S(2)}) collective-permute-start(bf16[512,1024]{1,0:T(8,128)(2,1)} %constant_dynamic-slice_fusion), channel_id=1, source_target_pairs={{4,0},{8,4},{12,8},{5,1},{9,5},{13,9},{6,2},{10,6},{14,10},{7,3},{... | collective-permute-start | bytes 3145736 | tf_op jit(solution)/shard_map/ppermute | solution.py:180
  191.3 3.3 %broadcast_select_fusion = (bf16[1024,768]{1,0:T(8,128)(2,1)S(1)}, bf16[1024,768]{1,0:T(8,128)(2,1)S(1)}) fusion(bf16[1024,768]{1,0:T(8,128)(2,1)} %collective-permute-done.4, bf16[1024,768]{1,0:T(8,128)(2,1)} %collective-permute-done.3, pred[]{:T(512)S(6)} %eq.128, bf16[1024,768]{1,0:T(8,128)(2,1)} %collective-permute-done.13, ...), kind=kLoop, calls=%fused_computation.16 | loop fusion | flops 3145728 | bytes 9437187 | tf_op jit(solution)/shard_map/jit(_where)/select_n | solution.py:499
  194.6 9.3 %shard_map.120.refs_5_ = f32[1024,768]{1,0:T(8,128)S(1)} custom-call(s32[3]{0:T(128)S(1)} %bitcast.36, bf16[1024,1024]{1,0:T(8,128)(2,1)S(1)} %pad_maximum_fusion.refs_0_, bf16[1024,1024]{1,0:T(8,128)(2,1)} %collective-permute-done.11.refs_1_, bf16[1024,1024]{1,0:T(8,128)(2,1)} %constant_dynamic-update-slice_fusion.refs_2_, ...), custom_call_target="tpu_custom_call" | custom-call | tf_op jit(solution)/shard_map/pallas_call | solution.py:222
  203.9 10.3 %shard_map.121 = bf16[1024,512]{1,0:T(8,128)(2,1)S(1)} custom-call(s32[1]{0:T(128)} %slice.27.at_ref, bf16[1024,1024]{1,0:T(8,128)(2,1)S(1)} %pad_maximum_fusion.refs_0_, bf16[1024,1024]{1,0:T(8,128)(2,1)} %collective-permute-done.11.refs_1_, bf16[1024,1024]{1,0:T(8,128)(2,1)} %constant_dynamic-update-slice_fusion.refs_2_, ...), custom_call_target="tpu_custom_call" | custom-call | tf_op jit(solution)/shard_map/pallas_call | solution.py:292
  223.8 18.3 %collective-permute-done.20 = bf16[512,1024]{1,0:T(8,128)(2,1)S(1)} collective-permute-done((bf16[512,1024]{1,0:T(8,128)(2,1)}, bf16[512,1024]{1,0:T(8,128)(2,1)S(1)}, u32[]{:S(2)}, u32[]{:S(2)}) %collective-permute-start.20) | collective-permute-done | bytes 1048608 | tf_op jit(solution)/shard_map/ppermute | solution.py:180
  242.0 4.1 %collective-permute-done.21 = bf16[512,1024]{1,0:T(8,128)(2,1)S(1)} collective-permute-done((bf16[512,1024]{1,0:T(8,128)(2,1)}, bf16[512,1024]{1,0:T(8,128)(2,1)S(1)}, u32[]{:S(2)}, u32[]{:S(2)}) %collective-permute-start.21) | collective-permute-done | bytes 1048608 | tf_op jit(solution)/shard_map/ppermute | solution.py:180
  251.5 19.7 %collective-permute-done.22 = bf16[512,1024]{1,0:T(8,128)(2,1)S(1)} collective-permute-done((bf16[512,1024]{1,0:T(8,128)(2,1)S(1)}, bf16[512,1024]{1,0:T(8,128)(2,1)S(1)}, u32[]{:S(2)}, u32[]{:S(2)}) %collective-permute-start.22) | collective-permute-done | bytes 1048608 | tf_op jit(solution)/shard_map/ppermute | solution.py:180
  281.9 11.9 %collective-permute-done.29 = bf16[512,512]{1,0:T(8,128)(2,1)S(1)} collective-permute-done((bf16[512,512]{1,0:T(8,128)(2,1)S(1)}, bf16[512,512]{1,0:T(8,128)(2,1)S(1)}, u32[]{:S(2)}, u32[]{:S(2)}) %collective-permute-start.29) | collective-permute-done | bytes 524320 | tf_op jit(solution)/shard_map/ppermute | solution.py:180
  294.8 5.5 %collective-permute-start.30 = (bf16[512,512]{1,0:T(8,128)(2,1)}, bf16[512,512]{1,0:T(8,128)(2,1)}, u32[]{:S(2)}, u32[]{:S(2)}) collective-permute-start(bf16[512,512]{1,0:T(8,128)(2,1)} %fusion.7), channel_id=1, source_target_pairs={{0,2},{16,18},{1,3},{17,19},{4,6},{20,22},{5,7},{21,23},{10,8},{26... | collective-permute-start | bytes 1572872 | tf_op jit(solution)/shard_map/ppermute | solution.py:180
  300.2 3.6 %collective-permute-done.25 = bf16[512,1024]{1,0:T(8,128)(2,1)S(1)} collective-permute-done((bf16[512,1024]{1,0:T(8,128)(2,1)S(1)}, bf16[512,1024]{1,0:T(8,128)(2,1)S(1)}, u32[]{:S(2)}, u32[]{:S(2)}) %collective-permute-start.25) | collective-permute-done | bytes 1048608 | tf_op jit(solution)/shard_map/ppermute | solution.py:180
  306.5 3.7 %collective-permute-start.31 = (bf16[512,512]{1,0:T(8,128)(2,1)}, bf16[512,512]{1,0:T(8,128)(2,1)}, u32[]{:S(2)}, u32[]{:S(2)}) collective-permute-start(bf16[512,512]{1,0:T(8,128)(2,1)} %convert_element_type.145), channel_id=1, source_target_pairs={{0,2},{16,18},{1,3},{17,19},{4,6},{20,22},{5,7},{21,23},{10,8},{26... | collective-permute-start | bytes 1572872 | tf_op jit(solution)/shard_map/ppermute | solution.py:180
  311.7 8.3 %collective-permute-done.31 = bf16[512,512]{1,0:T(8,128)(2,1)} collective-permute-done((bf16[512,512]{1,0:T(8,128)(2,1)}, bf16[512,512]{1,0:T(8,128)(2,1)}, u32[]{:S(2)}, u32[]{:S(2)}) %collective-permute-start.31) | collective-permute-done | bytes 524320 | tf_op jit(solution)/shard_map/ppermute | solution.py:180
  (146 shorter events, 77.6 us)
Async XLA Ops:
  2.9 86.2 %collective-permute-start.3 = (bf16[1024,768]{1,0:T(8,128)(2,1)S(1)}, bf16[1024,768]{1,0:T(8,128)(2,1)}, u32[]{:S(2)}, u32[]{:S(2)}) collective-permute-start(bf16[1024,768]{1,0:T(8,128)(2,1)S(1)} %pad_maximum_fusion.1.refs_4_), channel_id=1, source_target_pairs={{0,4},{4,8},{8,12},{1,5},{5,9},{9,13},{2,6},{6,10},{10,14},{3,7},{... | collective-permute-start | bytes 4718600 | tf_op jit(solution)/shard_map/ppermute | solution.py:180
  6.4 82.7 %collective-permute-start.4 = (bf16[1024,768]{1,0:T(8,128)(2,1)S(1)}, bf16[1024,768]{1,0:T(8,128)(2,1)}, u32[]{:S(2)}, u32[]{:S(2)}) collective-permute-start(bf16[1024,768]{1,0:T(8,128)(2,1)S(1)} %pad_maximum_fusion.1.refs_4_), channel_id=1, source_target_pairs={{4,0},{8,4},{12,8},{5,1},{9,5},{13,9},{6,2},{10,6},{14,10},{7,3},{... | collective-permute-start | bytes 4718600 | tf_op jit(solution)/shard_map/ppermute | solution.py:180
  15.4 50.5 %collective-permute-start = (bf16[256,1024]{1,0:T(8,128)(2,1)}, bf16[256,1024]{1,0:T(8,128)(2,1)S(1)}, u32[]{:S(2)}, u32[]{:S(2)}) collective-permute-start(bf16[256,1024]{1,0:T(8,128)(2,1)} %bitcast.55), channel_id=1, source_target_pairs={{0,4},{4,0},{8,12},{12,8},{1,5},{5,1},{9,13},{13,9},{2,6},{6,2},{1... | collective-permute-start | bytes 1572872 | tf_op jit(solution)/shard_map/ppermute | solution.py:180
  15.4 59.6 %collective-permute-start.1 = (bf16[256,1024]{1,0:T(8,128)(2,1)}, bf16[256,1024]{1,0:T(8,128)(2,1)S(1)}, u32[]{:S(2)}, u32[]{:S(2)}) collective-permute-start(bf16[256,1024]{1,0:T(8,128)(2,1)} %bitcast.54), channel_id=1, source_target_pairs={{0,8},{4,12},{8,0},{12,4},{1,9},{5,13},{9,1},{13,5},{2,10},{6,14},... | collective-permute-start | bytes 1572872 | tf_op jit(solution)/shard_map/ppermute | solution.py:180
  17.8 71.3 %collective-permute-start.2 = (bf16[256,1024]{1,0:T(8,128)(2,1)}, bf16[256,1024]{1,0:T(8,128)(2,1)S(1)}, u32[]{:S(2)}, u32[]{:S(2)}) collective-permute-start(bf16[256,1024]{1,0:T(8,128)(2,1)} %bitcast.53), channel_id=1, source_target_pairs={{0,12},{4,8},{8,4},{12,0},{1,13},{5,9},{9,5},{13,1},{2,14},{6,10},... | collective-permute-start | bytes 1572872 | tf_op jit(solution)/shard_map/ppermute | solution.py:180
  94.1 36.2 %collective-permute-start.7 = (bf16[1024,768]{1,0:T(8,128)(2,1)}, bf16[1024,768]{1,0:T(8,128)(2,1)}, u32[]{:S(2)}, u32[]{:S(2)}) collective-permute-start(bf16[1024,768]{1,0:T(8,128)(2,1)} %collective-permute-done.3), channel_id=1, source_target_pairs={{4,8},{8,12},{5,9},{9,13},{6,10},{10,14},{7,11},{11,15},{20,24},{2... | collective-permute-start | bytes 4718600 | tf_op jit(solution)/shard_map/ppermute | solution.py:180
  96.9 38.7 %collective-permute-start.8 = (bf16[1024,768]{1,0:T(8,128)(2,1)}, bf16[1024,768]{1,0:T(8,128)(2,1)}, u32[]{:S(2)}, u32[]{:S(2)}) collective-permute-start(bf16[1024,768]{1,0:T(8,128)(2,1)} %collective-permute-done.4), channel_id=1, source_target_pairs={{4,0},{8,4},{5,1},{9,5},{6,2},{10,6},{7,3},{11,7},{20,16},{24,20},... | collective-permute-start | bytes 4718600 | tf_op jit(solution)/shard_map/ppermute | solution.py:180
  104.0 24.2 %collective-permute-start.10 = (bf16[512,1024]{1,0:T(8,128)(2,1)S(1)}, bf16[512,1024]{1,0:T(8,128)(2,1)S(1)}, u32[]{:S(2)}, u32[]{:S(2)}) collective-permute-start(bf16[512,1024]{1,0:T(8,128)(2,1)S(1)} %fusion.1), channel_id=1, source_target_pairs={{0,2},{2,0},{1,3},{3,1},{4,6},{6,4},{5,7},{7,5},{8,10},{10,8},{9,1... | collective-permute-start | bytes 3145736 | tf_op jit(solution)/shard_map/ppermute | solution.py:180
  105.6 23.9 %collective-permute-start.9 = (bf16[512,1024]{1,0:T(8,128)(2,1)S(1)}, bf16[512,1024]{1,0:T(8,128)(2,1)}, u32[]{:S(2)}, u32[]{:S(2)}) collective-permute-start(bf16[512,1024]{1,0:T(8,128)(2,1)S(1)} %fusion.1), channel_id=1, source_target_pairs={{0,16},{16,0},{1,17},{17,1},{2,18},{18,2},{3,19},{19,3},{4,20},{20... | collective-permute-start | bytes 3145736 | tf_op jit(solution)/shard_map/ppermute | solution.py:180
  137.0 38.7 %collective-permute-start.11 = (bf16[1024,1024]{1,0:T(8,128)(2,1)S(1)}, bf16[1024,1024]{1,0:T(8,128)(2,1)}, u32[]{:S(2)}, u32[]{:S(2)}) collective-permute-start(bf16[1024,1024]{1,0:T(8,128)(2,1)S(1)} %pad_maximum_fusion.refs_0_), channel_id=1, source_target_pairs={{0,1},{1,0},{2,3},{3,2},{4,5},{5,4},{6,7},{7,6},{8,9},{9,8},{10,11... | collective-permute-start | bytes 6291464 | tf_op jit(solution)/shard_map/ppermute | solution.py:180
  137.0 30.8 %collective-permute-start.13 = (bf16[1024,768]{1,0:T(8,128)(2,1)}, bf16[1024,768]{1,0:T(8,128)(2,1)}, u32[]{:S(2)}, u32[]{:S(2)}) collective-permute-start(bf16[1024,768]{1,0:T(8,128)(2,1)} %collective-permute-done.7), channel_id=1, source_target_pairs={{8,12},{9,13},{10,14},{11,15},{24,28},{25,29},{26,30},{27,31}} | collective-permute-start | bytes 4718600 | tf_op jit(solution)/shard_map/ppermute | solution.py:180
  138.9 36.8 %collective-permute-start.14 = (bf16[1024,768]{1,0:T(8,128)(2,1)}, bf16[1024,768]{1,0:T(8,128)(2,1)}, u32[]{:S(2)}, u32[]{:S(2)}) collective-permute-start(bf16[1024,768]{1,0:T(8,128)(2,1)} %collective-permute-done.8), channel_id=1, source_target_pairs={{4,0},{5,1},{6,2},{7,3},{20,16},{21,17},{22,18},{23,19}} | collective-permute-start | bytes 4718600 | tf_op jit(solution)/shard_map/ppermute | solution.py:180
  142.2 25.6 %collective-permute-start.12 = (bf16[512,1024]{1,0:T(8,128)(2,1)}, bf16[512,1024]{1,0:T(8,128)(2,1)}, u32[]{:S(2)}, u32[]{:S(2)}) collective-permute-start(bf16[512,1024]{1,0:T(8,128)(2,1)} %collective-permute-done.9), channel_id=1, source_target_pairs={{0,2},{2,0},{1,3},{3,1},{4,6},{6,4},{5,7},{7,5},{8,10},{10,8},{9,1... | collective-permute-start | bytes 3145736 | tf_op jit(solution)/shard_map/ppermute | solution.py:180
  178.0 16.6 %collective-permute-start.15 = (bf16[1024,1024]{1,0:T(8,128)(2,1)}, bf16[1024,1024]{1,0:T(8,128)(2,1)}, u32[]{:S(2)}, u32[]{:S(2)}) collective-permute-start(bf16[1024,1024]{1,0:T(8,128)(2,1)} %constant_dynamic-update-slice_fusion.refs_2_), channel_id=1, source_target_pairs={{0,1},{1,0},{2,3},{3,2},{4,5},{5,4},{6,7},{7,6},{8,9},{9,8},{10,11... | collective-permute-start | bytes 6291464 | tf_op jit(solution)/shard_map/ppermute | solution.py:180
  179.7 34.5 %collective-permute-start.17 = (bf16[512,1024]{1,0:T(8,128)(2,1)}, bf16[512,1024]{1,0:T(8,128)(2,1)}, u32[]{:S(2)}, u32[]{:S(2)}) collective-permute-start(bf16[512,1024]{1,0:T(8,128)(2,1)} %constant_dynamic-slice_fusion), channel_id=1, source_target_pairs={{0,4},{4,8},{8,12},{1,5},{5,9},{9,13},{2,6},{6,10},{10,14},{3,7},{... | collective-permute-start | bytes 3145736 | tf_op jit(solution)/shard_map/ppermute | solution.py:180
  181.6 32.6 %collective-permute-start.18 = (bf16[512,1024]{1,0:T(8,128)(2,1)}, bf16[512,1024]{1,0:T(8,128)(2,1)}, u32[]{:S(2)}, u32[]{:S(2)}) collective-permute-start(bf16[512,1024]{1,0:T(8,128)(2,1)} %constant_dynamic-slice_fusion), channel_id=1, source_target_pairs={{4,0},{8,4},{12,8},{5,1},{9,5},{13,9},{6,2},{10,6},{14,10},{7,3},{... | collective-permute-start | bytes 3145736 | tf_op jit(solution)/shard_map/ppermute | solution.py:180
  217.1 24.9 %collective-permute-start.20 = (bf16[512,1024]{1,0:T(8,128)(2,1)}, bf16[512,1024]{1,0:T(8,128)(2,1)S(1)}, u32[]{:S(2)}, u32[]{:S(2)}) collective-permute-start(bf16[512,1024]{1,0:T(8,128)(2,1)} %collective-permute-done.17), channel_id=1, source_target_pairs={{4,8},{8,12},{5,9},{9,13},{6,10},{10,14},{7,11},{11,15},{20,24},{2... | collective-permute-start | bytes 3145736 | tf_op jit(solution)/shard_map/ppermute | solution.py:180
  218.5 27.7 %collective-permute-start.21 = (bf16[512,1024]{1,0:T(8,128)(2,1)}, bf16[512,1024]{1,0:T(8,128)(2,1)S(1)}, u32[]{:S(2)}, u32[]{:S(2)}) collective-permute-start(bf16[512,1024]{1,0:T(8,128)(2,1)} %collective-permute-done.18), channel_id=1, source_target_pairs={{4,0},{8,4},{5,1},{9,5},{6,2},{10,6},{7,3},{11,7},{20,16},{24,20},... | collective-permute-start | bytes 3145736 | tf_op jit(solution)/shard_map/ppermute | solution.py:180
  246.3 24.8 %collective-permute-start.22 = (bf16[512,1024]{1,0:T(8,128)(2,1)S(1)}, bf16[512,1024]{1,0:T(8,128)(2,1)S(1)}, u32[]{:S(2)}, u32[]{:S(2)}) collective-permute-start(bf16[512,1024]{1,0:T(8,128)(2,1)S(1)} %slice.50), channel_id=1, source_target_pairs={{0,16},{16,0},{1,17},{17,1},{2,18},{18,2},{3,19},{19,3},{4,20},{20... | collective-permute-start | bytes 3145736 | tf_op jit(solution)/shard_map/ppermute | solution.py:180
  247.9 23.7 %collective-permute-start.23 = (bf16[512,1024]{1,0:T(8,128)(2,1)S(1)}, bf16[512,1024]{1,0:T(8,128)(2,1)S(1)}, u32[]{:S(2)}, u32[]{:S(2)}) collective-permute-start(bf16[512,1024]{1,0:T(8,128)(2,1)S(1)} %collective-permute-done.20), channel_id=1, source_target_pairs={{8,12},{9,13},{10,14},{11,15},{24,28},{25,29},{26,30},{27,31}} | collective-permute-start | bytes 3145736 | tf_op jit(solution)/shard_map/ppermute | solution.py:180
  248.6 24.4 %collective-permute-start.24 = (bf16[512,1024]{1,0:T(8,128)(2,1)S(1)}, bf16[512,1024]{1,0:T(8,128)(2,1)S(1)}, u32[]{:S(2)}, u32[]{:S(2)}) collective-permute-start(bf16[512,1024]{1,0:T(8,128)(2,1)S(1)} %collective-permute-done.21), channel_id=1, source_target_pairs={{4,0},{5,1},{6,2},{7,3},{20,16},{21,17},{22,18},{23,19}} | collective-permute-start | bytes 3145736 | tf_op jit(solution)/shard_map/ppermute | solution.py:180
  276.8 27.0 %collective-permute-start.25 = (bf16[512,1024]{1,0:T(8,128)(2,1)S(1)}, bf16[512,1024]{1,0:T(8,128)(2,1)S(1)}, u32[]{:S(2)}, u32[]{:S(2)}) collective-permute-start(bf16[512,1024]{1,0:T(8,128)(2,1)S(1)} %convert_element_type.135), channel_id=1, source_target_pairs={{2,0},{18,16},{3,1},{19,17},{6,4},{22,20},{7,5},{23,21},{8,10},{24... | collective-permute-start | bytes 3145736 | tf_op jit(solution)/shard_map/ppermute | solution.py:180
  280.3 25.1 %collective-permute-start.27 = (bf16[512,512]{1,0:T(8,128)(2,1)S(1)}, bf16[512,512]{1,0:T(8,128)(2,1)S(1)}, u32[]{:S(2)}, u32[]{:S(2)}) collective-permute-start(bf16[512,512]{1,0:T(8,128)(2,1)S(1)} %slice.52), channel_id=1, source_target_pairs={{0,16},{16,0},{1,17},{17,1},{2,18},{18,2},{3,19},{19,3},{4,20},{20... | collective-permute-start | bytes 1572872 | tf_op jit(solution)/shard_map/ppermute | solution.py:180
  294.8 15.5 %collective-permute-start.30 = (bf16[512,512]{1,0:T(8,128)(2,1)}, bf16[512,512]{1,0:T(8,128)(2,1)}, u32[]{:S(2)}, u32[]{:S(2)}) collective-permute-start(bf16[512,512]{1,0:T(8,128)(2,1)} %fusion.7), channel_id=1, source_target_pairs={{0,2},{16,18},{1,3},{17,19},{4,6},{20,22},{5,7},{21,23},{10,8},{26... | collective-permute-start | bytes 1572872 | tf_op jit(solution)/shard_map/ppermute | solution.py:180
  (24 other events, 291.5 us)

commit v4 on v3

--- a/solution.py
+++ b/solution.py
@@ -445,8 +445,12 @@
     arrived = [outgoing[0]] + [
         shift(outgoing[m], "dp", [(i, i ^ m) for i in range(4)]) for m in range(1, 4)
     ]
-    *arrived, q_up[1], q_down[1] = lax.optimization_barrier((*arrived, q_up[1], q_down[1]))
+    *arrived, q_up[1], q_down[1], o_own = lax.optimization_barrier(
+        (*arrived, q_up[1], q_down[1], o_own)
+    )
     hop(q_up, q_down)
+    o_up, o_down = [o_own], [o_own]
+    hop(o_up, o_down)
     to_here = (tile_dest == z).astype(jnp.int32)
     from_each = jnp.sum(to_here, axis=1)
     first_place = jnp.cumsum(from_each) - from_each
@@ -481,19 +485,19 @@
     normed = (widened * lax.rsqrt(squares / (4 * width) + norm_eps) * gain).astype(jnp.bfloat16)
     peer = shift(normed, "groups", SWAP)
     across_own = shift(normed, "tensor", SWAP)
-    q_up[2], q_down[2], peer, across_own = lax.optimization_barrier(
-        (q_up[2], q_down[2], peer, across_own)
+    q_up[2], q_down[2], o_up[1], o_down[1], peer, across_own = lax.optimization_barrier(
+        (q_up[2], q_down[2], o_up[1], o_down[1], peer, across_own)
     )
     hop(q_up, q_down)
+    hop(o_up, o_down)
     here = jnp.concatenate([normed, peer], axis=0)
-    here_other, across_peer = shift(here, "pair", SWAP), shift(peer, "tensor", SWAP)
-    here_other, across_peer, o_own, q_up[3], q_down[3] = lax.optimization_barrier(
-        (here_other, across_peer, o_own, q_up[3], q_down[3])
-    )
+    across_peer = shift(peer, "tensor", SWAP)
+    across_peer, q_up[3], q_down[3], o_up[2], o_down[2] = lax.optimization_barrier(
+        (across_peer, q_up[3], q_down[3], o_up[2], o_down[2])
+    )
+    hop(o_up, o_down)
     across = jnp.concatenate([across_own, across_peer], axis=0)
-    shares = [here, here_other, across, shift(across, "pair", SWAP)]
-    o_up, o_down = [o_own], [o_own]
-    hop(o_up, o_down)
+    shares = [here, shift(here, "pair", SWAP), across, shift(across, "pair", SWAP)]
 
     def by_partner(up, down):
         first = jnp.where(z % 2 == 0, down[1], up[1])
@@ -507,8 +511,7 @@
     context = attend_rows(
         shares, at[3], by_partner(q_up, q_down)[3], lin, bias, cosine, sine, positions, tile_rows
     )
-    context, o_up[1], o_down[1] = lax.optimization_barrier((context, o_up[1], o_down[1]))
-    hop(o_up, o_down)
+    context, o_up[3], o_down[3] = lax.optimization_barrier((context, o_up[3], o_down[3]))
 
     every = ("groups", "dp", "tensor", "pair")
     index = lambda zz, yy, xx, cc: ((yy * 4 + zz) * 2 + xx) * 2 + cc
@@ -542,10 +545,7 @@
 
     o_first = jnp.where(z % 2 == 0, o_down[1], o_up[1])
     first = to_core(o_own, o_first)
-    first, o_up[2], o_down[2] = lax.optimization_barrier((first, o_up[2], o_down[2]))
-    hop(o_up, o_down)
     first = to_group(first)
-    first, o_up[3], o_down[3] = lax.optimization_barrier((first, o_up[3], o_down[3]))
     first = to_chip(first, 0, both)
     o_blocks = by_partner(o_up, o_down)
     second = [

time: 326 us -> 340 us (1.043)
  starting transfers between devices: 54.3 us -> 61.8 us
  waiting for transfers between devices: 197 us -> 201 us
    ppermute x32, starting transfers between devices: 54.3 us -> 61.8 us  [shift(): return lax.ppermute(values, axis, pairs)]
    ppermute x32, waiting for transfers between devices: 197 us -> 201 us  [shift(): return lax.ppermute(values, axis, pairs)]
  transfers between devices with their start and end apart: 32 -> 32, of which waited for: 18 -> 13; matrix products, arithmetic and copies ran while one was open for 9% -> 11% of each run, Pallas kernels for 7% -> 8%
where the time goes in v4:
time: 340 us; the launch traced here: 336 us
  waiting for transfers between devices  201 us (59%)
  starting transfers between devices  61.8 us (18%)
  other arithmetic  27.4 us (8%)
  Pallas kernels  26.5 us (8%)
  local copies, waits for them, and re-layouts  10.7 us (3%)
  matrix products  7.91 us (2%)
    ppermute x32, waiting for transfers between devices, shift(): return lax.ppermute(values, axis, pairs)  201 us
    ppermute x32, starting transfers between devices, shift(): return lax.ppermute(values, axis, pairs)  61.8 us
    pallas_call x1, Pallas kernels, attend_rows(): pl.pallas_call(attention_kernel, grid_spec=pltpu.PrefetchScalarGridSpec(n...  10.6 us
    pallas_call x1, Pallas kernels, linear_rows(): pl.pallas_call(linear_kernel, in_specs=[pl.BlockSpec(memory_space=pltpu.S...  9.33 us
    dot_general x6, matrix products, project(): return jnp.dot(context, block, preferred_element_type=jnp.float32)  7.91 us
  transfers between devices with their start and end apart: 32, of which 13 were waited for; matrix products, arithmetic and copies ran while one was open for 11% of the time, Pallas kernels for 8%

profile of v4, /device:TPU:12, one launch (start us, length us, event | category | flops | bytes accessed | tf_op | source)
XLA Modules:
  0.0 335.8 jit_solution(192799259766286193)
XLA Ops:
  2.9 3.5 %collective-permute-start.3 = (bf16[1024,768]{1,0:T(8,128)(2,1)S(1)}, bf16[1024,768]{1,0:T(8,128)(2,1)}, u32[]{:S(2)}, u32[]{:S(2)}) collective-permute-start(bf16[1024,768]{1,0:T(8,128)(2,1)S(1)} %pad_maximum_fusion.1.refs_4_), channel_id=1, source_target_pairs={{0,4},{4,8},{8,12},{1,5},{5,9},{9,13},{2,6},{6,10},{10,14},{3,7},{... | collective-permute-start | bytes 4718600 | tf_op jit(solution)/shard_map/ppermute | solution.py:180
  6.4 3.5 %collective-permute-start.4 = (bf16[1024,768]{1,0:T(8,128)(2,1)S(1)}, bf16[1024,768]{1,0:T(8,128)(2,1)}, u32[]{:S(2)}, u32[]{:S(2)}) collective-permute-start(bf16[1024,768]{1,0:T(8,128)(2,1)S(1)} %pad_maximum_fusion.1.refs_4_), channel_id=1, source_target_pairs={{4,0},{8,4},{12,8},{5,1},{9,5},{13,9},{6,2},{10,6},{14,10},{7,3},{... | collective-permute-start | bytes 4718600 | tf_op jit(solution)/shard_map/ppermute | solution.py:180
  11.6 3.6 %shard_map.118 = (bf16[2,128,1024]{2,1,0:T(8,128)(2,1)}, bf16[2,128,1024]{2,1,0:T(8,128)(2,1)}, bf16[2,128,1024]{2,1,0:T(8,128)(2,1)}, bf16[2,128,1024]{2,1,0:T(8,128)(2,1)}) custom-call(s32[8]{0:T(128)} %min.17.slots_ref, bf16[8,128,1024]{2,1,0:T(8,128)(2,1)} %bitcast.37, bf16[8,128,1024]{2,1,0:T(8,128)(2,1)} %bitcast.38, bf16[8,128,1024]{2,1,0:T(8,128)(2,1)} %bitcast.39, ...), custom_call_target="tpu_custom_call" | custom-call | bytes 4194304 | tf_op jit(solution)/shard_map/pallas_call | solution.py:328
  20.1 45.7 %collective-permute-done = bf16[256,1024]{1,0:T(8,128)(2,1)S(1)} collective-permute-done((bf16[256,1024]{1,0:T(8,128)(2,1)}, bf16[256,1024]{1,0:T(8,128)(2,1)S(1)}, u32[]{:S(2)}, u32[]{:S(2)}) %collective-permute-start) | collective-permute-done | bytes 524320 | tf_op jit(solution)/shard_map/ppermute | solution.py:180
  65.8 9.3 %collective-permute-done.1 = bf16[256,1024]{1,0:T(8,128)(2,1)S(1)} collective-permute-done((bf16[256,1024]{1,0:T(8,128)(2,1)}, bf16[256,1024]{1,0:T(8,128)(2,1)S(1)}, u32[]{:S(2)}, u32[]{:S(2)}) %collective-permute-start.1) | collective-permute-done | bytes 524320 | tf_op jit(solution)/shard_map/ppermute | solution.py:180
  75.1 14.1 %collective-permute-done.2 = bf16[256,1024]{1,0:T(8,128)(2,1)S(1)} collective-permute-done((bf16[256,1024]{1,0:T(8,128)(2,1)}, bf16[256,1024]{1,0:T(8,128)(2,1)S(1)}, u32[]{:S(2)}, u32[]{:S(2)}) %collective-permute-start.2) | collective-permute-done | bytes 524320 | tf_op jit(solution)/shard_map/ppermute | solution.py:180
  96.8 5.1 %collective-permute-start.7 = (bf16[1024,768]{1,0:T(8,128)(2,1)}, bf16[1024,768]{1,0:T(8,128)(2,1)}, u32[]{:S(2)}, u32[]{:S(2)}) collective-permute-start(bf16[1024,768]{1,0:T(8,128)(2,1)} %collective-permute-done.3), channel_id=1, source_target_pairs={{4,8},{8,12},{5,9},{9,13},{6,10},{10,14},{7,11},{11,15},{20,24},{2... | collective-permute-start | bytes 4718600 | tf_op jit(solution)/shard_map/ppermute | solution.py:180
  106.1 5.0 %collective-permute-start.9 = (bf16[512,1024]{1,0:T(8,128)(2,1)S(1)}, bf16[512,1024]{1,0:T(8,128)(2,1)}, u32[]{:S(2)}, u32[]{:S(2)}) collective-permute-start(bf16[512,1024]{1,0:T(8,128)(2,1)S(1)} %constant_dynamic-slice_fusion), channel_id=1, source_target_pairs={{0,4},{4,8},{8,12},{1,5},{5,9},{9,13},{2,6},{6,10},{10,14},{3,7},{... | collective-permute-start | bytes 3145736 | tf_op jit(solution)/shard_map/ppermute | solution.py:180
  113.2 4.8 %collective-permute-done.10 = bf16[512,1024]{1,0:T(8,128)(2,1)} collective-permute-done((bf16[512,1024]{1,0:T(8,128)(2,1)S(1)}, bf16[512,1024]{1,0:T(8,128)(2,1)}, u32[]{:S(2)}, u32[]{:S(2)}) %collective-permute-start.10) | collective-permute-done | bytes 1048608 | tf_op jit(solution)/shard_map/ppermute | solution.py:180
  119.5 38.1 %collective-permute-done.9 = bf16[512,1024]{1,0:T(8,128)(2,1)} collective-permute-done((bf16[512,1024]{1,0:T(8,128)(2,1)S(1)}, bf16[512,1024]{1,0:T(8,128)(2,1)}, u32[]{:S(2)}, u32[]{:S(2)}) %collective-permute-start.9) | collective-permute-done | bytes 1048608 | tf_op jit(solution)/shard_map/ppermute | solution.py:180
  163.6 6.7 %collective-permute-start.17 = (bf16[512,1024]{1,0:T(8,128)(2,1)}, bf16[512,1024]{1,0:T(8,128)(2,1)}, u32[]{:S(2)}, u32[]{:S(2)}) collective-permute-start(bf16[512,1024]{1,0:T(8,128)(2,1)} %collective-permute-done.9), channel_id=1, source_target_pairs={{4,8},{8,12},{5,9},{9,13},{6,10},{10,14},{7,11},{11,15},{20,24},{2... | collective-permute-start | bytes 3145736 | tf_op jit(solution)/shard_map/ppermute | solution.py:180
  175.1 12.1 %collective-permute-done.14 = bf16[512,1024]{1,0:T(8,128)(2,1)} collective-permute-done((bf16[512,1024]{1,0:T(8,128)(2,1)}, bf16[512,1024]{1,0:T(8,128)(2,1)}, u32[]{:S(2)}, u32[]{:S(2)}) %collective-permute-start.14) | collective-permute-done | bytes 1048608 | tf_op jit(solution)/shard_map/ppermute | solution.py:180
  187.2 4.2 %collective-permute-done.17 = bf16[512,1024]{1,0:T(8,128)(2,1)} collective-permute-done((bf16[512,1024]{1,0:T(8,128)(2,1)}, bf16[512,1024]{1,0:T(8,128)(2,1)}, u32[]{:S(2)}, u32[]{:S(2)}) %collective-permute-start.17) | collective-permute-done | bytes 1048608 | tf_op jit(solution)/shard_map/ppermute | solution.py:180
  191.4 26.2 %collective-permute-done.18 = bf16[512,1024]{1,0:T(8,128)(2,1)} collective-permute-done((bf16[512,1024]{1,0:T(8,128)(2,1)}, bf16[512,1024]{1,0:T(8,128)(2,1)}, u32[]{:S(2)}, u32[]{:S(2)}) %collective-permute-start.18) | collective-permute-done | bytes 1048608 | tf_op jit(solution)/shard_map/ppermute | solution.py:180
  223.3 5.4 %collective-permute-start.22 = (bf16[512,1024]{1,0:T(8,128)(2,1)}, bf16[512,1024]{1,0:T(8,128)(2,1)}, u32[]{:S(2)}, u32[]{:S(2)}) collective-permute-start(bf16[512,1024]{1,0:T(8,128)(2,1)} %collective-permute-done.18), channel_id=1, source_target_pairs={{4,0},{5,1},{6,2},{7,3},{20,16},{21,17},{22,18},{23,19}} | collective-permute-start | bytes 3145736 | tf_op jit(solution)/shard_map/ppermute | solution.py:180
  233.4 3.3 broadcast_select_fusion
  236.7 9.3 %shard_map.120.refs_5_ = f32[1024,768]{1,0:T(8,128)S(1)} custom-call(s32[3]{0:T(128)S(1)} %bitcast.36, bf16[1024,1024]{1,0:T(8,128)(2,1)S(1)} %pad_maximum_fusion.refs_0_, bf16[1024,1024]{1,0:T(8,128)(2,1)} %collective-permute-done.13.refs_1_, bf16[1024,1024]{1,0:T(8,128)(2,1)} %constant_dynamic-update-slice_fusion.refs_2_, ...), custom_call_target="tpu_custom_call" | custom-call | tf_op jit(solution)/shard_map/pallas_call | solution.py:222
  246.1 10.6 %shard_map.121 = bf16[1024,512]{1,0:T(8,128)(2,1)S(1)} custom-call(s32[1]{0:T(128)} %slice.27.at_ref, bf16[1024,1024]{1,0:T(8,128)(2,1)S(1)} %pad_maximum_fusion.refs_0_, bf16[1024,1024]{1,0:T(8,128)(2,1)} %collective-permute-done.13.refs_1_, bf16[1024,1024]{1,0:T(8,128)(2,1)} %constant_dynamic-update-slice_fusion.refs_2_, ...), custom_call_target="tpu_custom_call" | custom-call | tf_op jit(solution)/shard_map/pallas_call | solution.py:292
  271.1 22.3 %collective-permute-done.24 = bf16[512,1024]{1,0:T(8,128)(2,1)S(1)} collective-permute-done((bf16[512,1024]{1,0:T(8,128)(2,1)S(1)}, bf16[512,1024]{1,0:T(8,128)(2,1)S(1)}, u32[]{:S(2)}, u32[]{:S(2)}) %collective-permute-start.24) | collective-permute-done | bytes 1048608 | tf_op jit(solution)/shard_map/ppermute | solution.py:180
  297.5 7.2 %collective-permute-done.29 = bf16[512,512]{1,0:T(8,128)(2,1)S(1)} collective-permute-done((bf16[512,512]{1,0:T(8,128)(2,1)S(1)}, bf16[512,512]{1,0:T(8,128)(2,1)S(1)}, u32[]{:S(2)}, u32[]{:S(2)}) %collective-permute-start.29) | collective-permute-done | bytes 524320 | tf_op jit(solution)/shard_map/ppermute | solution.py:180
  305.6 3.5 %collective-permute-start.30 = (bf16[512,512]{1,0:T(8,128)(2,1)}, bf16[512,512]{1,0:T(8,128)(2,1)}, u32[]{:S(2)}, u32[]{:S(2)}) collective-permute-start(bf16[512,512]{1,0:T(8,128)(2,1)} %fusion.8), channel_id=1, source_target_pairs={{0,2},{16,18},{1,3},{17,19},{4,6},{20,22},{5,7},{21,23},{10,8},{26... | collective-permute-start | bytes 1572872 | tf_op jit(solution)/shard_map/ppermute | solution.py:180
  309.2 5.9 %collective-permute-done.27 = bf16[512,512]{1,0:T(8,128)(2,1)S(1)} collective-permute-done((bf16[512,512]{1,0:T(8,128)(2,1)S(1)}, bf16[512,512]{1,0:T(8,128)(2,1)S(1)}, u32[]{:S(2)}, u32[]{:S(2)}) %collective-permute-start.27) | collective-permute-done | bytes 524320 | tf_op jit(solution)/shard_map/ppermute | solution.py:180
  315.2 4.0 %collective-permute-done.25 = bf16[512,1024]{1,0:T(8,128)(2,1)S(1)} collective-permute-done((bf16[512,1024]{1,0:T(8,128)(2,1)S(1)}, bf16[512,1024]{1,0:T(8,128)(2,1)S(1)}, u32[]{:S(2)}, u32[]{:S(2)}) %collective-permute-start.25) | collective-permute-done | bytes 1048608 | tf_op jit(solution)/shard_map/ppermute | solution.py:180
  325.7 7.0 %collective-permute-done.31 = bf16[512,512]{1,0:T(8,128)(2,1)} collective-permute-done((bf16[512,512]{1,0:T(8,128)(2,1)}, bf16[512,512]{1,0:T(8,128)(2,1)}, u32[]{:S(2)}, u32[]{:S(2)}) %collective-permute-start.31) | collective-permute-done | bytes 524320 | tf_op jit(solution)/shard_map/ppermute | solution.py:180
  (153 shorter events, 74.8 us)
Async XLA Ops:
  2.9 86.2 %collective-permute-start.3 = (bf16[1024,768]{1,0:T(8,128)(2,1)S(1)}, bf16[1024,768]{1,0:T(8,128)(2,1)}, u32[]{:S(2)}, u32[]{:S(2)}) collective-permute-start(bf16[1024,768]{1,0:T(8,128)(2,1)S(1)} %pad_maximum_fusion.1.refs_4_), channel_id=1, source_target_pairs={{0,4},{4,8},{8,12},{1,5},{5,9},{9,13},{2,6},{6,10},{10,14},{3,7},{... | collective-permute-start | bytes 4718600 | tf_op jit(solution)/shard_map/ppermute | solution.py:180
  6.4 82.7 %collective-permute-start.4 = (bf16[1024,768]{1,0:T(8,128)(2,1)S(1)}, bf16[1024,768]{1,0:T(8,128)(2,1)}, u32[]{:S(2)}, u32[]{:S(2)}) collective-permute-start(bf16[1024,768]{1,0:T(8,128)(2,1)S(1)} %pad_maximum_fusion.1.refs_4_), channel_id=1, source_target_pairs={{4,0},{8,4},{12,8},{5,1},{9,5},{13,9},{6,2},{10,6},{14,10},{7,3},{... | collective-permute-start | bytes 4718600 | tf_op jit(solution)/shard_map/ppermute | solution.py:180
  15.2 50.6 %collective-permute-start = (bf16[256,1024]{1,0:T(8,128)(2,1)}, bf16[256,1024]{1,0:T(8,128)(2,1)S(1)}, u32[]{:S(2)}, u32[]{:S(2)}) collective-permute-start(bf16[256,1024]{1,0:T(8,128)(2,1)} %bitcast.55), channel_id=1, source_target_pairs={{0,4},{4,0},{8,12},{12,8},{1,5},{5,1},{9,13},{13,9},{2,6},{6,2},{1... | collective-permute-start | bytes 1572872 | tf_op jit(solution)/shard_map/ppermute | solution.py:180
  15.3 59.8 %collective-permute-start.1 = (bf16[256,1024]{1,0:T(8,128)(2,1)}, bf16[256,1024]{1,0:T(8,128)(2,1)S(1)}, u32[]{:S(2)}, u32[]{:S(2)}) collective-permute-start(bf16[256,1024]{1,0:T(8,128)(2,1)} %bitcast.54), channel_id=1, source_target_pairs={{0,8},{4,12},{8,0},{12,4},{1,9},{5,13},{9,1},{13,5},{2,10},{6,14},... | collective-permute-start | bytes 1572872 | tf_op jit(solution)/shard_map/ppermute | solution.py:180
  18.1 71.1 %collective-permute-start.2 = (bf16[256,1024]{1,0:T(8,128)(2,1)}, bf16[256,1024]{1,0:T(8,128)(2,1)S(1)}, u32[]{:S(2)}, u32[]{:S(2)}) collective-permute-start(bf16[256,1024]{1,0:T(8,128)(2,1)} %bitcast.53), channel_id=1, source_target_pairs={{0,12},{4,8},{8,4},{12,0},{1,13},{5,9},{9,5},{13,1},{2,14},{6,10},... | collective-permute-start | bytes 1572872 | tf_op jit(solution)/shard_map/ppermute | solution.py:180
  90.0 28.1 %collective-permute-start.10 = (bf16[512,1024]{1,0:T(8,128)(2,1)S(1)}, bf16[512,1024]{1,0:T(8,128)(2,1)}, u32[]{:S(2)}, u32[]{:S(2)}) collective-permute-start(bf16[512,1024]{1,0:T(8,128)(2,1)S(1)} %constant_dynamic-slice_fusion), channel_id=1, source_target_pairs={{4,0},{8,4},{12,8},{5,1},{9,5},{13,9},{6,2},{10,6},{14,10},{7,3},{... | collective-permute-start | bytes 3145736 | tf_op jit(solution)/shard_map/ppermute | solution.py:180
  96.8 60.9 %collective-permute-start.7 = (bf16[1024,768]{1,0:T(8,128)(2,1)}, bf16[1024,768]{1,0:T(8,128)(2,1)}, u32[]{:S(2)}, u32[]{:S(2)}) collective-permute-start(bf16[1024,768]{1,0:T(8,128)(2,1)} %collective-permute-done.3), channel_id=1, source_target_pairs={{4,8},{8,12},{5,9},{9,13},{6,10},{10,14},{7,11},{11,15},{20,24},{2... | collective-permute-start | bytes 4718600 | tf_op jit(solution)/shard_map/ppermute | solution.py:180
  101.9 55.8 %collective-permute-start.8 = (bf16[1024,768]{1,0:T(8,128)(2,1)}, bf16[1024,768]{1,0:T(8,128)(2,1)}, u32[]{:S(2)}, u32[]{:S(2)}) collective-permute-start(bf16[1024,768]{1,0:T(8,128)(2,1)} %collective-permute-done.4), channel_id=1, source_target_pairs={{4,0},{8,4},{5,1},{9,5},{6,2},{10,6},{7,3},{11,7},{20,16},{24,20},... | collective-permute-start | bytes 4718600 | tf_op jit(solution)/shard_map/ppermute | solution.py:180
  106.1 51.6 %collective-permute-start.9 = (bf16[512,1024]{1,0:T(8,128)(2,1)S(1)}, bf16[512,1024]{1,0:T(8,128)(2,1)}, u32[]{:S(2)}, u32[]{:S(2)}) collective-permute-start(bf16[512,1024]{1,0:T(8,128)(2,1)S(1)} %constant_dynamic-slice_fusion), channel_id=1, source_target_pairs={{0,4},{4,8},{8,12},{1,5},{5,9},{9,13},{2,6},{6,10},{10,14},{3,7},{... | collective-permute-start | bytes 3145736 | tf_op jit(solution)/shard_map/ppermute | solution.py:180
  112.7 45.0 %collective-permute-start.11 = (bf16[512,1024]{1,0:T(8,128)(2,1)S(1)}, bf16[512,1024]{1,0:T(8,128)(2,1)}, u32[]{:S(2)}, u32[]{:S(2)}) collective-permute-start(bf16[512,1024]{1,0:T(8,128)(2,1)S(1)} %fusion.1), channel_id=1, source_target_pairs={{0,16},{16,0},{1,17},{17,1},{2,18},{18,2},{3,19},{19,3},{4,20},{20... | collective-permute-start | bytes 3145736 | tf_op jit(solution)/shard_map/ppermute | solution.py:180
  118.1 39.6 %collective-permute-start.12 = (bf16[512,1024]{1,0:T(8,128)(2,1)S(1)}, bf16[512,1024]{1,0:T(8,128)(2,1)S(1)}, u32[]{:S(2)}, u32[]{:S(2)}) collective-permute-start(bf16[512,1024]{1,0:T(8,128)(2,1)S(1)} %fusion.1), channel_id=1, source_target_pairs={{0,2},{2,0},{1,3},{3,1},{4,6},{6,4},{5,7},{7,5},{8,10},{10,8},{9,1... | collective-permute-start | bytes 3145736 | tf_op jit(solution)/shard_map/ppermute | solution.py:180
  157.7 59.8 %collective-permute-start.15 = (bf16[1024,768]{1,0:T(8,128)(2,1)}, bf16[1024,768]{1,0:T(8,128)(2,1)}, u32[]{:S(2)}, u32[]{:S(2)}) collective-permute-start(bf16[1024,768]{1,0:T(8,128)(2,1)} %collective-permute-done.7), channel_id=1, source_target_pairs={{8,12},{9,13},{10,14},{11,15},{24,28},{25,29},{26,30},{27,31}} | collective-permute-start | bytes 4718600 | tf_op jit(solution)/shard_map/ppermute | solution.py:180
  159.7 57.8 %collective-permute-start.16 = (bf16[1024,768]{1,0:T(8,128)(2,1)}, bf16[1024,768]{1,0:T(8,128)(2,1)}, u32[]{:S(2)}, u32[]{:S(2)}) collective-permute-start(bf16[1024,768]{1,0:T(8,128)(2,1)} %collective-permute-done.8), channel_id=1, source_target_pairs={{4,0},{5,1},{6,2},{7,3},{20,16},{21,17},{22,18},{23,19}} | collective-permute-start | bytes 4718600 | tf_op jit(solution)/shard_map/ppermute | solution.py:180
  162.1 25.1 %collective-permute-start.14 = (bf16[512,1024]{1,0:T(8,128)(2,1)}, bf16[512,1024]{1,0:T(8,128)(2,1)}, u32[]{:S(2)}, u32[]{:S(2)}) collective-permute-start(bf16[512,1024]{1,0:T(8,128)(2,1)} %collective-permute-done.11), channel_id=1, source_target_pairs={{0,2},{2,0},{1,3},{3,1},{4,6},{6,4},{5,7},{7,5},{8,10},{10,8},{9,1... | collective-permute-start | bytes 3145736 | tf_op jit(solution)/shard_map/ppermute | solution.py:180
  163.6 27.7 %collective-permute-start.17 = (bf16[512,1024]{1,0:T(8,128)(2,1)}, bf16[512,1024]{1,0:T(8,128)(2,1)}, u32[]{:S(2)}, u32[]{:S(2)}) collective-permute-start(bf16[512,1024]{1,0:T(8,128)(2,1)} %collective-permute-done.9), channel_id=1, source_target_pairs={{4,8},{8,12},{5,9},{9,13},{6,10},{10,14},{7,11},{11,15},{20,24},{2... | collective-permute-start | bytes 3145736 | tf_op jit(solution)/shard_map/ppermute | solution.py:180
  170.3 47.2 %collective-permute-start.18 = (bf16[512,1024]{1,0:T(8,128)(2,1)}, bf16[512,1024]{1,0:T(8,128)(2,1)}, u32[]{:S(2)}, u32[]{:S(2)}) collective-permute-start(bf16[512,1024]{1,0:T(8,128)(2,1)} %collective-permute-done.10), channel_id=1, source_target_pairs={{4,0},{8,4},{5,1},{9,5},{6,2},{10,6},{7,3},{11,7},{20,16},{24,20},... | collective-permute-start | bytes 3145736 | tf_op jit(solution)/shard_map/ppermute | solution.py:180
  187.2 49.5 %collective-permute-start.13 = (bf16[1024,1024]{1,0:T(8,128)(2,1)S(1)}, bf16[1024,1024]{1,0:T(8,128)(2,1)}, u32[]{:S(2)}, u32[]{:S(2)}) collective-permute-start(bf16[1024,1024]{1,0:T(8,128)(2,1)S(1)} %pad_maximum_fusion.refs_0_), channel_id=1, source_target_pairs={{0,1},{1,0},{2,3},{3,2},{4,5},{5,4},{6,7},{7,6},{8,9},{9,8},{10,11... | collective-permute-start | bytes 6291464 | tf_op jit(solution)/shard_map/ppermute | solution.py:180
  221.7 35.0 %collective-permute-start.21 = (bf16[512,1024]{1,0:T(8,128)(2,1)}, bf16[512,1024]{1,0:T(8,128)(2,1)}, u32[]{:S(2)}, u32[]{:S(2)}) collective-permute-start(bf16[512,1024]{1,0:T(8,128)(2,1)} %collective-permute-done.17), channel_id=1, source_target_pairs={{8,12},{9,13},{10,14},{11,15},{24,28},{25,29},{26,30},{27,31}} | collective-permute-start | bytes 3145736 | tf_op jit(solution)/shard_map/ppermute | solution.py:180
  223.3 33.4 %collective-permute-start.22 = (bf16[512,1024]{1,0:T(8,128)(2,1)}, bf16[512,1024]{1,0:T(8,128)(2,1)}, u32[]{:S(2)}, u32[]{:S(2)}) collective-permute-start(bf16[512,1024]{1,0:T(8,128)(2,1)} %collective-permute-done.18), channel_id=1, source_target_pairs={{4,0},{5,1},{6,2},{7,3},{20,16},{21,17},{22,18},{23,19}} | collective-permute-start | bytes 3145736 | tf_op jit(solution)/shard_map/ppermute | solution.py:180
  267.3 26.1 %collective-permute-start.24 = (bf16[512,1024]{1,0:T(8,128)(2,1)S(1)}, bf16[512,1024]{1,0:T(8,128)(2,1)S(1)}, u32[]{:S(2)}, u32[]{:S(2)}) collective-permute-start(bf16[512,1024]{1,0:T(8,128)(2,1)S(1)} %slice.55), channel_id=1, source_target_pairs={{0,16},{16,0},{1,17},{17,1},{2,18},{18,2},{3,19},{19,3},{4,20},{20... | collective-permute-start | bytes 3145736 | tf_op jit(solution)/shard_map/ppermute | solution.py:180
  269.6 25.4 %collective-permute-start.26 = (bf16[1024,512]{1,0:T(8,128)(2,1)S(1)}, bf16[1024,512]{1,0:T(8,128)(2,1)S(1)}, u32[]{:S(2)}, u32[]{:S(2)}) collective-permute-start(bf16[1024,512]{1,0:T(8,128)(2,1)S(1)} %convolution_convert_fusion.2), channel_id=1, source_target_pairs={{0,1},{1,0},{2,3},{3,2},{4,5},{5,4},{6,7},{7,6},{8,9},{9,8},{10,11... | collective-permute-start | bytes 3145736 | tf_op jit(solution)/shard_map/ppermute | solution.py:180
  270.5 34.1 %collective-permute-start.29 = (bf16[512,512]{1,0:T(8,128)(2,1)S(1)}, bf16[512,512]{1,0:T(8,128)(2,1)S(1)}, u32[]{:S(2)}, u32[]{:S(2)}) collective-permute-start(bf16[512,512]{1,0:T(8,128)(2,1)S(1)} %slice.56), channel_id=1, source_target_pairs={{0,16},{16,0},{1,17},{17,1},{2,18},{18,2},{3,19},{19,3},{4,20},{20... | collective-permute-start | bytes 1572872 | tf_op jit(solution)/shard_map/ppermute | solution.py:180
  293.8 25.5 %collective-permute-start.25 = (bf16[512,1024]{1,0:T(8,128)(2,1)S(1)}, bf16[512,1024]{1,0:T(8,128)(2,1)S(1)}, u32[]{:S(2)}, u32[]{:S(2)}) collective-permute-start(bf16[512,1024]{1,0:T(8,128)(2,1)S(1)} %fusion.3), channel_id=1, source_target_pairs={{2,0},{18,16},{3,1},{19,17},{6,4},{22,20},{7,5},{23,21},{8,10},{24... | collective-permute-start | bytes 3145736 | tf_op jit(solution)/shard_map/ppermute | solution.py:180
  295.9 19.2 %collective-permute-start.27 = (bf16[512,512]{1,0:T(8,128)(2,1)S(1)}, bf16[512,512]{1,0:T(8,128)(2,1)S(1)}, u32[]{:S(2)}, u32[]{:S(2)}) collective-permute-start(bf16[512,512]{1,0:T(8,128)(2,1)S(1)} %slice.57), channel_id=1, source_target_pairs={{0,16},{16,0},{1,17},{17,1},{2,18},{18,2},{3,19},{19,3},{4,20},{20... | collective-permute-start | bytes 1572872 | tf_op jit(solution)/shard_map/ppermute | solution.py:180
  (28 other events, 601.9 us)

commit v5 on v4

--- a/solution.py
+++ b/solution.py
@@ -445,12 +445,8 @@
     arrived = [outgoing[0]] + [
         shift(outgoing[m], "dp", [(i, i ^ m) for i in range(4)]) for m in range(1, 4)
     ]
-    *arrived, q_up[1], q_down[1], o_own = lax.optimization_barrier(
-        (*arrived, q_up[1], q_down[1], o_own)
-    )
+    *arrived, q_up[1], q_down[1] = lax.optimization_barrier((*arrived, q_up[1], q_down[1]))
     hop(q_up, q_down)
-    o_up, o_down = [o_own], [o_own]
-    hop(o_up, o_down)
     to_here = (tile_dest == z).astype(jnp.int32)
     from_each = jnp.sum(to_here, axis=1)
     first_place = jnp.cumsum(from_each) - from_each
@@ -485,15 +481,16 @@
     normed = (widened * lax.rsqrt(squares / (4 * width) + norm_eps) * gain).astype(jnp.bfloat16)
     peer = shift(normed, "groups", SWAP)
     across_own = shift(normed, "tensor", SWAP)
-    q_up[2], q_down[2], o_up[1], o_down[1], peer, across_own = lax.optimization_barrier(
-        (q_up[2], q_down[2], o_up[1], o_down[1], peer, across_own)
+    q_up[2], q_down[2], peer, across_own, o_own = lax.optimization_barrier(
+        (q_up[2], q_down[2], peer, across_own, o_own)
     )
     hop(q_up, q_down)
+    o_up, o_down = [o_own], [o_own]
     hop(o_up, o_down)
     here = jnp.concatenate([normed, peer], axis=0)
     across_peer = shift(peer, "tensor", SWAP)
-    across_peer, q_up[3], q_down[3], o_up[2], o_down[2] = lax.optimization_barrier(
-        (across_peer, q_up[3], q_down[3], o_up[2], o_down[2])
+    across_peer, q_up[3], q_down[3], o_up[1], o_down[1] = lax.optimization_barrier(
+        (across_peer, q_up[3], q_down[3], o_up[1], o_down[1])
     )
     hop(o_up, o_down)
     across = jnp.concatenate([across_own, across_peer], axis=0)
@@ -511,7 +508,8 @@
     context = attend_rows(
         shares, at[3], by_partner(q_up, q_down)[3], lin, bias, cosine, sine, positions, tile_rows
     )
-    context, o_up[3], o_down[3] = lax.optimization_barrier((context, o_up[3], o_down[3]))
+    context, o_up[2], o_down[2] = lax.optimization_barrier((context, o_up[2], o_down[2]))
+    hop(o_up, o_down)
 
     every = ("groups", "dp", "tensor", "pair")
     index = lambda zz, yy, xx, cc: ((yy * 4 + zz) * 2 + xx) * 2 + cc
@@ -546,6 +544,7 @@
     o_first = jnp.where(z % 2 == 0, o_down[1], o_up[1])
     first = to_core(o_own, o_first)
     first = to_group(first)
+    first, o_up[3], o_down[3] = lax.optimization_barrier((first, o_up[3], o_down[3]))
     first = to_chip(first, 0, both)
     o_blocks = by_partner(o_up, o_down)
     second = [

time: 340 us -> 323 us (0.950)
  waiting for transfers between devices: 201 us -> 192 us
  starting transfers between devices: 61.8 us -> 56.7 us
    ppermute x32, waiting for transfers between devices: 201 us -> 192 us  [shift(): return lax.ppermute(values, axis, pairs)]
    ppermute x32, starting transfers between devices: 61.8 us -> 56.7 us  [shift(): return lax.ppermute(values, axis, pairs)]
  transfers between devices with their start and end apart: 32 -> 32, of which waited for: 13 -> 17; matrix products, arithmetic and copies ran while one was open for 11% -> 9% of each run, Pallas kernels for 8% -> 7%
where the time goes in v5:
time: 323 us; the launch traced here: 320 us
  waiting for transfers between devices  192 us (59%)
  starting transfers between devices  56.7 us (18%)
  other arithmetic  26.8 us (8%)
  Pallas kernels  26.3 us (8%)
  local copies, waits for them, and re-layouts  9.77 us (3%)
  matrix products  7.86 us (2%)
    ppermute x32, waiting for transfers between devices, shift(): return lax.ppermute(values, axis, pairs)  192 us
    ppermute x32, starting transfers between devices, shift(): return lax.ppermute(values, axis, pairs)  56.7 us
    pallas_call x1, Pallas kernels, attend_rows(): pl.pallas_call(attention_kernel, grid_spec=pltpu.PrefetchScalarGridSpec(n...  10.5 us
    pallas_call x1, Pallas kernels, linear_rows(): pl.pallas_call(linear_kernel, in_specs=[pl.BlockSpec(memory_space=pltpu.S...  9.28 us
    dot_general x6, matrix products, project(): return jnp.dot(context, block, preferred_element_type=jnp.float32)  7.86 us
  transfers between devices with their start and end apart: 32, of which 17 were waited for; matrix products, arithmetic and copies ran while one was open for 9% of the time, Pallas kernels for 7%

profile of v5, /device:TPU:12, one launch (start us, length us, event | category | flops | bytes accessed | tf_op | source)
XLA Modules:
  0.0 320.0 jit_solution(14058622092136990386)
XLA Ops:
  2.9 3.5 %collective-permute-start.3 = (bf16[1024,768]{1,0:T(8,128)(2,1)S(1)}, bf16[1024,768]{1,0:T(8,128)(2,1)}, u32[]{:S(2)}, u32[]{:S(2)}) collective-permute-start(bf16[1024,768]{1,0:T(8,128)(2,1)S(1)} %pad_maximum_fusion.1.refs_4_), channel_id=1, source_target_pairs={{0,4},{4,8},{8,12},{1,5},{5,9},{9,13},{2,6},{6,10},{10,14},{3,7},{... | collective-permute-start | bytes 4718600 | tf_op jit(solution)/shard_map/ppermute | solution.py:180
  6.4 3.5 %collective-permute-start.4 = (bf16[1024,768]{1,0:T(8,128)(2,1)S(1)}, bf16[1024,768]{1,0:T(8,128)(2,1)}, u32[]{:S(2)}, u32[]{:S(2)}) collective-permute-start(bf16[1024,768]{1,0:T(8,128)(2,1)S(1)} %pad_maximum_fusion.1.refs_4_), channel_id=1, source_target_pairs={{4,0},{8,4},{12,8},{5,1},{9,5},{13,9},{6,2},{10,6},{14,10},{7,3},{... | collective-permute-start | bytes 4718600 | tf_op jit(solution)/shard_map/ppermute | solution.py:180
  11.6 3.6 %shard_map.118 = (bf16[2,128,1024]{2,1,0:T(8,128)(2,1)}, bf16[2,128,1024]{2,1,0:T(8,128)(2,1)}, bf16[2,128,1024]{2,1,0:T(8,128)(2,1)}, bf16[2,128,1024]{2,1,0:T(8,128)(2,1)}) custom-call(s32[8]{0:T(128)} %min.17.slots_ref, bf16[8,128,1024]{2,1,0:T(8,128)(2,1)} %bitcast.37, bf16[8,128,1024]{2,1,0:T(8,128)(2,1)} %bitcast.38, bf16[8,128,1024]{2,1,0:T(8,128)(2,1)} %bitcast.39, ...), custom_call_target="tpu_custom_call" | custom-call | bytes 4194304 | tf_op jit(solution)/shard_map/pallas_call | solution.py:328
  19.6 46.1 %collective-permute-done = bf16[256,1024]{1,0:T(8,128)(2,1)S(1)} collective-permute-done((bf16[256,1024]{1,0:T(8,128)(2,1)}, bf16[256,1024]{1,0:T(8,128)(2,1)S(1)}, u32[]{:S(2)}, u32[]{:S(2)}) %collective-permute-start) | collective-permute-done | bytes 524320 | tf_op jit(solution)/shard_map/ppermute | solution.py:180
  65.8 9.3 %collective-permute-done.1 = bf16[256,1024]{1,0:T(8,128)(2,1)S(1)} collective-permute-done((bf16[256,1024]{1,0:T(8,128)(2,1)}, bf16[256,1024]{1,0:T(8,128)(2,1)S(1)}, u32[]{:S(2)}, u32[]{:S(2)}) %collective-permute-start.1) | collective-permute-done | bytes 524320 | tf_op jit(solution)/shard_map/ppermute | solution.py:180
  75.1 14.1 %collective-permute-done.2 = bf16[256,1024]{1,0:T(8,128)(2,1)S(1)} collective-permute-done((bf16[256,1024]{1,0:T(8,128)(2,1)}, bf16[256,1024]{1,0:T(8,128)(2,1)S(1)}, u32[]{:S(2)}, u32[]{:S(2)}) %collective-permute-start.2) | collective-permute-done | bytes 524320 | tf_op jit(solution)/shard_map/ppermute | solution.py:180
  90.0 2.9 shard_map.119
  106.3 22.0 %collective-permute-done.10 = bf16[512,1024]{1,0:T(8,128)(2,1)S(1)} collective-permute-done((bf16[512,1024]{1,0:T(8,128)(2,1)S(1)}, bf16[512,1024]{1,0:T(8,128)(2,1)S(1)}, u32[]{:S(2)}, u32[]{:S(2)}) %collective-permute-start.10) | collective-permute-done | bytes 1048608 | tf_op jit(solution)/shard_map/ppermute | solution.py:180
  130.4 5.3 %collective-permute-done.8 = bf16[1024,768]{1,0:T(8,128)(2,1)} collective-permute-done((bf16[1024,768]{1,0:T(8,128)(2,1)}, bf16[1024,768]{1,0:T(8,128)(2,1)}, u32[]{:S(2)}, u32[]{:S(2)}) %collective-permute-start.8) | collective-permute-done | bytes 1572896 | tf_op jit(solution)/shard_map/ppermute | solution.py:180
  137.5 3.3 %collective-permute-start.14 = (bf16[1024,768]{1,0:T(8,128)(2,1)}, bf16[1024,768]{1,0:T(8,128)(2,1)}, u32[]{:S(2)}, u32[]{:S(2)}) collective-permute-start(bf16[1024,768]{1,0:T(8,128)(2,1)} %collective-permute-done.8), channel_id=1, source_target_pairs={{4,0},{5,1},{6,2},{7,3},{20,16},{21,17},{22,18},{23,19}} | collective-permute-start | bytes 4718600 | tf_op jit(solution)/shard_map/ppermute | solution.py:180
  144.3 4.9 %collective-permute-start.16 = (bf16[512,1024]{1,0:T(8,128)(2,1)S(1)}, bf16[512,1024]{1,0:T(8,128)(2,1)}, u32[]{:S(2)}, u32[]{:S(2)}) collective-permute-start(bf16[512,1024]{1,0:T(8,128)(2,1)S(1)} %constant_dynamic-slice_fusion), channel_id=1, source_target_pairs={{4,0},{8,4},{12,8},{5,1},{9,5},{13,9},{6,2},{10,6},{14,10},{7,3},{... | collective-permute-start | bytes 3145736 | tf_op jit(solution)/shard_map/ppermute | solution.py:180
  152.4 13.3 %collective-permute-done.12 = bf16[512,1024]{1,0:T(8,128)(2,1)} collective-permute-done((bf16[512,1024]{1,0:T(8,128)(2,1)}, bf16[512,1024]{1,0:T(8,128)(2,1)}, u32[]{:S(2)}, u32[]{:S(2)}) %collective-permute-start.12) | collective-permute-done | bytes 1048608 | tf_op jit(solution)/shard_map/ppermute | solution.py:180
  168.6 27.3 %collective-permute-done.16 = bf16[512,1024]{1,0:T(8,128)(2,1)} collective-permute-done((bf16[512,1024]{1,0:T(8,128)(2,1)S(1)}, bf16[512,1024]{1,0:T(8,128)(2,1)}, u32[]{:S(2)}, u32[]{:S(2)}) %collective-permute-start.16) | collective-permute-done | bytes 1048608 | tf_op jit(solution)/shard_map/ppermute | solution.py:180
  202.3 3.9 %collective-permute-start.20 = (bf16[512,1024]{1,0:T(8,128)(2,1)}, bf16[512,1024]{1,0:T(8,128)(2,1)}, u32[]{:S(2)}, u32[]{:S(2)}) collective-permute-start(bf16[512,1024]{1,0:T(8,128)(2,1)} %collective-permute-done.16), channel_id=1, source_target_pairs={{4,0},{8,4},{5,1},{9,5},{6,2},{10,6},{7,3},{11,7},{20,16},{24,20},... | collective-permute-start | bytes 3145736 | tf_op jit(solution)/shard_map/ppermute | solution.py:180
  210.9 3.3 %broadcast_select_fusion = (bf16[1024,768]{1,0:T(8,128)(2,1)S(1)}, bf16[1024,768]{1,0:T(8,128)(2,1)S(1)}) fusion(bf16[1024,768]{1,0:T(8,128)(2,1)} %collective-permute-done.4, bf16[1024,768]{1,0:T(8,128)(2,1)} %collective-permute-done.3, pred[]{:T(512)S(6)} %eq.128, bf16[1024,768]{1,0:T(8,128)(2,1)} %collective-permute-done.13, ...), kind=kLoop, calls=%fused_computation.16 | loop fusion | flops 3145728 | bytes 9437187 | tf_op jit(solution)/shard_map/jit(_where)/select_n | solution.py:500
  214.2 9.3 %shard_map.120.refs_5_ = f32[1024,768]{1,0:T(8,128)S(1)} custom-call(s32[3]{0:T(128)S(1)} %bitcast.36, bf16[1024,1024]{1,0:T(8,128)(2,1)S(1)} %pad_maximum_fusion.refs_0_, bf16[1024,1024]{1,0:T(8,128)(2,1)} %collective-permute-done.11.refs_1_, bf16[1024,1024]{1,0:T(8,128)(2,1)} %constant_dynamic-update-slice_fusion.refs_2_, ...), custom_call_target="tpu_custom_call" | custom-call | tf_op jit(solution)/shard_map/pallas_call | solution.py:222
  223.5 10.5 %shard_map.121 = bf16[1024,512]{1,0:T(8,128)(2,1)S(1)} custom-call(s32[1]{0:T(128)} %slice.27.at_ref, bf16[1024,1024]{1,0:T(8,128)(2,1)S(1)} %pad_maximum_fusion.refs_0_, bf16[1024,1024]{1,0:T(8,128)(2,1)} %collective-permute-done.11.refs_1_, bf16[1024,1024]{1,0:T(8,128)(2,1)} %constant_dynamic-update-slice_fusion.refs_2_, ...), custom_call_target="tpu_custom_call" | custom-call | tf_op jit(solution)/shard_map/pallas_call | solution.py:292
  236.7 4.0 %collective-permute-done.21 = bf16[1024,1024]{1,0:T(8,128)(2,1)S(1)} collective-permute-done((bf16[1024,1024]{1,0:T(8,128)(2,1)S(1)}, bf16[1024,1024]{1,0:T(8,128)(2,1)S(1)}, u32[]{:S(2)}, u32[]{:S(2)}) %collective-permute-start.21) | collective-permute-done | bytes 2097184 | tf_op jit(solution)/shard_map/ppermute | solution.py:180
  249.4 19.3 %collective-permute-done.22 = bf16[512,1024]{1,0:T(8,128)(2,1)S(1)} collective-permute-done((bf16[512,1024]{1,0:T(8,128)(2,1)S(1)}, bf16[512,1024]{1,0:T(8,128)(2,1)S(1)}, u32[]{:S(2)}, u32[]{:S(2)}) %collective-permute-start.22) | collective-permute-done | bytes 1048608 | tf_op jit(solution)/shard_map/ppermute | solution.py:180
  278.8 11.9 %collective-permute-done.29 = bf16[512,512]{1,0:T(8,128)(2,1)S(1)} collective-permute-done((bf16[512,512]{1,0:T(8,128)(2,1)S(1)}, bf16[512,512]{1,0:T(8,128)(2,1)S(1)}, u32[]{:S(2)}, u32[]{:S(2)}) %collective-permute-start.29) | collective-permute-done | bytes 524320 | tf_op jit(solution)/shard_map/ppermute | solution.py:180
  291.7 5.4 %collective-permute-start.30 = (bf16[512,512]{1,0:T(8,128)(2,1)}, bf16[512,512]{1,0:T(8,128)(2,1)}, u32[]{:S(2)}, u32[]{:S(2)}) collective-permute-start(bf16[512,512]{1,0:T(8,128)(2,1)} %fusion.7), channel_id=1, source_target_pairs={{0,2},{16,18},{1,3},{17,19},{4,6},{20,22},{5,7},{21,23},{10,8},{26... | collective-permute-start | bytes 1572872 | tf_op jit(solution)/shard_map/ppermute | solution.py:180
  297.1 3.5 %collective-permute-done.25 = bf16[512,1024]{1,0:T(8,128)(2,1)S(1)} collective-permute-done((bf16[512,1024]{1,0:T(8,128)(2,1)S(1)}, bf16[512,1024]{1,0:T(8,128)(2,1)S(1)}, u32[]{:S(2)}, u32[]{:S(2)}) %collective-permute-start.25) | collective-permute-done | bytes 1048608 | tf_op jit(solution)/shard_map/ppermute | solution.py:180
  303.4 3.7 %collective-permute-start.31 = (bf16[512,512]{1,0:T(8,128)(2,1)}, bf16[512,512]{1,0:T(8,128)(2,1)}, u32[]{:S(2)}, u32[]{:S(2)}) collective-permute-start(bf16[512,512]{1,0:T(8,128)(2,1)} %convert_element_type.145), channel_id=1, source_target_pairs={{0,2},{16,18},{1,3},{17,19},{4,6},{20,22},{5,7},{21,23},{10,8},{26... | collective-permute-start | bytes 1572872 | tf_op jit(solution)/shard_map/ppermute | solution.py:180
  308.7 8.3 %collective-permute-done.31 = bf16[512,512]{1,0:T(8,128)(2,1)} collective-permute-done((bf16[512,512]{1,0:T(8,128)(2,1)}, bf16[512,512]{1,0:T(8,128)(2,1)}, u32[]{:S(2)}, u32[]{:S(2)}) %collective-permute-start.31) | collective-permute-done | bytes 524320 | tf_op jit(solution)/shard_map/ppermute | solution.py:180
  (156 shorter events, 76.9 us)
Async XLA Ops:
  2.9 86.2 %collective-permute-start.3 = (bf16[1024,768]{1,0:T(8,128)(2,1)S(1)}, bf16[1024,768]{1,0:T(8,128)(2,1)}, u32[]{:S(2)}, u32[]{:S(2)}) collective-permute-start(bf16[1024,768]{1,0:T(8,128)(2,1)S(1)} %pad_maximum_fusion.1.refs_4_), channel_id=1, source_target_pairs={{0,4},{4,8},{8,12},{1,5},{5,9},{9,13},{2,6},{6,10},{10,14},{3,7},{... | collective-permute-start | bytes 4718600 | tf_op jit(solution)/shard_map/ppermute | solution.py:180
  6.4 82.7 %collective-permute-start.4 = (bf16[1024,768]{1,0:T(8,128)(2,1)S(1)}, bf16[1024,768]{1,0:T(8,128)(2,1)}, u32[]{:S(2)}, u32[]{:S(2)}) collective-permute-start(bf16[1024,768]{1,0:T(8,128)(2,1)S(1)} %pad_maximum_fusion.1.refs_4_), channel_id=1, source_target_pairs={{4,0},{8,4},{12,8},{5,1},{9,5},{13,9},{6,2},{10,6},{14,10},{7,3},{... | collective-permute-start | bytes 4718600 | tf_op jit(solution)/shard_map/ppermute | solution.py:180
  15.3 50.5 %collective-permute-start = (bf16[256,1024]{1,0:T(8,128)(2,1)}, bf16[256,1024]{1,0:T(8,128)(2,1)S(1)}, u32[]{:S(2)}, u32[]{:S(2)}) collective-permute-start(bf16[256,1024]{1,0:T(8,128)(2,1)} %bitcast.55), channel_id=1, source_target_pairs={{0,4},{4,0},{8,12},{12,8},{1,5},{5,1},{9,13},{13,9},{2,6},{6,2},{1... | collective-permute-start | bytes 1572872 | tf_op jit(solution)/shard_map/ppermute | solution.py:180
  15.4 59.7 %collective-permute-start.1 = (bf16[256,1024]{1,0:T(8,128)(2,1)}, bf16[256,1024]{1,0:T(8,128)(2,1)S(1)}, u32[]{:S(2)}, u32[]{:S(2)}) collective-permute-start(bf16[256,1024]{1,0:T(8,128)(2,1)} %bitcast.54), channel_id=1, source_target_pairs={{0,8},{4,12},{8,0},{12,4},{1,9},{5,13},{9,1},{13,5},{2,10},{6,14},... | collective-permute-start | bytes 1572872 | tf_op jit(solution)/shard_map/ppermute | solution.py:180
  18.0 71.2 %collective-permute-start.2 = (bf16[256,1024]{1,0:T(8,128)(2,1)}, bf16[256,1024]{1,0:T(8,128)(2,1)S(1)}, u32[]{:S(2)}, u32[]{:S(2)}) collective-permute-start(bf16[256,1024]{1,0:T(8,128)(2,1)} %bitcast.53), channel_id=1, source_target_pairs={{0,12},{4,8},{8,4},{12,0},{1,13},{5,9},{9,5},{13,1},{2,14},{6,10},... | collective-permute-start | bytes 1572872 | tf_op jit(solution)/shard_map/ppermute | solution.py:180
  94.1 36.3 %collective-permute-start.7 = (bf16[1024,768]{1,0:T(8,128)(2,1)}, bf16[1024,768]{1,0:T(8,128)(2,1)}, u32[]{:S(2)}, u32[]{:S(2)}) collective-permute-start(bf16[1024,768]{1,0:T(8,128)(2,1)} %collective-permute-done.3), channel_id=1, source_target_pairs={{4,8},{8,12},{5,9},{9,13},{6,10},{10,14},{7,11},{11,15},{20,24},{2... | collective-permute-start | bytes 4718600 | tf_op jit(solution)/shard_map/ppermute | solution.py:180
  97.0 38.7 %collective-permute-start.8 = (bf16[1024,768]{1,0:T(8,128)(2,1)}, bf16[1024,768]{1,0:T(8,128)(2,1)}, u32[]{:S(2)}, u32[]{:S(2)}) collective-permute-start(bf16[1024,768]{1,0:T(8,128)(2,1)} %collective-permute-done.4), channel_id=1, source_target_pairs={{4,0},{8,4},{5,1},{9,5},{6,2},{10,6},{7,3},{11,7},{20,16},{24,20},... | collective-permute-start | bytes 4718600 | tf_op jit(solution)/shard_map/ppermute | solution.py:180
  104.2 24.2 %collective-permute-start.10 = (bf16[512,1024]{1,0:T(8,128)(2,1)S(1)}, bf16[512,1024]{1,0:T(8,128)(2,1)S(1)}, u32[]{:S(2)}, u32[]{:S(2)}) collective-permute-start(bf16[512,1024]{1,0:T(8,128)(2,1)S(1)} %fusion.1), channel_id=1, source_target_pairs={{0,2},{2,0},{1,3},{3,1},{4,6},{6,4},{5,7},{7,5},{8,10},{10,8},{9,1... | collective-permute-start | bytes 3145736 | tf_op jit(solution)/shard_map/ppermute | solution.py:180
  105.7 23.9 %collective-permute-start.9 = (bf16[512,1024]{1,0:T(8,128)(2,1)S(1)}, bf16[512,1024]{1,0:T(8,128)(2,1)}, u32[]{:S(2)}, u32[]{:S(2)}) collective-permute-start(bf16[512,1024]{1,0:T(8,128)(2,1)S(1)} %fusion.1), channel_id=1, source_target_pairs={{0,16},{16,0},{1,17},{17,1},{2,18},{18,2},{3,19},{19,3},{4,20},{20... | collective-permute-start | bytes 3145736 | tf_op jit(solution)/shard_map/ppermute | solution.py:180
  135.7 60.2 %collective-permute-start.13 = (bf16[1024,768]{1,0:T(8,128)(2,1)}, bf16[1024,768]{1,0:T(8,128)(2,1)}, u32[]{:S(2)}, u32[]{:S(2)}) collective-permute-start(bf16[1024,768]{1,0:T(8,128)(2,1)} %collective-permute-done.7), channel_id=1, source_target_pairs={{8,12},{9,13},{10,14},{11,15},{24,28},{25,29},{26,30},{27,31}} | collective-permute-start | bytes 4718600 | tf_op jit(solution)/shard_map/ppermute | solution.py:180
  137.5 58.4 %collective-permute-start.14 = (bf16[1024,768]{1,0:T(8,128)(2,1)}, bf16[1024,768]{1,0:T(8,128)(2,1)}, u32[]{:S(2)}, u32[]{:S(2)}) collective-permute-start(bf16[1024,768]{1,0:T(8,128)(2,1)} %collective-permute-done.8), channel_id=1, source_target_pairs={{4,0},{5,1},{6,2},{7,3},{20,16},{21,17},{22,18},{23,19}} | collective-permute-start | bytes 4718600 | tf_op jit(solution)/shard_map/ppermute | solution.py:180
  140.9 24.8 %collective-permute-start.12 = (bf16[512,1024]{1,0:T(8,128)(2,1)}, bf16[512,1024]{1,0:T(8,128)(2,1)}, u32[]{:S(2)}, u32[]{:S(2)}) collective-permute-start(bf16[512,1024]{1,0:T(8,128)(2,1)} %collective-permute-done.9), channel_id=1, source_target_pairs={{0,2},{2,0},{1,3},{3,1},{4,6},{6,4},{5,7},{7,5},{8,10},{10,8},{9,1... | collective-permute-start | bytes 3145736 | tf_op jit(solution)/shard_map/ppermute | solution.py:180
  142.4 26.2 %collective-permute-start.15 = (bf16[512,1024]{1,0:T(8,128)(2,1)S(1)}, bf16[512,1024]{1,0:T(8,128)(2,1)}, u32[]{:S(2)}, u32[]{:S(2)}) collective-permute-start(bf16[512,1024]{1,0:T(8,128)(2,1)S(1)} %constant_dynamic-slice_fusion), channel_id=1, source_target_pairs={{0,4},{4,8},{8,12},{1,5},{5,9},{9,13},{2,6},{6,10},{10,14},{3,7},{... | collective-permute-start | bytes 3145736 | tf_op jit(solution)/shard_map/ppermute | solution.py:180
  144.3 51.6 %collective-permute-start.16 = (bf16[512,1024]{1,0:T(8,128)(2,1)S(1)}, bf16[512,1024]{1,0:T(8,128)(2,1)}, u32[]{:S(2)}, u32[]{:S(2)}) collective-permute-start(bf16[512,1024]{1,0:T(8,128)(2,1)S(1)} %constant_dynamic-slice_fusion), channel_id=1, source_target_pairs={{4,0},{8,4},{12,8},{5,1},{9,5},{13,9},{6,2},{10,6},{14,10},{7,3},{... | collective-permute-start | bytes 3145736 | tf_op jit(solution)/shard_map/ppermute | solution.py:180
  165.7 48.5 %collective-permute-start.11 = (bf16[1024,1024]{1,0:T(8,128)(2,1)S(1)}, bf16[1024,1024]{1,0:T(8,128)(2,1)}, u32[]{:S(2)}, u32[]{:S(2)}) collective-permute-start(bf16[1024,1024]{1,0:T(8,128)(2,1)S(1)} %pad_maximum_fusion.refs_0_), channel_id=1, source_target_pairs={{0,1},{1,0},{2,3},{3,2},{4,5},{5,4},{6,7},{7,6},{8,9},{9,8},{10,11... | collective-permute-start | bytes 6291464 | tf_op jit(solution)/shard_map/ppermute | solution.py:180
  198.2 16.0 %collective-permute-start.17 = (bf16[1024,1024]{1,0:T(8,128)(2,1)}, bf16[1024,1024]{1,0:T(8,128)(2,1)}, u32[]{:S(2)}, u32[]{:S(2)}) collective-permute-start(bf16[1024,1024]{1,0:T(8,128)(2,1)} %constant_dynamic-update-slice_fusion.refs_2_), channel_id=1, source_target_pairs={{0,1},{1,0},{2,3},{3,2},{4,5},{5,4},{6,7},{7,6},{8,9},{9,8},{10,11... | collective-permute-start | bytes 6291464 | tf_op jit(solution)/shard_map/ppermute | solution.py:180
  200.0 34.0 %collective-permute-start.19 = (bf16[512,1024]{1,0:T(8,128)(2,1)}, bf16[512,1024]{1,0:T(8,128)(2,1)}, u32[]{:S(2)}, u32[]{:S(2)}) collective-permute-start(bf16[512,1024]{1,0:T(8,128)(2,1)} %collective-permute-done.15), channel_id=1, source_target_pairs={{4,8},{8,12},{5,9},{9,13},{6,10},{10,14},{7,11},{11,15},{20,24},{2... | collective-permute-start | bytes 3145736 | tf_op jit(solution)/shard_map/ppermute | solution.py:180
  202.3 31.7 %collective-permute-start.20 = (bf16[512,1024]{1,0:T(8,128)(2,1)}, bf16[512,1024]{1,0:T(8,128)(2,1)}, u32[]{:S(2)}, u32[]{:S(2)}) collective-permute-start(bf16[512,1024]{1,0:T(8,128)(2,1)} %collective-permute-done.16), channel_id=1, source_target_pairs={{4,0},{8,4},{5,1},{9,5},{6,2},{10,6},{7,3},{11,7},{20,16},{24,20},... | collective-permute-start | bytes 3145736 | tf_op jit(solution)/shard_map/ppermute | solution.py:180
  243.4 25.3 %collective-permute-start.22 = (bf16[512,1024]{1,0:T(8,128)(2,1)S(1)}, bf16[512,1024]{1,0:T(8,128)(2,1)S(1)}, u32[]{:S(2)}, u32[]{:S(2)}) collective-permute-start(bf16[512,1024]{1,0:T(8,128)(2,1)S(1)} %slice.51), channel_id=1, source_target_pairs={{0,16},{16,0},{1,17},{17,1},{2,18},{18,2},{3,19},{19,3},{4,20},{20... | collective-permute-start | bytes 3145736 | tf_op jit(solution)/shard_map/ppermute | solution.py:180
  245.1 24.1 %collective-permute-start.23 = (bf16[512,1024]{1,0:T(8,128)(2,1)}, bf16[512,1024]{1,0:T(8,128)(2,1)S(1)}, u32[]{:S(2)}, u32[]{:S(2)}) collective-permute-start(bf16[512,1024]{1,0:T(8,128)(2,1)} %collective-permute-done.19), channel_id=1, source_target_pairs={{8,12},{9,13},{10,14},{11,15},{24,28},{25,29},{26,30},{27,31}} | collective-permute-start | bytes 3145736 | tf_op jit(solution)/shard_map/ppermute | solution.py:180
  245.8 24.3 %collective-permute-start.24 = (bf16[512,1024]{1,0:T(8,128)(2,1)}, bf16[512,1024]{1,0:T(8,128)(2,1)S(1)}, u32[]{:S(2)}, u32[]{:S(2)}) collective-permute-start(bf16[512,1024]{1,0:T(8,128)(2,1)} %collective-permute-done.20), channel_id=1, source_target_pairs={{4,0},{5,1},{6,2},{7,3},{20,16},{21,17},{22,18},{23,19}} | collective-permute-start | bytes 3145736 | tf_op jit(solution)/shard_map/ppermute | solution.py:180
  273.7 27.0 %collective-permute-start.25 = (bf16[512,1024]{1,0:T(8,128)(2,1)S(1)}, bf16[512,1024]{1,0:T(8,128)(2,1)S(1)}, u32[]{:S(2)}, u32[]{:S(2)}) collective-permute-start(bf16[512,1024]{1,0:T(8,128)(2,1)S(1)} %convert_element_type.135), channel_id=1, source_target_pairs={{2,0},{18,16},{3,1},{19,17},{6,4},{22,20},{7,5},{23,21},{8,10},{24... | collective-permute-start | bytes 3145736 | tf_op jit(solution)/shard_map/ppermute | solution.py:180
  277.3 25.0 %collective-permute-start.27 = (bf16[512,512]{1,0:T(8,128)(2,1)S(1)}, bf16[512,512]{1,0:T(8,128)(2,1)S(1)}, u32[]{:S(2)}, u32[]{:S(2)}) collective-permute-start(bf16[512,512]{1,0:T(8,128)(2,1)S(1)} %slice.53), channel_id=1, source_target_pairs={{0,16},{16,0},{1,17},{17,1},{2,18},{18,2},{3,19},{19,3},{4,20},{20... | collective-permute-start | bytes 1572872 | tf_op jit(solution)/shard_map/ppermute | solution.py:180
  291.7 15.4 %collective-permute-start.30 = (bf16[512,512]{1,0:T(8,128)(2,1)}, bf16[512,512]{1,0:T(8,128)(2,1)}, u32[]{:S(2)}, u32[]{:S(2)}) collective-permute-start(bf16[512,512]{1,0:T(8,128)(2,1)} %fusion.7), channel_id=1, source_target_pairs={{0,2},{16,18},{1,3},{17,19},{4,6},{20,22},{5,7},{21,23},{10,8},{26... | collective-permute-start | bytes 1572872 | tf_op jit(solution)/shard_map/ppermute | solution.py:180
  (29 other events, 456.6 us)
